TPU v7x, 32 devices: a whole 2x2x4 slice. The times are simulated.
32 devices in a mesh: seq: 4 (over y, core), fsdp: 8 (over z, x).
Axes of the slice: x: 2, y: 2, z: 4, core: 2. Of those that a mesh axis runs over, the one named last changes fastest.
Arguments:
- tokens: bfloat16 [8, 4096, 768], P('fsdp', 'seq'), may hold values from -6 to 6
- lengths: int32 [8], P('fsdp'), may hold values from 3073 to 4096
- attn_gain: bfloat16 [768], P('fsdp'), may hold values from 0.5 to 1.5
- qkv_weight: bfloat16 [768, 2304], P('fsdp'), may hold values from -0.21875 to 0.21875
- proj_weight: bfloat16 [768, 768], P('fsdp'), may hold values from -6 to 6
- ffn_gain: bfloat16 [768], P('fsdp'), may hold values from 0.5 to 1.5
- in_weight: bfloat16 [768, 2304], P('fsdp'), may hold values from -0.21875 to 0.21875
- out_weight: bfloat16 [1152, 768], P('fsdp'), may hold values from -0.1875 to 0.1875
- out_grad: bfloat16 [8, 4096, 768], P('fsdp', 'seq'), may hold values from -6 to 6
Outputs:
- block_out: bfloat16 [8, 4096, 768], P('fsdp', 'seq')
- tokens_grad: float32 [8, 4096, 768], P('fsdp', 'seq')
- attn_gain_grad: float32 [768], P('fsdp')
- qkv_weight_grad: float32 [768, 2304], P('fsdp')
- proj_weight_grad: float32 [768, 768], P('fsdp')
- ffn_gain_grad: float32 [768], P('fsdp')
- in_weight_grad: float32 [768, 2304], P('fsdp')
- out_weight_grad: float32 [1152, 768], P('fsdp')
Inputs may be any that keep to these rules, and one draw needn't show every extreme that they name: `lengths`: positions at or beyond a sequence's length are padding, which no query attends to.
All inputs are finite; a program needn't handle non-finite values.
Results may differ from a plain program's by a relative error of at most 0.017.
Values may be sent and summed in bfloat16 or wider, within the bound.
No kernel may reach another device: no remote copies, remote signals or barrier semaphores. Data moves between devices by JAX's collectives and lax.ppermute only.
A program may use at most 192 MiB of HBM per device.

v0:
```python
import jax
import jax.numpy as jnp
from jax import lax
from jax.sharding import PartitionSpec as P

D = 768
HEADS = 12


epsilon = 1e-05
rope_base = 160000.0
masked_score = -1e30


def normalize(activation, gain_row):
    centred = activation - jnp.mean(activation, axis=-1, keepdims=True)
    inverse = lax.rsqrt(jnp.mean(centred * centred, axis=-1, keepdims=True) + epsilon)
    unit_rows = centred * inverse
    return (unit_rows * gain_row, unit_rows, inverse)


def normalize_back(gradient, unit_rows, inverse, gain_row):
    scaled = gradient * gain_row
    gain_grad = jnp.sum(gradient * unit_rows, axis=0)
    input_grad = inverse * (
        scaled
        - jnp.mean(scaled, axis=-1, keepdims=True)
        - unit_rows * jnp.mean(scaled * unit_rows, axis=-1, keepdims=True)
    )
    return (input_grad, gain_grad)


def rope_tables(positions, head_dim):
    half_dim = head_dim // 2
    frequency = rope_base ** (-(lax.iota(jnp.float32, half_dim) * 2.0) / head_dim)
    angles = positions.astype(jnp.float32)[:, None] * frequency[None, :]
    angles = jnp.concatenate([angles, angles], axis=1)
    return (jnp.cos(angles), jnp.sin(angles))


def rotate(activation, cosine, sine_table):
    half_dim = activation.shape[-1] // 2
    turned = jnp.concatenate([-activation[..., half_dim:], activation[..., :half_dim]], axis=-1)
    return activation * cosine[:, None, :] + turned * sine_table[:, None, :]


def geglu(gate_up):
    split_at = gate_up.shape[-1] // 2
    return jax.nn.gelu(gate_up[:, :split_at], approximate=False) * gate_up[:, split_at:]


def masked_scores(query_block, key_rows, valid_keys, score_scale):
    scores = (
        jnp.einsum("qhd,khd->hqk", query_block, key_rows, preferred_element_type=jnp.float32)
        * score_scale
    )
    return jnp.where(valid_keys[None, None, :], scores, masked_score)


def attend_block(query_block, key_rows, values, valid_keys, score_scale):
    scores = masked_scores(query_block, key_rows, valid_keys, score_scale)
    row_max = jnp.max(scores, axis=-1, keepdims=True)
    log_total = row_max + jnp.log(jnp.sum(jnp.exp(scores - row_max), axis=-1, keepdims=True))
    weights = jnp.exp(scores - log_total).astype(jnp.bfloat16)
    mixed_block = jnp.einsum("hqk,khd->qhd", weights, values, preferred_element_type=jnp.float32)
    return (mixed_block, log_total[..., 0])


def body(
    tokens, lengths, attn_gain, qkv_weight, proj_weight, ffn_gain, in_weight, out_weight, out_grad
):
    local_rows = tokens.shape[1]
    model_width = tokens.shape[2]
    groups = lax.axis_size("seq")
    full_rows = local_rows * groups
    head_dim = D // HEADS
    group_width = model_width // groups
    local_heads = group_width // head_dim
    score_scale = head_dim ** (-0.5)
    block_rows = min(512, full_rows)
    block_count = full_rows // block_rows
    inputs = tokens[0].astype(jnp.float32)
    gains_one, qkv_full, proj_full = (
        lax.all_gather(attn_gain, "fsdp", axis=0, tiled=True),
        lax.all_gather(qkv_weight, "fsdp", axis=0, tiled=True),
        lax.all_gather(proj_weight, "fsdp", axis=0, tiled=True),
    )
    normed, unit_one, inverse_one = normalize(inputs, gains_one.astype(jnp.float32))
    normed_low = normed.astype(jnp.bfloat16)
    packed = jnp.dot(normed_low, qkv_full, preferred_element_type=jnp.float32).reshape(
        local_rows, 3, HEADS, head_dim
    )
    positions = lax.axis_index("seq") * local_rows + lax.iota(jnp.int32, local_rows)
    cosine, sine_table = rope_tables(positions, head_dim)
    rotated = jnp.stack(
        [
            rotate(packed[:, 0], cosine, sine_table),
            rotate(packed[:, 1], cosine, sine_table),
            packed[:, 2],
        ],
        axis=1,
    )
    sent_heads = rotated.reshape(local_rows, 3, model_width).astype(jnp.bfloat16)
    arrived = lax.all_to_all(sent_heads, "seq", split_axis=2, concat_axis=0, tiled=True)
    queries = arrived[:, 0].reshape(full_rows, local_heads, head_dim)
    key_rows = arrived[:, 1].reshape(full_rows, local_heads, head_dim)
    values = arrived[:, 2].reshape(full_rows, local_heads, head_dim)
    valid_keys = lax.iota(jnp.int32, full_rows) < lengths[0]
    query_blocks = queries.reshape(block_count, block_rows, local_heads, head_dim)
    mixed_heads, log_totals = lax.map(
        lambda query_block: attend_block(query_block, key_rows, values, valid_keys, score_scale),
        query_blocks,
    )
    mixed_low = mixed_heads.reshape(full_rows, group_width).astype(jnp.bfloat16)
    gathered_heads = lax.all_to_all(mixed_low, "seq", split_axis=0, concat_axis=1, tiled=True)
    hidden = inputs + jnp.dot(gathered_heads, proj_full, preferred_element_type=jnp.float32)
    gains_two, in_full, out_full = (
        lax.all_gather(ffn_gain, "fsdp", axis=0, tiled=True),
        lax.all_gather(in_weight, "fsdp", axis=0, tiled=True),
        lax.all_gather(out_weight, "fsdp", axis=0, tiled=True),
    )
    second, unit_two, inverse_two = normalize(hidden, gains_two.astype(jnp.float32))
    second_low = second.astype(jnp.bfloat16)
    gate_up = jnp.dot(second_low, in_full, preferred_element_type=jnp.float32)
    inner_low = geglu(gate_up).astype(jnp.bfloat16)
    result = hidden + jnp.dot(inner_low, out_full, preferred_element_type=jnp.float32)
    cotangent = out_grad[0].astype(jnp.float32)
    gains_two, in_full, out_full = (
        lax.all_gather(ffn_gain, "fsdp", axis=0, tiled=True),
        lax.all_gather(in_weight, "fsdp", axis=0, tiled=True),
        lax.all_gather(out_weight, "fsdp", axis=0, tiled=True),
    )
    d_ffn_out = cotangent.astype(jnp.bfloat16)
    d_inner = jnp.dot(d_ffn_out, out_full.T, preferred_element_type=jnp.float32)
    grad_out_weight = jnp.dot(inner_low.T, d_ffn_out, preferred_element_type=jnp.float32)
    geglu_back = jax.vjp(geglu, gate_up)[1]
    d_gate_up = geglu_back(d_inner)[0].astype(jnp.bfloat16)
    grad_in_weight = jnp.dot(second_low.T, d_gate_up, preferred_element_type=jnp.float32)
    d_second = jnp.dot(d_gate_up, in_full.T, preferred_element_type=jnp.float32)
    d_norm_two, grad_ffn_gain = normalize_back(
        d_second, unit_two, inverse_two, gains_two.astype(jnp.float32)
    )
    d_hidden = cotangent + d_norm_two
    ffn_gain_part, in_weight_part, out_weight_part = (
        lax.psum_scatter(grad_ffn_gain, "fsdp", scatter_dimension=0, tiled=True),
        lax.psum_scatter(grad_in_weight, "fsdp", scatter_dimension=0, tiled=True),
        lax.psum_scatter(grad_out_weight, "fsdp", scatter_dimension=0, tiled=True),
    )
    ffn_gain_grad, in_weight_grad, out_weight_grad = (
        lax.psum(ffn_gain_part.astype(jnp.bfloat16), "seq").astype(jnp.float32),
        lax.psum(in_weight_part.astype(jnp.bfloat16), "seq").astype(jnp.float32),
        lax.psum(out_weight_part.astype(jnp.bfloat16), "seq").astype(jnp.float32),
    )
    gains_one, qkv_full, proj_full = (
        lax.all_gather(attn_gain, "fsdp", axis=0, tiled=True),
        lax.all_gather(qkv_weight, "fsdp", axis=0, tiled=True),
        lax.all_gather(proj_weight, "fsdp", axis=0, tiled=True),
    )
    d_branch = d_hidden.astype(jnp.bfloat16)
    grad_proj_weight = jnp.dot(gathered_heads.T, d_branch, preferred_element_type=jnp.float32)
    d_heads_low = jnp.dot(d_branch, proj_full.T, preferred_element_type=jnp.float32).astype(
        jnp.bfloat16
    )
    d_mixed = lax.all_to_all(d_heads_low, "seq", split_axis=1, concat_axis=0, tiled=True).reshape(
        block_count, block_rows, local_heads, head_dim
    )

    def attend_back(running, block_in):
        key_sum, value_sum = running
        query_block, d_block, log_block = block_in
        scores = masked_scores(query_block, key_rows, valid_keys, score_scale)
        probabilities = jnp.exp(scores - log_block[:, :, None])
        d_probs = jnp.einsum("qhd,khd->hqk", d_block, values, preferred_element_type=jnp.float32)
        row_dot = jnp.sum(probabilities * d_probs, axis=-1, keepdims=True)
        d_scores = (probabilities * (d_probs - row_dot)).astype(jnp.bfloat16)
        d_query = (
            jnp.einsum("hqk,khd->qhd", d_scores, key_rows, preferred_element_type=jnp.float32)
            * score_scale
        )
        key_sum = (
            key_sum
            + jnp.einsum("hqk,qhd->khd", d_scores, query_block, preferred_element_type=jnp.float32)
            * score_scale
        )
        value_sum = value_sum + jnp.einsum(
            "hqk,qhd->khd",
            probabilities.astype(jnp.bfloat16),
            d_block,
            preferred_element_type=jnp.float32,
        )
        return ((key_sum, value_sum), d_query)

    zero_heads = jnp.zeros((full_rows, local_heads, head_dim), jnp.float32)
    (key_grad, value_grad), query_grad = lax.scan(
        attend_back, (zero_heads, zero_heads), (query_blocks, d_mixed, log_totals)
    )
    returned = jnp.stack(
        [
            query_grad.reshape(full_rows, group_width),
            key_grad.reshape(full_rows, group_width),
            value_grad.reshape(full_rows, group_width),
        ],
        axis=1,
    ).astype(jnp.bfloat16)
    d_packed = (
        lax.all_to_all(returned, "seq", split_axis=0, concat_axis=2, tiled=True)
        .astype(jnp.float32)
        .reshape(local_rows, 3, HEADS, head_dim)
    )
    d_rotated = jnp.stack(
        [
            rotate(d_packed[:, 0], cosine, -sine_table),
            rotate(d_packed[:, 1], cosine, -sine_table),
            d_packed[:, 2],
        ],
        axis=1,
    )
    d_qkv_low = d_rotated.reshape(local_rows, 3 * model_width).astype(jnp.bfloat16)
    grad_qkv_weight = jnp.dot(normed_low.T, d_qkv_low, preferred_element_type=jnp.float32)
    d_normed = jnp.dot(d_qkv_low, qkv_full.T, preferred_element_type=jnp.float32)
    d_norm_one, grad_attn_gain = normalize_back(
        d_normed, unit_one, inverse_one, gains_one.astype(jnp.float32)
    )
    tokens_grad = d_hidden + d_norm_one
    attn_gain_part, qkv_weight_part, proj_weight_part = (
        lax.psum_scatter(grad_attn_gain, "fsdp", scatter_dimension=0, tiled=True),
        lax.psum_scatter(grad_qkv_weight, "fsdp", scatter_dimension=0, tiled=True),
        lax.psum_scatter(grad_proj_weight, "fsdp", scatter_dimension=0, tiled=True),
    )
    attn_gain_grad, qkv_weight_grad, proj_weight_grad = (
        lax.psum(attn_gain_part.astype(jnp.bfloat16), "seq").astype(jnp.float32),
        lax.psum(qkv_weight_part.astype(jnp.bfloat16), "seq").astype(jnp.float32),
        lax.psum(proj_weight_part.astype(jnp.bfloat16), "seq").astype(jnp.float32),
    )
    return (
        result.astype(jnp.bfloat16)[None],
        tokens_grad[None],
        attn_gain_grad,
        qkv_weight_grad,
        proj_weight_grad,
        ffn_gain_grad,
        in_weight_grad,
        out_weight_grad,
    )


def solution(mesh):
    in_specs = (
        P("fsdp", "seq", None),
        P("fsdp"),
        P("fsdp"),
        P("fsdp", None),
        P("fsdp", None),
        P("fsdp"),
        P("fsdp", None),
        P("fsdp", None),
        P("fsdp", "seq", None),
    )
    out_specs = (
        P("fsdp", "seq", None),
        P("fsdp", "seq", None),
        P("fsdp"),
        P("fsdp", None),
        P("fsdp", None),
        P("fsdp"),
        P("fsdp", None),
        P("fsdp", None),
    )
    return jax.shard_map(body, mesh=mesh, in_specs=in_specs, out_specs=out_specs, check_vma=False)
```

profile of v0, /device:TPU:1, one launch (start us, length us, event | category | flops | bytes accessed | tf_op | source)
XLA Modules:
  0.0 1587.6 jit_solution(9065884944835919501)
XLA Ops:
  11.6 19.6 %all-reduce.7 = (bf16[768]{0:T(1024)(128)(2,1)S(1)}, bf16[768]{0:T(1024)(128)(2,1)}) all-reduce(bf16[768]{0:T(1024)(128)(2,1)S(1)} %dynamic-update-slice, bf16[768]{0:T(1024)(128)(2,1)S(1)} %dynamic-update-slice.1), channel_id=1, replica_groups=mesh['seq'=4,'fsdp'=8] {'fsdp'}, use_global_device_ids=true, to_apply=%add.2 | all-reduce | flops 1536 | bytes 6144
  35.4 41.3 %all-gather.5.cloned.1.call-done = bf16[768,2304]{1,0:T(8,128)(2,1)} async-done(((bf16[96,2304]{1,0:T(8,128)(2,1)}), bf16[768,2304]{1,0:T(8,128)(2,1)}) %all-gather.5.cloned.1.call-update) | async-done | bytes 3538960 | tf_op jit(solution)/shard_map/all_gather | solution.py:85
  120.4 68.4 %all-to-all-done = bf16[1024,3,768]{0,1,2:T(4,128)(2,1)} async-done(((bf16[1024,3,768]{0,1,2:T(4,128)(2,1)}), bf16[1024,3,768]{0,1,2:T(4,128)(2,1)}, u32[]{:S(2)}, u32[]{:S(2)}) %all-to-all-start) | async-done | bytes 4718624 | tf_op jit(solution)/shard_map/all_to_all | solution.py:104
  215.0 203.9 %while.28 = (s32[]{:T(128)}, bf16[8,512,3,64]{1,3,2,0:T(8,128)(2,1)}, f32[8,3,512]{2,1,0:T(4,128)S(1)}, bf16[8,512,3,64]{1,3,2,0:T(8,128)(2,1)}, bf16[4096,3,64]...) while((s32[]{:T(128)}, bf16[8,512,3,64]{1,3,2,0:T(8,128)(2,1)}, ...), condition=%wide.region_5.6_spmd.clone, body=%wide.region_2.5_spmd.clone.sunk | while | flops 1679821312 | bytes 179970192 | solution.py:110
  279.5 11.9 fusion.147
  356.0 11.9 fusion.147
  437.6 16.8 %all-to-all-done.1 = bf16[4,1024,192]{1,2,0:T(8,128)(2,1)} async-done(((bf16[4,1024,192]{1,2,0:T(8,128)(2,1)}), bf16[4,1024,192]{1,2,0:T(8,128)(2,1)}, u32[]{:S(2)}, u32[]{:S(2)}) %all-to-all-start.1) | async-done | bytes 1572896 | tf_op jit(solution)/shard_map/all_to_all | solution.py:115
  481.2 14.9 fusion.87
  563.2 668.2 %while.29 = (s32[]{:T(128)}, f32[4096,3,64]{0,2,1:T(8,128)S(1)}, f32[4096,3,64]{0,2,1:T(8,128)}, bf16[8,512,3,64]{1,3,2,0:T(8,128)(2,1)}, bf16[8,512,3,64]{1,3,2...) while((s32[]{:T(128)}, f32[4096,3,64]{0,2,1:T(8,128)S(1)}, ...), condition=%wide.region_12.13_spmd.clone, body=%wide.region_10.12_spmd.clone.sunk | while | flops 4124936704 | bytes 207284384 | solution.py:194
  564.0 13.6 fusion.157
  577.6 12.4 fusion.159
  590.0 17.3 %multiply_reduce_fusion.7 = (f32[3,512]{1,0:T(4,128)S(1)}, f32[3,512,4096]{2,1,0:T(8,128)}) fusion(f32[3,512,4096]{2,1,0:T(8,128)} %fusion.157, f32[3,512]{1,0:T(4,128)S(1)} %dynamic-slice_bitcast_fusion.2, pred[4096]{0:T(1024)(128)(4,1)S(1)} %iota_compare_fusion.5, bf16[4096,3,64]{0,2,1:T(8,128)(2,1)} %get-tuple-element.505, ...), kind=kOutput, calls=%fused_computation.20.clone.1 | convolution fusion | flops 836762112 | bytes 52117508 | tf_op jit(solution)/shard_map/while/body/eval_jaxpr/qhd,khd->hqk/dot_general | solution.py:173
  607.3 22.7 %multiply_convert_fusion.6 = bf16[3,512,4096]{2,1,0:T(8,128)(2,1)} fusion(f32[3,512,4096]{2,1,0:T(8,128)} %get-tuple-element.447, f32[3,512,4096]{2,1,0:T(8,128)} %fusion.157, f32[3,512]{1,0:T(4,128)S(1)} %get-tuple-element.448, f32[3,512]{1,0:T(4,128)S(1)} %dynamic-slice_bitcast_fusion.2, pred[4096]{0:T(1024)(128)(4,1)S(1)} %iota_compare_fusion.5), kind=kLoop, calls=%fused_computation.19.clone.1 | loop fusion | flops 37748736 | bytes 62930944 | tf_op jit(solution)/shard_map/while/body/eval_jaxpr/convert_element_type | solution.py:175
  647.8 13.5 fusion.157
  661.4 13.7 fusion.159
  675.1 17.7 %multiply_reduce_fusion.7 = (f32[3,512]{1,0:T(4,128)S(1)}, f32[3,512,4096]{2,1,0:T(8,128)}) fusion(f32[3,512,4096]{2,1,0:T(8,128)} %fusion.157, f32[3,512]{1,0:T(4,128)S(1)} %dynamic-slice_bitcast_fusion.2, pred[4096]{0:T(1024)(128)(4,1)S(1)} %iota_compare_fusion.5, bf16[4096,3,64]{0,2,1:T(8,128)(2,1)} %get-tuple-element.505, ...), kind=kOutput, calls=%fused_computation.20.clone.1 | convolution fusion | flops 836762112 | bytes 52117508 | tf_op jit(solution)/shard_map/while/body/eval_jaxpr/qhd,khd->hqk/dot_general | solution.py:173
  692.8 22.5 %multiply_convert_fusion.6 = bf16[3,512,4096]{2,1,0:T(8,128)(2,1)} fusion(f32[3,512,4096]{2,1,0:T(8,128)} %get-tuple-element.447, f32[3,512,4096]{2,1,0:T(8,128)} %fusion.157, f32[3,512]{1,0:T(4,128)S(1)} %get-tuple-element.448, f32[3,512]{1,0:T(4,128)S(1)} %dynamic-slice_bitcast_fusion.2, pred[4096]{0:T(1024)(128)(4,1)S(1)} %iota_compare_fusion.5), kind=kLoop, calls=%fused_computation.19.clone.1 | loop fusion | flops 37748736 | bytes 62930944 | tf_op jit(solution)/shard_map/while/body/eval_jaxpr/convert_element_type | solution.py:175
  733.1 13.7 fusion.157
  746.8 13.8 fusion.159
  760.5 17.5 %multiply_reduce_fusion.7 = (f32[3,512]{1,0:T(4,128)S(1)}, f32[3,512,4096]{2,1,0:T(8,128)}) fusion(f32[3,512,4096]{2,1,0:T(8,128)} %fusion.157, f32[3,512]{1,0:T(4,128)S(1)} %dynamic-slice_bitcast_fusion.2, pred[4096]{0:T(1024)(128)(4,1)S(1)} %iota_compare_fusion.5, bf16[4096,3,64]{0,2,1:T(8,128)(2,1)} %get-tuple-element.505, ...), kind=kOutput, calls=%fused_computation.20.clone.1 | convolution fusion | flops 836762112 | bytes 52117508 | tf_op jit(solution)/shard_map/while/body/eval_jaxpr/qhd,khd->hqk/dot_general | solution.py:173
  778.0 21.6 %multiply_convert_fusion.6 = bf16[3,512,4096]{2,1,0:T(8,128)(2,1)} fusion(f32[3,512,4096]{2,1,0:T(8,128)} %get-tuple-element.447, f32[3,512,4096]{2,1,0:T(8,128)} %fusion.157, f32[3,512]{1,0:T(4,128)S(1)} %get-tuple-element.448, f32[3,512]{1,0:T(4,128)S(1)} %dynamic-slice_bitcast_fusion.2, pred[4096]{0:T(1024)(128)(4,1)S(1)} %iota_compare_fusion.5), kind=kLoop, calls=%fused_computation.19.clone.1 | loop fusion | flops 37748736 | bytes 62930944 | tf_op jit(solution)/shard_map/while/body/eval_jaxpr/convert_element_type | solution.py:175
  817.2 13.3 fusion.157
  830.5 13.6 fusion.159
  844.1 17.0 %multiply_reduce_fusion.7 = (f32[3,512]{1,0:T(4,128)S(1)}, f32[3,512,4096]{2,1,0:T(8,128)}) fusion(f32[3,512,4096]{2,1,0:T(8,128)} %fusion.157, f32[3,512]{1,0:T(4,128)S(1)} %dynamic-slice_bitcast_fusion.2, pred[4096]{0:T(1024)(128)(4,1)S(1)} %iota_compare_fusion.5, bf16[4096,3,64]{0,2,1:T(8,128)(2,1)} %get-tuple-element.505, ...), kind=kOutput, calls=%fused_computation.20.clone.1 | convolution fusion | flops 836762112 | bytes 52117508 | tf_op jit(solution)/shard_map/while/body/eval_jaxpr/qhd,khd->hqk/dot_general | solution.py:173
  861.1 21.3 %multiply_convert_fusion.6 = bf16[3,512,4096]{2,1,0:T(8,128)(2,1)} fusion(f32[3,512,4096]{2,1,0:T(8,128)} %get-tuple-element.447, f32[3,512,4096]{2,1,0:T(8,128)} %fusion.157, f32[3,512]{1,0:T(4,128)S(1)} %get-tuple-element.448, f32[3,512]{1,0:T(4,128)S(1)} %dynamic-slice_bitcast_fusion.2, pred[4096]{0:T(1024)(128)(4,1)S(1)} %iota_compare_fusion.5), kind=kLoop, calls=%fused_computation.19.clone.1 | loop fusion | flops 37748736 | bytes 62930944 | tf_op jit(solution)/shard_map/while/body/eval_jaxpr/convert_element_type | solution.py:175
  900.1 13.3 fusion.157
  913.4 13.6 fusion.159
  927.0 17.0 %multiply_reduce_fusion.7 = (f32[3,512]{1,0:T(4,128)S(1)}, f32[3,512,4096]{2,1,0:T(8,128)}) fusion(f32[3,512,4096]{2,1,0:T(8,128)} %fusion.157, f32[3,512]{1,0:T(4,128)S(1)} %dynamic-slice_bitcast_fusion.2, pred[4096]{0:T(1024)(128)(4,1)S(1)} %iota_compare_fusion.5, bf16[4096,3,64]{0,2,1:T(8,128)(2,1)} %get-tuple-element.505, ...), kind=kOutput, calls=%fused_computation.20.clone.1 | convolution fusion | flops 836762112 | bytes 52117508 | tf_op jit(solution)/shard_map/while/body/eval_jaxpr/qhd,khd->hqk/dot_general | solution.py:173
  944.0 21.3 %multiply_convert_fusion.6 = bf16[3,512,4096]{2,1,0:T(8,128)(2,1)} fusion(f32[3,512,4096]{2,1,0:T(8,128)} %get-tuple-element.447, f32[3,512,4096]{2,1,0:T(8,128)} %fusion.157, f32[3,512]{1,0:T(4,128)S(1)} %get-tuple-element.448, f32[3,512]{1,0:T(4,128)S(1)} %dynamic-slice_bitcast_fusion.2, pred[4096]{0:T(1024)(128)(4,1)S(1)} %iota_compare_fusion.5), kind=kLoop, calls=%fused_computation.19.clone.1 | loop fusion | flops 37748736 | bytes 62930944 | tf_op jit(solution)/shard_map/while/body/eval_jaxpr/convert_element_type | solution.py:175
  983.0 13.3 fusion.157
  996.3 13.6 fusion.159
  1009.9 17.0 %multiply_reduce_fusion.7 = (f32[3,512]{1,0:T(4,128)S(1)}, f32[3,512,4096]{2,1,0:T(8,128)}) fusion(f32[3,512,4096]{2,1,0:T(8,128)} %fusion.157, f32[3,512]{1,0:T(4,128)S(1)} %dynamic-slice_bitcast_fusion.2, pred[4096]{0:T(1024)(128)(4,1)S(1)} %iota_compare_fusion.5, bf16[4096,3,64]{0,2,1:T(8,128)(2,1)} %get-tuple-element.505, ...), kind=kOutput, calls=%fused_computation.20.clone.1 | convolution fusion | flops 836762112 | bytes 52117508 | tf_op jit(solution)/shard_map/while/body/eval_jaxpr/qhd,khd->hqk/dot_general | solution.py:173
  1027.0 21.3 %multiply_convert_fusion.6 = bf16[3,512,4096]{2,1,0:T(8,128)(2,1)} fusion(f32[3,512,4096]{2,1,0:T(8,128)} %get-tuple-element.447, f32[3,512,4096]{2,1,0:T(8,128)} %fusion.157, f32[3,512]{1,0:T(4,128)S(1)} %get-tuple-element.448, f32[3,512]{1,0:T(4,128)S(1)} %dynamic-slice_bitcast_fusion.2, pred[4096]{0:T(1024)(128)(4,1)S(1)} %iota_compare_fusion.5), kind=kLoop, calls=%fused_computation.19.clone.1 | loop fusion | flops 37748736 | bytes 62930944 | tf_op jit(solution)/shard_map/while/body/eval_jaxpr/convert_element_type | solution.py:175
  1065.9 13.3 fusion.157
  1079.2 13.6 fusion.159
  1092.8 17.0 %multiply_reduce_fusion.7 = (f32[3,512]{1,0:T(4,128)S(1)}, f32[3,512,4096]{2,1,0:T(8,128)}) fusion(f32[3,512,4096]{2,1,0:T(8,128)} %fusion.157, f32[3,512]{1,0:T(4,128)S(1)} %dynamic-slice_bitcast_fusion.2, pred[4096]{0:T(1024)(128)(4,1)S(1)} %iota_compare_fusion.5, bf16[4096,3,64]{0,2,1:T(8,128)(2,1)} %get-tuple-element.505, ...), kind=kOutput, calls=%fused_computation.20.clone.1 | convolution fusion | flops 836762112 | bytes 52117508 | tf_op jit(solution)/shard_map/while/body/eval_jaxpr/qhd,khd->hqk/dot_general | solution.py:173
  1109.9 21.3 %multiply_convert_fusion.6 = bf16[3,512,4096]{2,1,0:T(8,128)(2,1)} fusion(f32[3,512,4096]{2,1,0:T(8,128)} %get-tuple-element.447, f32[3,512,4096]{2,1,0:T(8,128)} %fusion.157, f32[3,512]{1,0:T(4,128)S(1)} %get-tuple-element.448, f32[3,512]{1,0:T(4,128)S(1)} %dynamic-slice_bitcast_fusion.2, pred[4096]{0:T(1024)(128)(4,1)S(1)} %iota_compare_fusion.5), kind=kLoop, calls=%fused_computation.19.clone.1 | loop fusion | flops 37748736 | bytes 62930944 | tf_op jit(solution)/shard_map/while/body/eval_jaxpr/convert_element_type | solution.py:175
  1148.8 13.3 fusion.157
  1162.1 13.6 fusion.159
  1175.7 17.0 %multiply_reduce_fusion.7 = (f32[3,512]{1,0:T(4,128)S(1)}, f32[3,512,4096]{2,1,0:T(8,128)}) fusion(f32[3,512,4096]{2,1,0:T(8,128)} %fusion.157, f32[3,512]{1,0:T(4,128)S(1)} %dynamic-slice_bitcast_fusion.2, pred[4096]{0:T(1024)(128)(4,1)S(1)} %iota_compare_fusion.5, bf16[4096,3,64]{0,2,1:T(8,128)(2,1)} %get-tuple-element.505, ...), kind=kOutput, calls=%fused_computation.20.clone.1 | convolution fusion | flops 836762112 | bytes 52117508 | tf_op jit(solution)/shard_map/while/body/eval_jaxpr/qhd,khd->hqk/dot_general | solution.py:173
  1192.7 21.3 %multiply_convert_fusion.6 = bf16[3,512,4096]{2,1,0:T(8,128)(2,1)} fusion(f32[3,512,4096]{2,1,0:T(8,128)} %get-tuple-element.447, f32[3,512,4096]{2,1,0:T(8,128)} %fusion.157, f32[3,512]{1,0:T(4,128)S(1)} %get-tuple-element.448, f32[3,512]{1,0:T(4,128)S(1)} %dynamic-slice_bitcast_fusion.2, pred[4096]{0:T(1024)(128)(4,1)S(1)} %iota_compare_fusion.5), kind=kLoop, calls=%fused_computation.19.clone.1 | loop fusion | flops 37748736 | bytes 62930944 | tf_op jit(solution)/shard_map/while/body/eval_jaxpr/convert_element_type | solution.py:175
  1243.6 12.7 copy.78
  1256.3 100.2 %all_to_all.59 = bf16[4096,3,192]{2,1,0:T(4,128)(2,1)} all-to-all(bf16[4096,3,192]{2,1,0:T(4,128)(2,1)} %copy.78), channel_id=1, replica_groups=mesh['seq'=4,'fsdp'=8] {'seq'}, dimensions={0} | all-to-all | bytes 9437184 | tf_op jit(solution)/shard_map/all_to_all | solution.py:206
  1356.5 12.8 copy.79
  1369.3 12.0 reshape.357
  1420.7 17.8 %all-reduce.6 = (bf16[768]{0:T(1024)(128)(2,1)S(1)}, bf16[768]{0:T(1024)(128)(2,1)S(1)}) all-reduce(f32[768]{0:T(1024)S(1)} %get-tuple-element.243, f32[768]{0:T(1024)S(1)} %copy-done.23), channel_id=2, replica_groups=mesh['seq'=4,'fsdp'=8] {'fsdp'}, use_global_device_ids=true, to_apply=%region_16.17.clone | all-reduce | flops 1536 | bytes 9216
  1454.6 76.6 %reduce-scatter.5.cloned.1.call-done = f32[96,2304]{1,0:T(8,128)} async-done(((f32[768,2304]{1,0:T(8,128)}), f32[96,2304]{1,0:T(8,128)}) %reduce-scatter.5.cloned.1.call-update) | async-done | bytes 884752 | tf_op jit(solution)/shard_map/reduce_scatter | solution.py:227
  1542.4 31.2 %all-reduce.12.cloned.1.call-done = (bf16[96,2304]{1,0:T(8,128)(2,1)}, bf16[96,768]{1,0:T(8,128)(2,1)}, bf16[96,2304]{1,0:T(8,128)(2,1)}, bf16[144,768]{1,0:T(8,128)(2,1)}) async-done(((bf16[96,2304]{1,0:T(8,128)(2,1)}, bf16[96,768]{1,0:T(8,128)(2,1)}, bf16[96,2304]{1,0:T(8,128)(2,1)}, bf16[144,768]{1,0:T(8,128)(2,1)}), (bf16[96,2304]{1,0:T(8,128)(2,1)}, bf16[96,768]{1,0:T(8,128)(2,1)}, ...) | async-done | bytes 1253392 | tf_op jit(solution)/shard_map/psum | solution.py:232
  (251 shorter events, 596.3 us)
Async XLA Ops:
  7.2 69.5 %all-gather.5.cloned.1.call-start = ((), (), s32[]{:S(2)}) async-start(), calls=%async_computation.8 | async-start | bytes 3981312 | tf_op jit(solution)/shard_map/all_gather | solution.py:85
  31.2 51.3 %copy-start.19 = (f32[768]{0:T(1024)}, f32[768]{0:T(1024)S(1)}, u32[]{:S(2)}) copy-start(f32[768]{0:T(1024)S(1)} %convert_element_type.134) | copy-start | bytes 9220
  32.9 49.6 %copy-start.2 = (bf16[1,1024,768]{1,2,0:T(8,128)(2,1)}, bf16[1,1024,768]{1,2,0:T(8,128)(2,1)S(1)}, u32[]{:S(2)}) copy-start(bf16[1,1024,768]{1,2,0:T(8,128)(2,1)S(1)} %copy.62) | copy-start | bytes 4718596
  34.7 58.6 %copy-start.13 = (f32[1024,64]{0,1:T(8,128)}, f32[1024,64]{0,1:T(8,128)S(1)}, u32[]{:S(2)}) copy-start(f32[1024,64]{0,1:T(8,128)S(1)} %get-tuple-element.323) | copy-start | bytes 786436
  34.9 47.5 %copy-start.17 = (f32[1024]{0:T(1024)}, f32[1024]{0:T(1024)S(1)}, u32[]{:S(2)}) copy-start(f32[1024]{0:T(1024)S(1)} %broadcast_multiply_fusion.6) | copy-start | bytes 12292
  35.4 47.1 %copy-start.21 = (f32[1024]{0:T(1024)}, f32[1024]{0:T(1024)S(1)}, u32[]{:S(2)}) copy-start(f32[1024]{0:T(1024)S(1)} %add_rsqrt_fusion.1) | copy-start | bytes 12292
  112.1 76.7 %all-to-all-start = ((bf16[1024,3,768]{0,1,2:T(4,128)(2,1)}), bf16[1024,3,768]{0,1,2:T(4,128)(2,1)}, u32[]{:S(2)}, u32[]{:S(2)}) async-start(bf16[1024,3,768]{0,1,2:T(4,128)(2,1)} %pad_maximum_fusion), calls=%async_computation | async-start | bytes 12582912 | tf_op jit(solution)/shard_map/all_to_all | solution.py:104
  118.9 318.7 %all-gather.7.cloned.1.call-start = ((), (), s32[]{:S(2)}) async-start(), calls=%async_computation.9 | async-start | bytes 1327104 | tf_op jit(solution)/shard_map/all_gather | solution.py:86
  119.7 340.1 %all-gather.9.cloned.1.call-start = ((), (), s32[]{:S(2)}) async-start(), calls=%async_computation.10 | async-start | bytes 3981312 | tf_op jit(solution)/shard_map/all_gather | solution.py:119
  220.2 8.3 copy-start
  245.7 8.3 copy-start
  271.2 8.3 copy-start
  296.7 8.3 copy-start
  322.2 8.3 copy-start
  347.6 8.3 copy-start
  373.1 8.3 copy-start
  398.6 8.3 copy-start
  418.9 7.7 copy-start.1
  426.6 9.1 copy-start.24
  429.7 6.1 copy-start.15
  429.7 24.8 %copy-start.3 = (bf16[1,1024,768]{1,2,0:T(8,128)(2,1)S(1)}, bf16[1,1024,768]{1,2,0:T(8,128)(2,1)}, u32[]{:S(2)}) copy-start(bf16[1,1024,768]{1,2,0:T(8,128)(2,1)} %copy-done.2) | copy-start | bytes 4718596
  429.7 24.8 %all-to-all-start.1 = ((bf16[4,1024,192]{1,2,0:T(8,128)(2,1)}), bf16[4,1024,192]{1,2,0:T(8,128)(2,1)}, u32[]{:S(2)}, u32[]{:S(2)}) async-start(bf16[4,1024,192]{1,2,0:T(8,128)(2,1)} %copy.71), calls=%async_computation.1 | async-start | bytes 3145728 | tf_op jit(solution)/shard_map/all_to_all | solution.py:115
  435.1 46.0 %all-gather.11.cloned.1.call-start = ((), (), s32[]{:S(2)}) async-start(), calls=%async_computation.11 | async-start | bytes 1990656 | tf_op jit(solution)/shard_map/all_gather | solution.py:120
  435.7 1013.6 %reduce-scatter.7.cloned.1.call-start = ((), (), s32[]{:S(2)}) async-start(), calls=%async_computation.13 | async-start | bytes 2654208 | tf_op jit(solution)/shard_map/reduce_scatter | solution.py:228
  457.7 1.7 copy-start.5
  481.2 14.9 copy-start.8
  496.1 3.6 copy-start.6
  499.7 10.1 copy-start.11
  499.7 10.1 copy-start.9
  510.8 11.5 copy-start.7
  516.2 934.7 %reduce-scatter.11.cloned.1.call-start = ((), (), s32[]{:S(2)}) async-start(), calls=%async_computation.15 | async-start | bytes 3981312 | tf_op jit(solution)/shard_map/reduce_scatter | solution.py:147
  526.1 25.3 %all-to-all-start.2 = ((bf16[1024,4,192]{0,2,1:T(8,128)(2,1)}), bf16[1024,4,192]{0,2,1:T(8,128)(2,1)}, u32[]{:S(2)}, u32[]{:S(2)}) async-start(bf16[1024,4,192]{0,2,1:T(8,128)(2,1)} %bitcast.232), calls=%async_computation.2 | async-start | bytes 3145728 | tf_op jit(solution)/shard_map/all_to_all | solution.py:164
  532.1 920.5 %reduce-scatter.9.cloned.1.call-start = ((), (), s32[]{:S(2)}) async-start(), calls=%async_computation.14 | async-start | bytes 7962624 | tf_op jit(solution)/shard_map/reduce_scatter | solution.py:146
  543.7 987.5 %reduce-scatter.5.cloned.1.call-start = ((), (), s32[]{:S(2)}) async-start(), calls=%async_computation.12 | async-start | bytes 7962624 | tf_op jit(solution)/shard_map/reduce_scatter | solution.py:227
  1238.8 2.4 copy-start.10
  1391.5 1.0 copy-start.14
  1391.5 1.0 copy-start.16
  1394.6 2.8 copy-start.4
  1394.6 2.8 copy-start.18
  1394.6 2.8 copy-start.20
  1394.6 2.8 copy-start.22
  1395.2 2.2 copy-start.12
  1403.6 169.9 %all-reduce.12.cloned.1.call-start = ((), (), s32[]{:S(2)}) async-start(), calls=%async_computation.16 | async-start | bytes 2506752 | tf_op jit(solution)/shard_map/psum | solution.py:232
  1411.4 9.3 copy-start.23
Sparse Core Ops, SparseCore 0:
  10.2 66.4 all-gather.4
  121.9 38.4 all-gather.6
  162.6 64.0 all-gather.8
  437.8 43.2 all-gather.10
  516.3 68.1 reduce-scatter.6
  588.0 79.0 reduce-scatter.10
  670.7 127.8 reduce-scatter.8
  1403.7 127.4 reduce-scatter.4
  1534.5 39.0 all-reduce.11
where the time goes:
time: 1600 us; the launch traced here: 1590 us
  matrix products  713 us (45%)
  other arithmetic  284 us (18%)
  waiting for transfers between devices  255 us (16%)
  local copies, waits for them, and re-layouts  152 us (10%)
  blocking collectives  147 us (9%)
  starting transfers between devices  18.8 us (1%)
    convert_element_type x8, other arithmetic, attend_back(): d_scores = (probabilities * (d_probs - row_dot)).astype(jnp.bfloat16)  173 us
    dot_general x16, matrix products, masked_scores(): jnp.einsum('qhd,khd->hqk', query_block, key_rows, preferred_element_type=...  144 us
    dot_general x8, matrix products, attend_back(): jnp.einsum('qhd,khd->hqk', d_block, values, preferred_element_type=jnp.fl...  138 us
    dot_general x8, matrix products, attend_back(): jnp.einsum('hqk,qhd->khd', probabilities.astype(jnp.bfloat16), d_block, p...  108 us
    all_to_all x1, blocking collectives, body(): lax.all_to_all(returned, 'seq', split_axis=0, concat_axis=2, tiled=True)  100 us
    dot_general x8, matrix products, attend_block(): jnp.einsum('hqk,khd->qhd', weights, values, preferred_element_type=jnp.fl...  95.6 us
    dot_general x8, matrix products, attend_back(): jnp.einsum('hqk,khd->qhd', d_scores, key_rows, preferred_element_type=jnp...  77 us
    reduce_scatter x1, waiting for transfers between devices, body(): lax.psum_scatter(grad_qkv_weight, 'fsdp', scatter_dimension=0, tiled=True)  76.6 us
  transfers between devices with their start and end apart: 12, of which 7 were waited for; matrix products, arithmetic and copies ran while one was open for 65% of the time, Pallas kernels for 0%

commit v1 on v0

v1 whole, which is shorter than its diff:
```python
import functools

import jax
import jax.numpy as jnp
from jax import lax
from jax.experimental import pallas as pl
from jax.experimental.pallas import tpu as pltpu
from jax.sharding import PartitionSpec as P

D = 768
HEADS = 12
HD = 64

epsilon = 1e-05
rope_base = 160000.0
masked_score = -1e30
LOG2E = 1.4426950408889634
LN2 = 0.6931471805599453

bf = jnp.bfloat16
f32 = jnp.float32
NN = ((1,), (0,))
NT = ((1,), (1,))
TN = ((0,), (0,))


def dg(a, b, dims):
    return lax.dot_general(a, b, (dims, ((), ())), preferred_element_type=f32)


def unit_rows_of(x):
    centred = x - jnp.mean(x, axis=-1, keepdims=True)
    inverse = lax.rsqrt(jnp.mean(centred * centred, axis=-1, keepdims=True) + epsilon)
    return centred * inverse, inverse


def qkv_kernel(heads, info_ref, x_ref, gain_ref, w_ref, cs_ref, *refs):
    n_ref, k_ref, v_ref, qt_ref, kt_ref, vt_ref = refs[-6:]
    rb = x_ref.shape[0]
    unit, _ = unit_rows_of(x_ref[...].astype(f32))
    normed = (unit * gain_ref[...]).astype(bf)
    n_ref[...] = normed
    cs = cs_ref[...]
    lane = lax.broadcasted_iota(jnp.int32, (rb, 128), 1)
    row = lax.broadcasted_iota(jnp.int32, (rb, 128), 0)
    position = info_ref[0] + pl.program_id(0) * rb + row
    bias = jnp.where(position < info_ref[1], 0.0, masked_score)
    key_tail = jnp.where(lane == HD, bias, 0.0)
    query_tail = jnp.where(lane == HD, 1.0, 0.0)
    value_tail = jnp.where(lane < HD + 2, -1.0, 0.0)
    head_lane = lane < HD
    for h in range(heads):
        y = dg(normed, w_ref[:, h * 384 : (h + 1) * 384], NN)
        q = y[:, :128] * cs
        q = q + pltpu.roll(q, HD, 1)
        k = y[:, 128:256] * cs
        k = k + pltpu.roll(k, HD, 1)
        v = y[:, 256:]
        qe = jnp.where(head_lane, q * (HD**-0.5 * LOG2E), query_tail)
        qt_ref[h] = qe.T.astype(bf)
        ke = jnp.where(head_lane, k, key_tail)
        k_ref[h] = ke.astype(bf)
        kt_ref[h] = ke.T[:HD].astype(bf)
        v_ref[h] = jnp.where(head_lane, v, value_tail).astype(bf)
        ve = jnp.where(head_lane, v, query_tail)
        vt_ref[h] = ve.T[:80].astype(bf)


def qkv_call(block, blocks, info, x, gain, w, cs, carried):
    rows = x.shape[0]
    S = rows * blocks
    heads = w.shape[1] // 384
    rb = min(256, rows)
    steps = rows // rb
    at = lambda i: block * steps + i
    outs = (
        jax.ShapeDtypeStruct((S, D), bf),
        jax.ShapeDtypeStruct((heads, S, 128), bf),
        jax.ShapeDtypeStruct((heads, S, 128), bf),
        jax.ShapeDtypeStruct((heads, 128, S), bf),
        jax.ShapeDtypeStruct((heads, HD, S), bf),
        jax.ShapeDtypeStruct((heads, 80, S), bf),
    )
    in_specs = [
        pl.BlockSpec(memory_space=pltpu.SMEM),
        pl.BlockSpec((rb, D), lambda i: (i, 0)),
        pl.BlockSpec((1, D), lambda i: (0, 0)),
        pl.BlockSpec(w.shape, lambda i: (0, 0)),
        pl.BlockSpec((rb, 128), lambda i: (at(i), 0)),
    ]
    aliases = {}
    if carried is not None:
        in_specs += [pl.BlockSpec(memory_space=pl.ANY)] * 6
        aliases = {5 + n: n for n in range(6)}
    return pl.pallas_call(
        functools.partial(qkv_kernel, heads),
        grid=(steps,),
        out_shape=outs,
        in_specs=in_specs,
        out_specs=(
            pl.BlockSpec((rb, D), lambda i: (at(i), 0)),
            pl.BlockSpec((heads, rb, 128), lambda i: (0, at(i), 0)),
            pl.BlockSpec((heads, rb, 128), lambda i: (0, at(i), 0)),
            pl.BlockSpec((heads, 128, rb), lambda i: (0, 0, at(i))),
            pl.BlockSpec((heads, HD, rb), lambda i: (0, 0, at(i))),
            pl.BlockSpec((heads, 80, rb), lambda i: (0, 0, at(i))),
        ),
        input_output_aliases=aliases,
        compiler_params=pltpu.CompilerParams(vmem_limit_bytes=48 * 2**20),
        cost_estimate=pl.CostEstimate(
            flops=4 * rows * D * w.shape[1], bytes_accessed=rows * 8192, transcendentals=0
        ),
        name="qkv",
    )(info, x, gain, w, cs, *(carried or ()))


def attend_kernel(kc, k_ref, q_ref, v_ref, p_ref, o_ref, ob_ref, linv_ref, s_ref):
    rows = k_ref.shape[1]
    bq = q_ref.shape[2]
    q = q_ref[0]
    m = jnp.full((8, bq), -jnp.inf, f32)
    for c in range(rows // kc):
        at = slice(c * kc, (c + 1) * kc)
        s = dg(k_ref[0, at, :], q, NN)
        s_ref[at, :] = s
        m = jnp.maximum(m, jnp.max(s.reshape(kc // 8, 8, bq), axis=0))
    m = jnp.max(m, axis=0, keepdims=True)
    acc = jnp.zeros((v_ref.shape[1], bq), f32)
    for c in range(rows // kc):
        at = slice(c * kc, (c + 1) * kc)
        p = jnp.exp2(s_ref[at, :] - m).astype(bf)
        p_ref[0, at, :] = p
        acc = acc + dg(v_ref[0, :, at], p, NN)
    linv = 1.0 / acc[HD : HD + 1, :]
    o = acc[:HD, :] * linv
    o_ref[...] = o
    ob_ref[0] = o.astype(bf)
    linv_ref[0] = linv


def attend(h, k, qt, vt, groups, bq=512, kc=512):
    S = k.shape[1]
    nq = S // bq
    per = nq // groups
    return pl.pallas_call(
        functools.partial(attend_kernel, kc),
        grid=(nq,),
        out_shape=(
            jax.ShapeDtypeStruct((nq, S, bq), bf),
            jax.ShapeDtypeStruct((HD, S), f32),
            jax.ShapeDtypeStruct((groups, HD, S // groups), bf),
            jax.ShapeDtypeStruct((nq, 1, bq), f32),
        ),
        in_specs=[
            pl.BlockSpec((1, S, 128), lambda i: (h, 0, 0)),
            pl.BlockSpec((1, 128, bq), lambda i: (h, 0, i)),
            pl.BlockSpec((1, 80, S), lambda i: (h, 0, 0)),
        ],
        out_specs=(
            pl.BlockSpec((1, S, bq), lambda i: (i, 0, 0)),
            pl.BlockSpec((HD, bq), lambda i: (0, i)),
            pl.BlockSpec((1, HD, bq), lambda i: (i // per, 0, i % per)),
            pl.BlockSpec((1, 1, bq), lambda i: (i, 0, 0)),
        ),
        scratch_shapes=[pltpu.VMEM((S, bq), f32)],
        compiler_params=pltpu.CompilerParams(vmem_limit_bytes=48 * 2**20),
        cost_estimate=pl.CostEstimate(
            flops=16 * HD * S * S, bytes_accessed=2 * S * S, transcendentals=S * S
        ),
        name="attend",
    )(k, qt, vt)


def attend_back_kernel(
    kc, nq, per, v_ref, kt_ref, q_ref, do_ref, o_ref, linv_ref, p_ref, cos_ref, sin_ref, out_ref, acc_ref
):
    i = pl.program_id(0)
    rows = v_ref.shape[1]
    bq = q_ref.shape[2]

    @pl.when(i == 0)
    def _():
        acc_ref[...] = jnp.zeros_like(acc_ref)

    dop = (do_ref[0].astype(f32) * linv_ref[0]).astype(bf)
    delta = jnp.sum(dop.astype(f32) * o_ref[...], axis=0, keepdims=True)
    high = delta.astype(bf).astype(f32)
    r = lax.broadcasted_iota(jnp.int32, (16, bq), 0)
    tail = jnp.where(r == 0, high, jnp.where(r == 1, delta - high, 0.0)).astype(bf)
    doe = jnp.concatenate([dop, tail, jnp.zeros((128 - HD - 16, bq), bf)], axis=0)
    zero = jnp.zeros((HD, bq), bf)
    right_v = jnp.concatenate([dop, zero], axis=0)
    right_k = jnp.concatenate([zero, q_ref[0, :HD, :]], axis=0)
    dq = jnp.zeros((HD, bq), f32)
    for c in range(rows // kc):
        at = slice(c * kc, (c + 1) * kc)
        p = p_ref[0, at, :]
        ds = p * dg(v_ref[0, at, :], doe, NN).astype(bf)
        acc_ref[at, :] = acc_ref[at, :] + dg(p, right_v, NT) + dg(ds, right_k, NT)
        dq = dq + dg(kt_ref[0, :, at], ds, NN)
    dq = dq * HD**-0.5
    turned = jnp.concatenate([dq[HD // 2 :], -dq[: HD // 2]], axis=0)
    here = pl.ds(pl.multiple_of(i * bq, bq), bq)
    dq = dq * cos_ref[:, here] + turned * sin_ref[:, here]
    out_ref[i // per, :HD, pl.ds(pl.multiple_of((i % per) * bq, bq), bq)] = dq.astype(bf)

    @pl.when(i == nq - 1)
    def _():
        groups = out_ref.shape[0]
        width = rows // groups
        for j in range(groups):
            at = slice(j * width, (j + 1) * width)
            t = acc_ref[at, :].T
            dk = t[HD:] * LN2
            turned_k = jnp.concatenate([dk[HD // 2 :], -dk[: HD // 2]], axis=0)
            dk = dk * cos_ref[:, at] + turned_k * sin_ref[:, at]
            out_ref[j, HD : 2 * HD] = dk.astype(bf)
            out_ref[j, 2 * HD :] = t[:HD].astype(bf)


def attend_back(h, v, kt, qt, do, o, linv, p, cos, sin, groups, bq=512, kc=512):
    S = v.shape[1]
    nq = S // bq
    per = nq // groups
    return pl.pallas_call(
        functools.partial(attend_back_kernel, kc, nq, per),
        grid=(nq,),
        out_shape=jax.ShapeDtypeStruct((groups, 3 * HD, S // groups), bf),
        in_specs=[
            pl.BlockSpec((1, S, 128), lambda i: (h, 0, 0)),
            pl.BlockSpec((1, HD, S), lambda i: (h, 0, 0)),
            pl.BlockSpec((1, 128, bq), lambda i: (h, 0, i)),
            pl.BlockSpec((1, HD, bq), lambda i: (i // per, 0, i % per)),
            pl.BlockSpec((HD, bq), lambda i: (0, i)),
            pl.BlockSpec((1, 1, bq), lambda i: (i, 0, 0)),
            pl.BlockSpec((1, S, bq), lambda i: (i, 0, 0)),
            pl.BlockSpec((HD, S), lambda i: (0, 0)),
            pl.BlockSpec((HD, S), lambda i: (0, 0)),
        ],
        out_specs=pl.BlockSpec((groups, 3 * HD, S // groups), lambda i: (0, 0, 0)),
        scratch_shapes=[pltpu.VMEM((S, 128), f32)],
        compiler_params=pltpu.CompilerParams(vmem_limit_bytes=48 * 2**20),
        cost_estimate=pl.CostEstimate(
            flops=24 * HD * S * S, bytes_accessed=2 * S * S, transcendentals=0
        ),
        name="attend_back",
    )(v, kt, qt, do, o, linv, p, cos, sin)


def normalize_back(gradient, unit_rows, inverse, gain_row):
    scaled = gradient * gain_row
    gain_grad = jnp.sum(gradient * unit_rows, axis=0)
    input_grad = inverse * (
        scaled
        - jnp.mean(scaled, axis=-1, keepdims=True)
        - unit_rows * jnp.mean(scaled * unit_rows, axis=-1, keepdims=True)
    )
    return (input_grad, gain_grad)


def body(
    tokens, lengths, attn_gain, qkv_weight, proj_weight, ffn_gain, in_weight, out_weight, out_grad
):
    rows = tokens.shape[1]
    groups = lax.axis_size("seq")
    S = rows * groups
    heads = HEADS // groups
    me = lax.axis_index("seq")

    def swap(array, j):
        return lax.ppermute(array, "seq", [(i, i ^ j) for i in range(groups)])

    def exchange(chunks):
        return [chunks[0]] + [swap(chunks[j], j) for j in range(1, groups)]

    def relative(array, axis):
        return [lax.dynamic_index_in_dim(array, me ^ j, axis, False) for j in range(groups)]

    def gather(array):
        return lax.all_gather(array, "fsdp", axis=0, tiled=True)

    x0 = tokens[0]
    blocks = [x0]
    step = 1
    while step < groups:
        blocks = blocks + [swap(b, step) for b in blocks]
        step *= 2

    own_columns = lax.dynamic_index_in_dim(
        qkv_weight.reshape(-1, 3, groups, heads * HD), me, 2, False
    ).reshape(-1, 3 * heads * HD)
    first = gather(jnp.concatenate([own_columns, attn_gain[:, None]], axis=1))
    own_full = first[:, : 3 * heads * HD].reshape(D, 3, heads, HD)
    gain_one = first[:, 3 * heads * HD].astype(f32)[None, :]
    turned = jnp.concatenate([-own_full[..., HD // 2 :], own_full[..., : HD // 2]], axis=-1)
    turned = jnp.concatenate([turned[:, :2], jnp.zeros_like(turned[:, :1])], axis=1)
    w_ext = (
        jnp.concatenate([own_full, turned], axis=-1).transpose(0, 2, 1, 3).reshape(D, heads * 384)
    )

    half = HD // 2
    frequency = rope_base ** (-(lax.iota(f32, half) * 2.0) / HD)
    starts = [(me ^ j) * rows for j in range(groups)]
    positions = jnp.concatenate([s + lax.iota(jnp.int32, rows) for s in starts]).astype(f32)
    angles = frequency[:, None] * positions[None, :]
    cosine, sine = jnp.cos(angles), jnp.sin(angles)
    cos_t = jnp.concatenate([cosine, cosine], axis=0)
    sin_t = jnp.concatenate([sine, sine], axis=0)
    cs = jnp.concatenate([cos_t, sin_t], axis=0).T

    carried = None
    for j in range(groups):
        info = jnp.stack([starts[j], lengths[0]]).astype(jnp.int32)
        carried = qkv_call(j, groups, info, blocks[j], gain_one, w_ext, cs, carried)
    normed, k, v, qt, kt, vt = carried

    proj_full = gather(proj_weight)
    gain_two = gather(ffn_gain).astype(f32)[None, :]
    in_full = gather(in_weight)
    out_full = gather(out_weight)
    qkv_full = gather(qkv_weight)

    kept = []
    mixed_parts = []
    for h in range(heads):
        p, o, ob, linv = attend(h, k, qt, vt, groups)
        kept.append((p, o, linv))
        mixed_parts += exchange([ob[j] for j in range(groups)])
    mixed_t = jnp.concatenate(mixed_parts, axis=0)
    proj_rel = jnp.stack(
        relative(proj_full.reshape(groups, heads, HD, D), 0), axis=1
    ).reshape(D, D)

    x = x0.astype(f32)
    hidden = x + dg(mixed_t, proj_rel, TN)
    unit_two, inverse_two = unit_rows_of(hidden)
    second_low = (unit_two * gain_two).astype(bf)
    gate_up = dg(second_low, in_full, NN)
    ff = gate_up.shape[1] // 2
    gate, up = gate_up[:, :ff], gate_up[:, ff:]
    bell = 0.5 * (1.0 + lax.erf(gate * 0.7071067811865476))
    gelu = gate * bell
    inner_low = (gelu * up).astype(bf)
    result = hidden + dg(inner_low, out_full, NN)
    dy_low = out_grad[0]
    cotangent = dy_low.astype(f32)
    d_inner = dg(dy_low, out_full, NT)
    slope = bell + gate * (jnp.exp(-0.5 * gate * gate) * 0.3989422804014327)
    d_gate_up = jnp.concatenate([d_inner * up * slope, d_inner * gelu], axis=1).astype(bf)
    d_second = dg(d_gate_up, in_full, NT)
    d_norm_two, grad_ffn_gain = normalize_back(d_second, unit_two, inverse_two, gain_two)
    d_hidden = cotangent + d_norm_two
    d_branch = d_hidden.astype(bf)
    d_heads = dg(proj_rel, d_branch, NT).astype(bf).reshape(heads, groups, HD, rows)
    d_mixed = [jnp.stack(exchange([d_heads[h, j] for j in range(groups)])) for h in range(heads)]

    grad_out = dg(inner_low, dy_low, TN)
    grad_in = dg(second_low, d_gate_up, TN)
    grad_proj = dg(mixed_t, d_branch, NN).reshape(heads, groups, HD, D)
    grad_proj = jnp.stack(relative(grad_proj, 1), axis=0).reshape(D, D)

    def over_seq(array):
        parts = array.astype(bf).reshape(array.shape[0], groups, -1)
        mine = relative(parts, 1)
        total = mine[0].astype(f32)
        for j in range(1, groups):
            total = total + swap(mine[j], j).astype(f32)
        return total.astype(bf)

    def to_owner(array):
        return lax.psum_scatter(array, "fsdp", scatter_dimension=0, tiled=True)

    wide = to_owner(over_seq(jnp.concatenate([grad_in, grad_proj], axis=1)))
    tall = to_owner(over_seq(grad_out))
    wide = lax.all_gather(wide, "seq", axis=1, tiled=True).astype(f32)
    out_weight_grad = lax.all_gather(tall, "seq", axis=1, tiled=True).astype(f32)
    in_weight_grad, proj_weight_grad = wide[:, : 2 * ff], wide[:, 2 * ff :]

    wt = qkv_full.T.reshape(3, groups, heads, HD, D)
    wt = jnp.stack(relative(wt, 1), axis=0)
    normed_blocks = normed.reshape(groups, rows, D)
    d_normed = jnp.zeros((rows, D), f32)
    qkv_parts = []
    for h in range(heads):
        p, o, linv = kept[h]
        d_own = attend_back(h, v, kt, qt, d_mixed[h], o, linv, p, cos_t, sin_t, groups)
        received = jnp.concatenate(exchange([d_own[j] for j in range(groups)]), axis=0)
        d_normed = d_normed + dg(received, wt[:, :, h].reshape(3 * groups * HD, D), TN)
        grad = jnp.einsum("jdp,jpf->fd", d_own, normed_blocks, preferred_element_type=f32)
        qkv_parts.append(to_owner(grad.astype(bf)))
    qkv_own = jnp.stack(qkv_parts)
    qkv_all = lax.all_gather(qkv_own, "seq", axis=0)
    qkv_weight_grad = (
        qkv_all.reshape(groups, heads, -1, 3, HD)
        .transpose(2, 3, 0, 1, 4)
        .reshape(-1, 3 * D)
        .astype(f32)
    )
    unit_one, inverse_one = unit_rows_of(x)
    d_norm_one, grad_attn_gain = normalize_back(d_normed, unit_one, inverse_one, gain_one)
    tokens_grad = d_hidden + d_norm_one
    gains = lax.psum(jnp.stack([grad_attn_gain, grad_ffn_gain]), ("seq", "fsdp"))
    shard = D // lax.axis_size("fsdp")
    gains = lax.dynamic_slice_in_dim(gains, lax.axis_index("fsdp") * shard, shard, 1)
    return (
        result.astype(bf)[None],
        tokens_grad[None],
        gains[0],
        qkv_weight_grad,
        proj_weight_grad,
        gains[1],
        in_weight_grad,
        out_weight_grad,
    )


def solution(mesh):
    in_specs = (
        P("fsdp", "seq", None),
        P("fsdp"),
        P("fsdp"),
        P("fsdp", None),
        P("fsdp", None),
        P("fsdp"),
        P("fsdp", None),
        P("fsdp", None),
        P("fsdp", "seq", None),
    )
    out_specs = (
        P("fsdp", "seq", None),
        P("fsdp", "seq", None),
        P("fsdp"),
        P("fsdp", None),
        P("fsdp", None),
        P("fsdp"),
        P("fsdp", None),
        P("fsdp", None),
    )
    return jax.shard_map(body, mesh=mesh, in_specs=in_specs, out_specs=out_specs, check_vma=False)
```

time: 1600 us -> 725 us (0.45)
  matrix products: 713 us -> 74.7 us
  other arithmetic: 284 us -> 31.9 us
  Pallas kernels: 0 us -> 238 us
  waiting for transfers between devices: 255 us -> 128 us
  local copies, waits for them, and re-layouts: 152 us -> 81.7 us
  blocking collectives: 147 us -> 109 us
  starting transfers between devices: 18.8 us -> 38.5 us
    dot_general x68 -> x15, matrix products: 713 us -> 74.7 us  [the longest x12 61.4 us: dg(): return lax.dot_general(a, b, (dims, ((), ())), preferred_element_type=f32)]
    pallas_call x0 -> x10, Pallas kernels: none -> 238 us  [the longest x3 116 us: attend_back(): pl.pallas_call(functools.partial(attend_back_kernel, kc, nq, per), grid=(...]
    convert_element_type x22 -> x6, other arithmetic: 190 us -> 5.67 us  [the longest x2 5.32 us: over_seq(): return total.astype(bf)]
    all_to_all x1 -> x0, blocking collectives: 100 us -> none  [body(): lax.all_to_all(returned, 'seq', split_axis=0, concat_axis=2, tiled=True)]
    all_to_all x3 -> x0, waiting for transfers between devices: 92.9 us -> none  [the longest x1 68.4 us: body(): lax.all_to_all(sent_heads, 'seq', split_axis=2, concat_axis=0, tiled=True)]
    ppermute x0 -> x36, waiting for transfers between devices: none -> 92.4 us  [swap(): return lax.ppermute(array, 'seq', [(i, i ^ j) for i in range(groups)])]
    all_gather x0 -> x4, blocking collectives: none -> 55.6 us  [the longest x1 30 us: gather(): return lax.all_gather(array, 'fsdp', axis=0, tiled=True)]
    all_gather x4, waiting for transfers between devices: 52 us -> 0.03 us  [gather(): return lax.all_gather(array, 'fsdp', axis=0, tiled=True)]
  transfers between devices with their start and end apart: 12 -> 45, of which waited for: 7 -> 13; matrix products, arithmetic and copies ran while one was open for 65% -> 23% of each run, Pallas kernels for 0% -> 33%
where the time goes in v1:
time: 725 us; the launch traced here: 718 us
  Pallas kernels  238 us (33%)
  waiting for transfers between devices  128 us (18%)
  blocking collectives  109 us (15%)
  local copies, waits for them, and re-layouts  81.7 us (11%)
  matrix products  74.7 us (10%)
  starting transfers between devices  38.5 us (5%)
  other arithmetic  31.9 us (4%)
  between operations  16.4 us (2%)
    pallas_call x3, Pallas kernels, attend_back(): pl.pallas_call(functools.partial(attend_back_kernel, kc, nq, per), grid=(...  116 us
    pallas_call x3, Pallas kernels, attend(): pl.pallas_call(functools.partial(attend_kernel, kc), grid=(nq,), out_shap...  93.6 us
    ppermute x36, waiting for transfers between devices, swap(): return lax.ppermute(array, 'seq', [(i, i ^ j) for i in range(groups)])  92.4 us
    dot_general x12, matrix products, dg(): return lax.dot_general(a, b, (dims, ((), ())), preferred_element_type=f32)  61.4 us
    ppermute x36, starting transfers between devices, swap(): return lax.ppermute(array, 'seq', [(i, i ^ j) for i in range(groups)])  37.9 us
    psum x1, blocking collectives, body(): lax.psum(jnp.stack([grad_attn_gain, grad_ffn_gain]), ('seq', 'fsdp'))  35.8 us
    reduce_scatter x4, waiting for transfers between devices, to_owner(): return lax.psum_scatter(array, 'fsdp', scatter_dimension=0, tiled=True)  33.2 us
    unnamed x131, local copies, waits for them, and re-layouts  30.5 us
  transfers between devices with their start and end apart: 45, of which 13 were waited for; matrix products, arithmetic and copies ran while one was open for 23% of the time, Pallas kernels for 33%

profile of v1, /device:TPU:1, one launch (start us, length us, event | category | flops | bytes accessed | tf_op | source)
XLA Modules:
  0.0 717.5 jit_solution(13510437788746519989)
XLA Ops:
  9.6 2.7 collective-permute-start.2
  18.7 2.9 copy.165.cs_ref
  22.4 30.0 %all_gather.30 = bf16[768,577]{1,0:T(8,128)(2,1)S(1)} all-gather(bf16[96,577]{1,0:T(8,128)(2,1)S(1)} %copy.155), channel_id=1, replica_groups=mesh['seq'=4,'fsdp'=8] {'fsdp'}, dimensions={0}, use_global_device_ids=true | all-gather | bytes 997056 | tf_op jit(solution)/shard_map/all_gather | solution.py:280
  56.7 2.8 copy.164.w_ref
  62.8 6.8 qkv.4
  72.3 17.3 %all-reduce = bf16[768]{0:T(1024)(128)(2,1)S(1)} all-reduce(bf16[768]{0:T(1024)(128)(2,1)S(1)} %dynamic-update-slice), channel_id=1, replica_groups=mesh['seq'=4,'fsdp'=8] {'fsdp'}, use_global_device_ids=true, to_apply=%add | all-reduce | flops 768 | bytes 3072
  91.9 6.9 qkv.5
  98.8 6.9 qkv.6
  107.3 7.3 %qkv.7 = (bf16[4096,768]{1,0:T(8,128)(2,1)}, bf16[3,4096,128]{2,1,0:T(8,128)(2,1)}, bf16[3,4096,128]{2,1,0:T(8,128)(2,1)}, bf16[3,128,4096]{2,1,0:T(8,128)(2,1)}...) custom-call(s32[2]{0:T(128)S(1)} %pad_add_fusion.info_ref, ...), custom_call_target="tpu_custom_call", output_to_operand_aliasing={{0}: (5, {}), {1}: (6, {}), {2}: (7, {}), {3}: (8, {}), {4}... | custom-call | flops 3623878656 | bytes 8388608 | tf_op jit(solution)/shard_map/qkv/pallas_call | solution.py:95
  116.7 31.1 %attend.5 = (bf16[8,4096,512]{2,1,0:T(8,128)(2,1)}, f32[64,4096]{1,0:T(8,128)S(1)}, bf16[4,64,1024]{2,1,0:T(8,128)(2,1)S(1)}, f32[8,1,512]{2,1,0:T(1,128)S(1)}) custom-call(bf16[3,4096,128]{2,1,0:T(8,128)(2,1)} %get-tuple-element.62.k_ref, bf16[3,128,4096]{2,1,0:T(8,128)(2,1)} %get-tuple-element.63.q_ref, bf16[3,80,4096]{2,1,0:T(8,128)(2,1)S(1)} %copy-done), custom_call_target="tpu_custom_call" | custom-call | flops 17179869184 | bytes 33554432 | tf_op jit(solution)/shard_map/attend/pallas_call | solution.py:145
  148.7 31.1 %attend.4 = (bf16[8,4096,512]{2,1,0:T(8,128)(2,1)}, f32[64,4096]{1,0:T(8,128)S(1)}, bf16[4,64,1024]{2,1,0:T(8,128)(2,1)S(1)}, f32[8,1,512]{2,1,0:T(1,128)S(1)}) custom-call(bf16[3,4096,128]{2,1,0:T(8,128)(2,1)} %get-tuple-element.62.k_ref, bf16[3,128,4096]{2,1,0:T(8,128)(2,1)} %get-tuple-element.63.q_ref, bf16[3,80,4096]{2,1,0:T(8,128)(2,1)S(1)} %copy-done), custom_call_target="tpu_custom_call" | custom-call | flops 17179869184 | bytes 33554432 | tf_op jit(solution)/shard_map/attend/pallas_call | solution.py:145
  180.9 31.4 %attend.3 = (bf16[8,4096,512]{2,1,0:T(8,128)(2,1)}, f32[64,4096]{1,0:T(8,128)S(1)}, bf16[4,64,1024]{2,1,0:T(8,128)(2,1)S(1)}, f32[8,1,512]{2,1,0:T(1,128)S(1)}) custom-call(bf16[3,4096,128]{2,1,0:T(8,128)(2,1)} %get-tuple-element.62.k_ref, bf16[3,128,4096]{2,1,0:T(8,128)(2,1)} %get-tuple-element.63.q_ref, bf16[3,80,4096]{2,1,0:T(8,128)(2,1)S(1)} %copy-done), custom_call_target="tpu_custom_call" | custom-call | flops 17179869184 | bytes 33554432 | tf_op jit(solution)/shard_map/attend/pallas_call | solution.py:145
  212.4 9.2 %collective-permute-start.3 = (bf16[64,1024]{1,0:T(8,128)(2,1)S(1)}, bf16[64,1024]{1,0:T(8,128)(2,1)S(1)}, u32[]{:S(2)}, u32[]{:S(2)}) collective-permute-start(bf16[64,1024]{1,0:T(8,128)(2,1)S(1)} %get-tuple-element.177), channel_id=1, source_target_pairs={{0,8},{8,0},{16,24},{24,16},{1,9},{9,1},{17,25},{25,17},{2,10},{10... | collective-permute-start | bytes 393224 | tf_op jit(solution)/shard_map/ppermute | solution.py:271
  232.3 3.7 collective-permute-done.8
  238.0 2.9 collective-permute-done.11
  240.8 3.2 fusion.72
  246.5 10.7 %fusion.70 = f32[1024,2304]{1,0:T(8,128)} fusion(bf16[768,2304]{1,0:T(8,128)(2,1)} %all-gather.9.cloned.1.call-done, f32[1024,768]{1,0:T(8,128)} %get-tuple-element.183, f32[768]{0:T(1024)S(1)} %convert_element_type.126, f32[1024]{0:T(1024)S(1)} %add_rsqrt_fusion.1, f32[1024]{0:T(1024)S(1)} %broadcast_multiply_fusion.5), kind=kOutput, calls=%fused_computation.205 | convolution fusion | flops 3627024384 | bytes 16133120 | tf_op jit(solution)/shard_map/dot_general | solution.py:28
  257.2 6.9 fusion.5
  269.3 6.1 multiply_reduce_fusion
  275.4 2.8 multiply_add_fusion
  280.1 6.1 convolution_convert_fusion
  286.2 2.8 pad_maximum_fusion.1
  289.0 10.2 %convert_element_type.142 = bf16[768,4,768]{2,1,0:T(4,128)(2,1)} reshape(bf16[768,3072]{1,0:T(8,128)(2,1)} %pad_maximum_fusion.1) | data formatting | bytes 9437184 | tf_op jit(solution)/shard_map/convert_element_type | solution.py:363
  299.2 3.5 convolution_convert_fusion.2
  305.7 11.1 %constant_dynamic-slice_fusion.3 = (bf16[768,1,768]{2,1,0:T(2,128)(2,1)}, bf16[768,1,768]{2,1,0:T(2,128)(2,1)}, bf16[768,1,768]{2,1,0:T(2,128)(2,1)}, bf16[768,1,768]{2,1,0:T(2,128)(2,1)}) fusion(bf16[768,4,768]{2,1,0:T(4,128)(2,1)S(1)} %copy-done.18, s32[]{:T(128)S(6)} %select_n.38, s32[]{:T(128)S(6)} %select_n.40, s32[]{:T(128)S(6)} %select_n.39, ...), kind=kLoop, calls=%fused_computation.178 | loop fusion | bytes 9437200 | tf_op jit(solution)/shard_map/jit(dynamic_index_in_dim)/dynamic_slice | solution.py:277
  316.8 5.8 copy.168
  327.0 5.2 fusion.51
  342.9 38.9 %attend_back.3 = bf16[4,192,1024]{2,1,0:T(8,128)(2,1)S(1)} custom-call(bf16[3,4096,128]{2,1,0:T(8,128)(2,1)} %get-tuple-element.68.v_ref, bf16[3,64,4096]{2,1,0:T(8,128)(2,1)} %copy-done.1, bf16[3,128,4096]{2,1,0:T(8,128)(2,1)} %get-tuple-element.63.q_ref, bf16[4,64,1024]{2,1,0:T(8,128)(2,1)S(1)} %pad_maximum_fusion.9.do_ref, ...), custom_call_target="tpu_custom_call" | custom-call | flops 25769803776 | bytes 33554432 | tf_op jit(solution)/shard_map/attend_back/pallas_call | solution.py:225
  381.9 2.6 fusion.52
  391.6 38.6 %attend_back.4 = bf16[4,192,1024]{2,1,0:T(8,128)(2,1)S(1)} custom-call(bf16[3,4096,128]{2,1,0:T(8,128)(2,1)} %get-tuple-element.68.v_ref, bf16[3,64,4096]{2,1,0:T(8,128)(2,1)} %copy-done.1, bf16[3,128,4096]{2,1,0:T(8,128)(2,1)} %get-tuple-element.63.q_ref, bf16[4,64,1024]{2,1,0:T(8,128)(2,1)S(1)} %pad_maximum_fusion.10.do_ref, f32[64,4096]{1,0:T(8,128)S(1)} %copy-done.17, ...), custom_call_target="tpu_custom_call" | custom-call | flops 25769803776 | bytes 33554432 | tf_op jit(solution)/shard_map/attend_back/pallas_call | solution.py:225
  430.1 5.4 fusion.53
  440.5 38.8 %attend_back.5 = bf16[4,192,1024]{2,1,0:T(8,128)(2,1)S(1)} custom-call(bf16[3,4096,128]{2,1,0:T(8,128)(2,1)} %get-tuple-element.68.v_ref, bf16[3,64,4096]{2,1,0:T(8,128)(2,1)} %copy-done.1, bf16[3,128,4096]{2,1,0:T(8,128)(2,1)} %get-tuple-element.63.q_ref, bf16[4,64,1024]{2,1,0:T(8,128)(2,1)S(1)} %pad_maximum_fusion.11.do_ref, f32[64,4096]{1,0:T(8,128)S(1)} %copy-done.15, ...), custom_call_target="tpu_custom_call" | custom-call | flops 25769803776 | bytes 33554432 | tf_op jit(solution)/shard_map/attend_back/pallas_call | solution.py:225
  480.4 5.4 fusion.54
  493.5 5.1 collective-permute-done.22
  502.8 54.9 %collective-permute-done.23 = bf16[192,1024]{1,0:T(8,128)(2,1)} collective-permute-done((bf16[192,1024]{1,0:T(8,128)(2,1)}, bf16[192,1024]{1,0:T(8,128)(2,1)}, u32[]{:S(2)}, u32[]{:S(2)}) %collective-permute-start.23) | collective-permute-done | bytes 393248 | tf_op jit(solution)/shard_map/ppermute | solution.py:271
  559.7 4.5 fusion.30
  564.2 4.3 collective-permute-done.16
  570.2 7.0 collective-permute-done.17
  578.8 4.3 fusion.22
  584.2 3.7 fusion.21
  588.3 8.8 %collective-permute-done.29 = bf16[192,1024]{1,0:T(8,128)(2,1)} collective-permute-done((bf16[192,1024]{1,0:T(8,128)(2,1)}, bf16[192,1024]{1,0:T(8,128)(2,1)}, u32[]{:S(2)}, u32[]{:S(2)}) %collective-permute-start.29) | collective-permute-done | bytes 393248 | tf_op jit(solution)/shard_map/ppermute | solution.py:271
  597.1 7.2 %fusion.16 = (f32[768]{0:T(1024)S(1)}, f32[1024]{0:T(1024)S(1)}, f32[1024]{0:T(1024)S(1)}, f32[1024,768]{1,0:T(8,128)}) fusion(f32[1024]{0:T(1024)S(1)} %copy-done.41, f32[1024]{0:T(1024)S(1)} %copy-done.38, bf16[1,1024,768]{2,1,0:T(8,128)(2,1)S(1)} %copy-done.5, f32[768]{0:T(1024)S(1)} %copy-done.40, bf16[768,768]{1,0:T(8,128)(2,1)S(1)} %bitcast.259, ...), kind=kOutput, calls=%fused_computation.29 | convolution fusion | flops 1222898944 | bytes 13785088 | tf_op jit(solution)/shard_map/dot_general | solution.py:28
  604.3 35.8 %psum.7 = f32[2,768]{1,0:T(2,128)S(1)} all-reduce(f32[2,768]{1,0:T(2,128)S(1)} %pad_maximum_fusion.14), channel_id=1, replica_groups=mesh['seq'=4,'fsdp'=8] {'seq','fsdp'}, use_global_device_ids=true, to_apply=%region_10.11 | all-reduce | flops 1536 | bytes 12288 | tf_op jit(solution)/shard_map/psum | solution.py:402
  640.7 4.5 fusion.15
  646.1 9.7 %all-gather = bf16[12,96,192]{2,1,0:T(8,128)(2,1)S(1)} all-gather(bf16[3,96,192]{2,1,0:T(8,128)(2,1)S(1)} %pad_maximum_fusion.13), channel_id=2, replica_groups=mesh['seq'=4,'fsdp'=8] {'seq'}, dimensions={0}, use_global_device_ids=true | all-gather | bytes 552960 | tf_op jit(solution)/shard_map/all_gather | solution.py:392
  658.8 6.0 all-gather.1
  666.1 33.1 %reduce-scatter.14.cloned.1.call-done = bf16[96,768]{1,0:T(8,128)(2,1)} async-done(((bf16[768,768]{1,0:T(8,128)(2,1)}), bf16[96,768]{1,0:T(8,128)(2,1)}) %reduce-scatter.14.cloned.1.call-update) | async-done | bytes 147472 | tf_op jit(solution)/shard_map/reduce_scatter | solution.py:371
  699.2 9.8 %all_gather.38 = bf16[96,3072]{1,0:T(8,128)(2,1)S(1)} all-gather(bf16[96,768]{1,0:T(8,128)(2,1)} %reduce-scatter.14.cloned.1.call-done), channel_id=1, replica_groups=mesh['seq'=4,'fsdp'=8] {'seq'}, dimensions={1}, use_global_device_ids=true | all-gather | bytes 737280 | tf_op jit(solution)/shard_map/all_gather | solution.py:375
  (290 shorter events, 105.6 us)
Async XLA Ops:
  7.2 98.6 %all-gather.7.cloned.1.call-start = ((), (), s32[]{:S(2)}) async-start(), calls=%async_computation.5 | async-start | bytes 1327104 | tf_op jit(solution)/shard_map/all_gather | solution.py:280
  7.9 238.6 %all-gather.9.cloned.1.call-start = ((), (), s32[]{:S(2)}) async-start(), calls=%async_computation.6 | async-start | bytes 3981312 | tf_op jit(solution)/shard_map/all_gather | solution.py:280
  8.7 248.5 %all-gather.11.cloned.1.call-start = ((), (), s32[]{:S(2)}) async-start(), calls=%async_computation.7 | async-start | bytes 1990656 | tf_op jit(solution)/shard_map/all_gather | solution.py:280
  9.4 307.4 %all-gather.13.cloned.1.call-start = ((), (), s32[]{:S(2)}) async-start(), calls=%async_computation.8 | async-start | bytes 3981312 | tf_op jit(solution)/shard_map/all_gather | solution.py:280
  9.4 61.3 %collective-permute-start = (bf16[1024,768]{1,0:T(8,128)(2,1)}, bf16[1024,768]{1,0:T(8,128)(2,1)}, u32[]{:S(2)}, u32[]{:S(2)}) collective-permute-start(bf16[1024,768]{1,0:T(8,128)(2,1)} %bitcast.240), channel_id=1, source_target_pairs={{0,8},{8,0},{16,24},{24,16},{1,9},{9,1},{17,25},{25,17},{2,10},{10... | collective-permute-start | bytes 4718600 | tf_op jit(solution)/shard_map/ppermute | solution.py:271
  9.6 89.3 %collective-permute-start.2 = (bf16[1024,768]{1,0:T(8,128)(2,1)}, bf16[1024,768]{1,0:T(8,128)(2,1)}, u32[]{:S(2)}, u32[]{:S(2)}) collective-permute-start(bf16[1024,768]{1,0:T(8,128)(2,1)} %bitcast.241), channel_id=1, source_target_pairs={{0,16},{8,24},{16,0},{24,8},{1,17},{9,25},{17,1},{25,9},{2,18},{10... | collective-permute-start | bytes 4718600 | tf_op jit(solution)/shard_map/ppermute | solution.py:271
  12.3 632.9 %reduce-scatter.8.cloned.1.call-start = ((), (), s32[]{:S(2)}) async-start(), calls=%async_computation.9 | async-start | bytes 442368 | tf_op jit(solution)/shard_map/reduce_scatter | solution.py:371
  70.7 36.5 %collective-permute-start.1 = (bf16[1024,768]{1,0:T(8,128)(2,1)}, bf16[1024,768]{1,0:T(8,128)(2,1)}, u32[]{:S(2)}, u32[]{:S(2)}) collective-permute-start(bf16[1024,768]{1,0:T(8,128)(2,1)} %collective-permute-done.x_ref), channel_id=1, source_target_pairs={{0,16},{8,24},{16,0},{24,8},{1,17},{9,25},{17,1},{25,9},{2,18},{10... | collective-permute-start | bytes 4718600 | tf_op jit(solution)/shard_map/ppermute | solution.py:271
  107.2 133.6 %copy-start.34 = (bf16[3,4,64,768]{3,2,1,0:T(8,128)(2,1)}, bf16[3,4,64,768]{3,2,1,0:T(8,128)(2,1)S(1)}, u32[]{:S(2)}) copy-start(bf16[3,4,64,768]{3,2,1,0:T(8,128)(2,1)S(1)} %pad_maximum_fusion.5) | copy-start | bytes 3538948
  212.4 12.7 %collective-permute-start.3 = (bf16[64,1024]{1,0:T(8,128)(2,1)S(1)}, bf16[64,1024]{1,0:T(8,128)(2,1)S(1)}, u32[]{:S(2)}, u32[]{:S(2)}) collective-permute-start(bf16[64,1024]{1,0:T(8,128)(2,1)S(1)} %get-tuple-element.177), channel_id=1, source_target_pairs={{0,8},{8,0},{16,24},{24,16},{1,9},{9,1},{17,25},{25,17},{2,10},{10... | collective-permute-start | bytes 393224 | tf_op jit(solution)/shard_map/ppermute | solution.py:271
  221.5 5.2 collective-permute-start.4
  223.0 7.0 collective-permute-start.5
  223.3 8.6 %collective-permute-start.6 = (bf16[64,1024]{1,0:T(8,128)(2,1)S(1)}, bf16[64,1024]{1,0:T(8,128)(2,1)S(1)}, u32[]{:S(2)}, u32[]{:S(2)}) collective-permute-start(bf16[64,1024]{1,0:T(8,128)(2,1)S(1)} %get-tuple-element.174), channel_id=1, source_target_pairs={{0,8},{8,0},{16,24},{24,16},{1,9},{9,1},{17,25},{25,17},{2,10},{10... | collective-permute-start | bytes 393224 | tf_op jit(solution)/shard_map/ppermute | solution.py:271
  223.5 8.8 %collective-permute-start.7 = (bf16[64,1024]{1,0:T(8,128)(2,1)S(1)}, bf16[64,1024]{1,0:T(8,128)(2,1)S(1)}, u32[]{:S(2)}, u32[]{:S(2)}) collective-permute-start(bf16[64,1024]{1,0:T(8,128)(2,1)S(1)} %get-tuple-element.173), channel_id=1, source_target_pairs={{0,16},{8,24},{16,0},{24,8},{1,17},{9,25},{17,1},{25,9},{2,18},{10... | collective-permute-start | bytes 393224 | tf_op jit(solution)/shard_map/ppermute | solution.py:271
  225.0 11.0 %collective-permute-start.8 = (bf16[64,1024]{1,0:T(8,128)(2,1)S(1)}, bf16[64,1024]{1,0:T(8,128)(2,1)S(1)}, u32[]{:S(2)}, u32[]{:S(2)}) collective-permute-start(bf16[64,1024]{1,0:T(8,128)(2,1)S(1)} %get-tuple-element.172), channel_id=1, source_target_pairs={{0,24},{8,16},{16,8},{24,0},{1,25},{9,17},{17,9},{25,1},{2,26},{10... | collective-permute-start | bytes 393224 | tf_op jit(solution)/shard_map/ppermute | solution.py:271
  226.7 9.4 %collective-permute-start.9 = (bf16[64,1024]{1,0:T(8,128)(2,1)S(1)}, bf16[64,1024]{1,0:T(8,128)(2,1)S(1)}, u32[]{:S(2)}, u32[]{:S(2)}) collective-permute-start(bf16[64,1024]{1,0:T(8,128)(2,1)S(1)} %get-tuple-element.171), channel_id=1, source_target_pairs={{0,8},{8,0},{16,24},{24,16},{1,9},{9,1},{17,25},{25,17},{2,10},{10... | collective-permute-start | bytes 393224 | tf_op jit(solution)/shard_map/ppermute | solution.py:271
  230.0 7.9 %collective-permute-start.10 = (bf16[64,1024]{1,0:T(8,128)(2,1)S(1)}, bf16[64,1024]{1,0:T(8,128)(2,1)S(1)}, u32[]{:S(2)}, u32[]{:S(2)}) collective-permute-start(bf16[64,1024]{1,0:T(8,128)(2,1)S(1)} %get-tuple-element.170), channel_id=1, source_target_pairs={{0,16},{8,24},{16,0},{24,8},{1,17},{9,25},{17,1},{25,9},{2,18},{10... | collective-permute-start | bytes 393224 | tf_op jit(solution)/shard_map/ppermute | solution.py:271
  231.9 8.9 %collective-permute-start.11 = (bf16[64,1024]{1,0:T(8,128)(2,1)S(1)}, bf16[64,1024]{1,0:T(8,128)(2,1)S(1)}, u32[]{:S(2)}, u32[]{:S(2)}) collective-permute-start(bf16[64,1024]{1,0:T(8,128)(2,1)S(1)} %get-tuple-element.169), channel_id=1, source_target_pairs={{0,24},{8,16},{16,8},{24,0},{1,25},{9,17},{17,9},{25,1},{2,26},{10... | collective-permute-start | bytes 393224 | tf_op jit(solution)/shard_map/ppermute | solution.py:271
  267.6 222.5 %collective-permute-start.33 = (bf16[1152,192]{0,1:T(8,128)(2,1)}, bf16[1152,192]{0,1:T(8,128)(2,1)}, u32[]{:S(2)}, u32[]{:S(2)}) collective-permute-start(bf16[1152,192]{0,1:T(8,128)(2,1)} %get-tuple-element.132), channel_id=1, source_target_pairs={{0,8},{8,0},{16,24},{24,16},{1,9},{9,1},{17,25},{25,17},{2,10},{10... | collective-permute-start | bytes 1327112 | tf_op jit(solution)/shard_map/ppermute | solution.py:271
  267.9 223.7 %collective-permute-start.34 = (bf16[1152,192]{0,1:T(8,128)(2,1)}, bf16[1152,192]{0,1:T(8,128)(2,1)}, u32[]{:S(2)}, u32[]{:S(2)}) collective-permute-start(bf16[1152,192]{0,1:T(8,128)(2,1)} %get-tuple-element.134), channel_id=1, source_target_pairs={{0,16},{8,24},{16,0},{24,8},{1,17},{9,25},{17,1},{25,9},{2,18},{10... | collective-permute-start | bytes 1327112 | tf_op jit(solution)/shard_map/ppermute | solution.py:271
  303.5 36.3 %collective-permute-start.12 = (bf16[64,1024]{1,0:T(8,128)(2,1)S(1)}, bf16[64,1024]{1,0:T(8,128)(2,1)S(1)}, u32[]{:S(2)}, u32[]{:S(2)}) collective-permute-start(bf16[64,1024]{1,0:T(8,128)(2,1)S(1)} %get-tuple-element.149), channel_id=1, source_target_pairs={{0,8},{8,0},{16,24},{24,16},{1,9},{9,1},{17,25},{25,17},{2,10},{10... | collective-permute-start | bytes 393224 | tf_op jit(solution)/shard_map/ppermute | solution.py:271
  304.1 35.9 %collective-permute-start.13 = (bf16[64,1024]{1,0:T(8,128)(2,1)S(1)}, bf16[64,1024]{1,0:T(8,128)(2,1)S(1)}, u32[]{:S(2)}, u32[]{:S(2)}) collective-permute-start(bf16[64,1024]{1,0:T(8,128)(2,1)S(1)} %get-tuple-element.148), channel_id=1, source_target_pairs={{0,16},{8,24},{16,0},{24,8},{1,17},{9,25},{17,1},{25,9},{2,18},{10... | collective-permute-start | bytes 393224 | tf_op jit(solution)/shard_map/ppermute | solution.py:271
  304.1 35.9 %collective-permute-start.14 = (bf16[64,1024]{1,0:T(8,128)(2,1)S(1)}, bf16[64,1024]{1,0:T(8,128)(2,1)}, u32[]{:S(2)}, u32[]{:S(2)}) collective-permute-start(bf16[64,1024]{1,0:T(8,128)(2,1)S(1)} %get-tuple-element.147), channel_id=1, source_target_pairs={{0,24},{8,16},{16,8},{24,0},{1,25},{9,17},{17,9},{25,1},{2,26},{10... | collective-permute-start | bytes 393224 | tf_op jit(solution)/shard_map/ppermute | solution.py:271
  332.2 49.6 %slice-start = ((s8[6291456]{0:T(1024)(128)(4,1)}), s8[4194304]{0:T(1024)(128)(4,1)S(1)}, s32[]{:S(2)}) async-start(s8[6291456]{0:T(1024)(128)(4,1)} %bitcast.245), calls=%async_computation.14 | async-start | bytes 8388608
  339.8 44.8 %collective-permute-start.18 = (bf16[64,1024]{1,0:T(8,128)(2,1)}, bf16[64,1024]{1,0:T(8,128)(2,1)}, u32[]{:S(2)}, u32[]{:S(2)}) collective-permute-start(bf16[64,1024]{1,0:T(8,128)(2,1)} %get-tuple-element.145), channel_id=1, source_target_pairs={{0,8},{8,0},{16,24},{24,16},{1,9},{9,1},{17,25},{25,17},{2,10},{10... | collective-permute-start | bytes 393224 | tf_op jit(solution)/shard_map/ppermute | solution.py:271
  340.0 44.6 %collective-permute-start.19 = (bf16[64,1024]{1,0:T(8,128)(2,1)}, bf16[64,1024]{1,0:T(8,128)(2,1)}, u32[]{:S(2)}, u32[]{:S(2)}) collective-permute-start(bf16[64,1024]{1,0:T(8,128)(2,1)} %get-tuple-element.144), channel_id=1, source_target_pairs={{0,16},{8,24},{16,0},{24,8},{1,17},{9,25},{17,1},{25,9},{2,18},{10... | collective-permute-start | bytes 393224 | tf_op jit(solution)/shard_map/ppermute | solution.py:271
  340.1 44.8 %collective-permute-start.20 = (bf16[64,1024]{1,0:T(8,128)(2,1)S(1)}, bf16[64,1024]{1,0:T(8,128)(2,1)}, u32[]{:S(2)}, u32[]{:S(2)}) collective-permute-start(bf16[64,1024]{1,0:T(8,128)(2,1)S(1)} %get-tuple-element.143), channel_id=1, source_target_pairs={{0,24},{8,16},{16,8},{24,0},{1,25},{9,17},{17,9},{25,1},{2,26},{10... | collective-permute-start | bytes 393224 | tf_op jit(solution)/shard_map/ppermute | solution.py:271
  384.5 260.7 %reduce-scatter.10.cloned.1.call-start = ((), (), s32[]{:S(2)}) async-start(), calls=%async_computation.10 | async-start | bytes 442368 | tf_op jit(solution)/shard_map/reduce_scatter | solution.py:371
  384.6 51.0 %collective-permute-start.24 = (bf16[64,1024]{1,0:T(8,128)(2,1)}, bf16[64,1024]{1,0:T(8,128)(2,1)}, u32[]{:S(2)}, u32[]{:S(2)}) collective-permute-start(bf16[64,1024]{1,0:T(8,128)(2,1)} %get-tuple-element.142), channel_id=1, source_target_pairs={{0,8},{8,0},{16,24},{24,16},{1,9},{9,1},{17,25},{25,17},{2,10},{10... | collective-permute-start | bytes 393224 | tf_op jit(solution)/shard_map/ppermute | solution.py:271
  384.7 51.0 %collective-permute-start.25 = (bf16[64,1024]{1,0:T(8,128)(2,1)}, bf16[64,1024]{1,0:T(8,128)(2,1)}, u32[]{:S(2)}, u32[]{:S(2)}) collective-permute-start(bf16[64,1024]{1,0:T(8,128)(2,1)} %get-tuple-element.141), channel_id=1, source_target_pairs={{0,16},{8,24},{16,0},{24,8},{1,17},{9,25},{17,1},{25,9},{2,18},{10... | collective-permute-start | bytes 393224 | tf_op jit(solution)/shard_map/ppermute | solution.py:271
  384.9 50.8 %collective-permute-start.26 = (bf16[64,1024]{1,0:T(8,128)(2,1)S(1)}, bf16[64,1024]{1,0:T(8,128)(2,1)}, u32[]{:S(2)}, u32[]{:S(2)}) collective-permute-start(bf16[64,1024]{1,0:T(8,128)(2,1)S(1)} %get-tuple-element.140), channel_id=1, source_target_pairs={{0,24},{8,16},{16,8},{24,0},{1,25},{9,17},{17,9},{25,1},{2,26},{10... | collective-permute-start | bytes 393224 | tf_op jit(solution)/shard_map/ppermute | solution.py:271
  435.5 209.7 %reduce-scatter.12.cloned.1.call-start = ((), (), s32[]{:S(2)}) async-start(), calls=%async_computation.11 | async-start | bytes 442368 | tf_op jit(solution)/shard_map/reduce_scatter | solution.py:371
  435.6 56.1 %collective-permute-start.35 = (bf16[1152,192]{0,1:T(8,128)(2,1)}, bf16[1152,192]{0,1:T(8,128)(2,1)}, u32[]{:S(2)}, u32[]{:S(2)}) collective-permute-start(bf16[1152,192]{0,1:T(8,128)(2,1)} %get-tuple-element.133), channel_id=1, source_target_pairs={{0,24},{8,16},{16,8},{24,0},{1,25},{9,17},{17,9},{25,1},{2,26},{10... | collective-permute-start | bytes 1327112 | tf_op jit(solution)/shard_map/ppermute | solution.py:271
  487.0 6.4 collective-permute-start.21
  487.6 11.1 %collective-permute-start.22 = (bf16[192,1024]{1,0:T(8,128)(2,1)}, bf16[192,1024]{1,0:T(8,128)(2,1)}, u32[]{:S(2)}, u32[]{:S(2)}) collective-permute-start(bf16[192,1024]{1,0:T(8,128)(2,1)} %get-tuple-element.153), channel_id=1, source_target_pairs={{0,16},{8,24},{16,0},{24,8},{1,17},{9,25},{17,1},{25,9},{2,18},{10... | collective-permute-start | bytes 1179656 | tf_op jit(solution)/shard_map/ppermute | solution.py:271
  490.1 167.6 %reduce-scatter.16.cloned.1.call-start = ((), (), s32[]{:S(2)}) async-start(), calls=%async_computation.13 | async-start | bytes 663552
  490.2 88.3 %collective-permute-start.30 = (bf16[768,768]{1,0:T(8,128)(2,1)}, bf16[768,768]{1,0:T(8,128)(2,1)}, u32[]{:S(2)}, u32[]{:S(2)}) collective-permute-start(bf16[768,768]{1,0:T(8,128)(2,1)} %bitcast.261), channel_id=1, source_target_pairs={{0,8},{8,0},{16,24},{24,16},{1,9},{9,1},{17,25},{25,17},{2,10},{10... | collective-permute-start | bytes 3538952 | tf_op jit(solution)/shard_map/ppermute | solution.py:271
  491.6 68.1 %copy-start.32 = (bf16[4,3,1,64,768]{4,3,2,1,0:T(8,128)(2,1)S(1)}, bf16[4,3,1,64,768]{4,3,2,1,0:T(8,128)(2,1)}, u32[]{:S(2)}) copy-start(bf16[4,3,1,64,768]{4,3,2,1,0:T(8,128)(2,1)} %get-tuple-element.126) | copy-start | bytes 3538948
  491.6 91.5 %collective-permute-start.31 = (bf16[768,768]{1,0:T(8,128)(2,1)}, bf16[768,768]{1,0:T(8,128)(2,1)S(1)}, u32[]{:S(2)}, u32[]{:S(2)}) collective-permute-start(bf16[768,768]{1,0:T(8,128)(2,1)} %bitcast.237), channel_id=1, source_target_pairs={{0,16},{8,24},{16,0},{24,8},{1,17},{9,25},{17,1},{25,9},{2,18},{10... | collective-permute-start | bytes 3538952 | tf_op jit(solution)/shard_map/ppermute | solution.py:271
  491.8 91.4 %collective-permute-start.32 = (bf16[768,768]{1,0:T(8,128)(2,1)}, bf16[768,768]{1,0:T(8,128)(2,1)}, u32[]{:S(2)}, u32[]{:S(2)}) collective-permute-start(bf16[768,768]{1,0:T(8,128)(2,1)} %bitcast.236), channel_id=1, source_target_pairs={{0,24},{8,16},{16,8},{24,0},{1,25},{9,17},{17,9},{25,1},{2,26},{10... | collective-permute-start | bytes 3538952 | tf_op jit(solution)/shard_map/ppermute | solution.py:271
  493.4 64.3 %collective-permute-start.23 = (bf16[192,1024]{1,0:T(8,128)(2,1)}, bf16[192,1024]{1,0:T(8,128)(2,1)}, u32[]{:S(2)}, u32[]{:S(2)}) collective-permute-start(bf16[192,1024]{1,0:T(8,128)(2,1)} %get-tuple-element.152), channel_id=1, source_target_pairs={{0,24},{8,16},{16,8},{24,0},{1,25},{9,17},{17,9},{25,1},{2,26},{10... | collective-permute-start | bytes 1179656 | tf_op jit(solution)/shard_map/ppermute | solution.py:271
  498.6 60.4 %collective-permute-start.15 = (bf16[192,1024]{1,0:T(8,128)(2,1)}, bf16[192,1024]{1,0:T(8,128)(2,1)}, u32[]{:S(2)}, u32[]{:S(2)}) collective-permute-start(bf16[192,1024]{1,0:T(8,128)(2,1)} %get-tuple-element.158), channel_id=1, source_target_pairs={{0,8},{8,0},{16,24},{24,16},{1,9},{9,1},{17,25},{25,17},{2,10},{10... | collective-permute-start | bytes 1179656 | tf_op jit(solution)/shard_map/ppermute | solution.py:271
  502.5 196.7 %reduce-scatter.14.cloned.1.call-start = ((), (), s32[]{:S(2)}) async-start(), calls=%async_computation.12 | async-start | bytes 1327104 | tf_op jit(solution)/shard_map/reduce_scatter | solution.py:371
  557.7 10.7 %collective-permute-start.16 = (bf16[192,1024]{1,0:T(8,128)(2,1)}, bf16[192,1024]{1,0:T(8,128)(2,1)S(1)}, u32[]{:S(2)}, u32[]{:S(2)}) collective-permute-start(bf16[192,1024]{1,0:T(8,128)(2,1)} %get-tuple-element.157), channel_id=1, source_target_pairs={{0,16},{8,24},{16,0},{24,8},{1,17},{9,25},{17,1},{25,9},{2,18},{10... | collective-permute-start | bytes 1179656 | tf_op jit(solution)/shard_map/ppermute | solution.py:271
  559.0 18.2 %collective-permute-start.17 = (bf16[192,1024]{1,0:T(8,128)(2,1)}, bf16[192,1024]{1,0:T(8,128)(2,1)S(1)}, u32[]{:S(2)}, u32[]{:S(2)}) collective-permute-start(bf16[192,1024]{1,0:T(8,128)(2,1)} %get-tuple-element.156), channel_id=1, source_target_pairs={{0,24},{8,16},{16,8},{24,0},{1,25},{9,17},{17,9},{25,1},{2,26},{10... | collective-permute-start | bytes 1179656 | tf_op jit(solution)/shard_map/ppermute | solution.py:271
  568.4 19.4 %collective-permute-start.27 = (bf16[192,1024]{1,0:T(8,128)(2,1)}, bf16[192,1024]{1,0:T(8,128)(2,1)}, u32[]{:S(2)}, u32[]{:S(2)}) collective-permute-start(bf16[192,1024]{1,0:T(8,128)(2,1)} %get-tuple-element.138), channel_id=1, source_target_pairs={{0,8},{8,0},{16,24},{24,16},{1,9},{9,1},{17,25},{25,17},{2,10},{10... | collective-permute-start | bytes 1179656 | tf_op jit(solution)/shard_map/ppermute | solution.py:271
  577.2 11.1 %collective-permute-start.28 = (bf16[192,1024]{1,0:T(8,128)(2,1)}, bf16[192,1024]{1,0:T(8,128)(2,1)}, u32[]{:S(2)}, u32[]{:S(2)}) collective-permute-start(bf16[192,1024]{1,0:T(8,128)(2,1)} %get-tuple-element.137), channel_id=1, source_target_pairs={{0,16},{8,24},{16,0},{24,8},{1,17},{9,25},{17,1},{25,9},{2,18},{10... | collective-permute-start | bytes 1179656 | tf_op jit(solution)/shard_map/ppermute | solution.py:271
  578.5 18.6 %collective-permute-start.29 = (bf16[192,1024]{1,0:T(8,128)(2,1)}, bf16[192,1024]{1,0:T(8,128)(2,1)}, u32[]{:S(2)}, u32[]{:S(2)}) collective-permute-start(bf16[192,1024]{1,0:T(8,128)(2,1)} %get-tuple-element.136), channel_id=1, source_target_pairs={{0,24},{8,16},{16,8},{24,0},{1,25},{9,17},{17,9},{25,1},{2,26},{10... | collective-permute-start | bytes 1179656 | tf_op jit(solution)/shard_map/ppermute | solution.py:271
  (51 other events, 359.6 us)
Sparse Core Ops, SparseCore 0:
  10.2 50.6 all-gather.6
  63.1 63.0 all-gather.8
  128.3 44.1 all-gather.10
  174.5 64.3 all-gather.12
  384.6 55.2 reduce-scatter.7
  443.1 60.4 reduce-scatter.9
  506.8 60.3 reduce-scatter.11
  571.1 61.1 reduce-scatter.15
  636.1 63.1 reduce-scatter.13

commit v2 on v1

v2 whole, which is shorter than its diff:
```python
import functools

import jax
import jax.numpy as jnp
from jax import lax
from jax.experimental import pallas as pl
from jax.experimental.pallas import tpu as pltpu
from jax.sharding import PartitionSpec as P

D = 768
HEADS = 12
HD = 64

epsilon = 1e-05
rope_base = 160000.0
masked_score = -1e30
LOG2E = 1.4426950408889634
LN2 = 0.6931471805599453

bf = jnp.bfloat16
f32 = jnp.float32
NN = ((1,), (0,))
NT = ((1,), (1,))
TN = ((0,), (0,))


def dg(a, b, dims):
    return lax.dot_general(a, b, (dims, ((), ())), preferred_element_type=f32)


def unit_rows_of(x):
    centred = x - jnp.mean(x, axis=-1, keepdims=True)
    inverse = lax.rsqrt(jnp.mean(centred * centred, axis=-1, keepdims=True) + epsilon)
    return centred * inverse, inverse


def qkv_kernel(heads, count, info_ref, x_ref, cos_ref, sin_ref, *refs):
    parts = refs[:count]
    n_ref, k_ref, v_ref, qt_ref, kt_ref, vt_ref, w_ref, g_ref = refs[-8:]
    rb = x_ref.shape[0]
    value_at = heads * 128

    @pl.when(pl.program_id(0) == 0)
    def _():
        shard = parts[0].shape[0]
        for j in range(count):
            start = pl.multiple_of((info_ref[2] ^ j) * shard, shard) if count > 1 else 0
            w_ref[pl.ds(start, shard), :] = parts[j][...]
        last = w_ref[:, w_ref.shape[1] - 128 :].astype(f32).T
        g_ref[...] = last[HD : HD + 8]

    unit, _ = unit_rows_of(x_ref[...].astype(f32))
    normed = (unit * g_ref[:1]).astype(bf)
    n_ref[...] = normed
    lane = lax.broadcasted_iota(jnp.int32, (rb, 128), 1)
    row = lax.broadcasted_iota(jnp.int32, (rb, 128), 0)
    position = info_ref[0] + pl.program_id(0) * rb + row
    bias = jnp.where(position < info_ref[1], 0.0, masked_score)
    key_tail = jnp.where(lane == HD, bias, 0.0)
    value_tail = jnp.where(lane < HD + 2, -1.0, 0.0)
    head_lane = lane < HD
    lower = (lane & (HD - 1)) < HD // 2
    one_row = jnp.where(lax.broadcasted_iota(jnp.int32, (HD, rb), 0) == 0, 1.0, 0.0).astype(bf)
    y = dg(normed, w_ref[...], NN)
    for h in range(heads):
        t = y[:, h * 128 : (h + 1) * 128]
        turned = jnp.where(lower, pltpu.roll(t, 128 - HD // 2, 1), pltpu.roll(t, HD // 2, 1))
        t = t * cos_ref[...] + turned * sin_ref[...]
        k_ref[h] = jnp.where(head_lane, pltpu.roll(t, HD, 1), key_tail).astype(bf)
        t = t.T.astype(bf)
        qt_ref[h, :HD] = t[:HD]
        qt_ref[h, HD:] = one_row
        kt_ref[h] = t[HD:]
    for h in range(heads):
        at = value_at + h // 2 * 128
        t = y[:, at : at + 128]
        turned = t if h % 2 == 0 else pltpu.roll(t, HD, 1)
        v_ref[h] = jnp.where(head_lane, turned, value_tail).astype(bf)
        if h % 2 == 0:
            t_rows = t.T.astype(bf)
        vt_ref[h, :HD] = t_rows[:HD] if h % 2 == 0 else t_rows[HD:]
        vt_ref[h, HD:] = one_row[:16]


def qkv_call(block, blocks, heads, info, x, cos, sin, parts, carried):
    rows = x.shape[0]
    S = rows * blocks
    rb = min(256, rows)
    steps = rows // rb
    width = parts[0].shape[1]
    at = lambda i: block * steps + i
    outs = (
        jax.ShapeDtypeStruct((S, D), bf),
        jax.ShapeDtypeStruct((heads, S, 128), bf),
        jax.ShapeDtypeStruct((heads, S, 128), bf),
        jax.ShapeDtypeStruct((heads, 128, S), bf),
        jax.ShapeDtypeStruct((heads, HD, S), bf),
        jax.ShapeDtypeStruct((heads, 80, S), bf),
    )
    in_specs = [
        pl.BlockSpec(memory_space=pltpu.SMEM),
        pl.BlockSpec((rb, D), lambda i: (i, 0)),
        pl.BlockSpec((rb, 128), lambda i: (at(i), 0)),
        pl.BlockSpec((rb, 128), lambda i: (at(i), 0)),
    ] + [pl.BlockSpec(part.shape, lambda i: (0, 0)) for part in parts]
    aliases = {}
    if carried is not None:
        first = len(in_specs)
        in_specs += [pl.BlockSpec(memory_space=pl.ANY)] * 6
        aliases = {first + n: n for n in range(6)}
    return pl.pallas_call(
        functools.partial(qkv_kernel, heads, len(parts)),
        grid=(steps,),
        out_shape=outs,
        in_specs=in_specs,
        out_specs=(
            pl.BlockSpec((rb, D), lambda i: (at(i), 0)),
            pl.BlockSpec((heads, rb, 128), lambda i: (0, at(i), 0)),
            pl.BlockSpec((heads, rb, 128), lambda i: (0, at(i), 0)),
            pl.BlockSpec((heads, 128, rb), lambda i: (0, 0, at(i))),
            pl.BlockSpec((heads, HD, rb), lambda i: (0, 0, at(i))),
            pl.BlockSpec((heads, 80, rb), lambda i: (0, 0, at(i))),
        ),
        scratch_shapes=[pltpu.VMEM((D, width), bf), pltpu.VMEM((8, D), f32)],
        input_output_aliases=aliases,
        compiler_params=pltpu.CompilerParams(vmem_limit_bytes=48 * 2**20),
        cost_estimate=pl.CostEstimate(
            flops=4 * rows * D * width, bytes_accessed=rows * 8192, transcendentals=0
        ),
        name="qkv",
    )(info, x, cos, sin, *parts, *(carried or ()))


def attend_kernel(kc, k_ref, q_ref, v_ref, p_ref, o_ref, ob_ref, linv_ref, s_ref):
    rows = k_ref.shape[1]
    bq = q_ref.shape[2]
    q = q_ref[0]
    m = jnp.full((8, bq), -jnp.inf, f32)
    for c in range(rows // kc):
        at = slice(c * kc, (c + 1) * kc)
        s = dg(k_ref[0, at, :], q, NN)
        s_ref[at, :] = s
        m = jnp.maximum(m, jnp.max(s.reshape(kc // 8, 8, bq), axis=0))
    m = jnp.max(m, axis=0, keepdims=True)
    acc = jnp.zeros((v_ref.shape[1], bq), f32)
    for c in range(rows // kc):
        at = slice(c * kc, (c + 1) * kc)
        p = jnp.exp2(s_ref[at, :] - m).astype(bf)
        p_ref[0, at, :] = p
        acc = acc + dg(v_ref[0, :, at], p, NN)
    linv = 1.0 / acc[HD : HD + 1, :]
    o = acc[:HD, :] * linv
    o_ref[...] = o
    ob_ref[0] = o.astype(bf)
    linv_ref[0] = linv


def attend(h, k, qt, vt, groups, bq=512, kc=512):
    S = k.shape[1]
    nq = S // bq
    per = nq // groups
    return pl.pallas_call(
        functools.partial(attend_kernel, kc),
        grid=(nq,),
        out_shape=(
            jax.ShapeDtypeStruct((nq, S, bq), bf),
            jax.ShapeDtypeStruct((HD, S), f32),
            jax.ShapeDtypeStruct((groups, HD, S // groups), bf),
            jax.ShapeDtypeStruct((nq, 1, bq), f32),
        ),
        in_specs=[
            pl.BlockSpec((1, S, 128), lambda i: (h, 0, 0)),
            pl.BlockSpec((1, 128, bq), lambda i: (h, 0, i)),
            pl.BlockSpec((1, 80, S), lambda i: (h, 0, 0)),
        ],
        out_specs=(
            pl.BlockSpec((1, S, bq), lambda i: (i, 0, 0)),
            pl.BlockSpec((HD, bq), lambda i: (0, i)),
            pl.BlockSpec((1, HD, bq), lambda i: (i // per, 0, i % per)),
            pl.BlockSpec((1, 1, bq), lambda i: (i, 0, 0)),
        ),
        scratch_shapes=[pltpu.VMEM((S, bq), f32)],
        compiler_params=pltpu.CompilerParams(vmem_limit_bytes=48 * 2**20),
        cost_estimate=pl.CostEstimate(
            flops=16 * HD * S * S, bytes_accessed=2 * S * S, transcendentals=S * S
        ),
        name="attend",
    )(k, qt, vt)


def attend_back_kernel(
    kc, nq, per, v_ref, kt_ref, q_ref, o_ref, linv_ref, p_ref, cos_ref, sin_ref, *refs
):
    out_ref, acc_ref, do_ref = refs[-3:]
    i = pl.program_id(0)
    rows = v_ref.shape[1]
    bq = q_ref.shape[2]

    @pl.when(i == 0)
    def _():
        acc_ref[...] = jnp.zeros_like(acc_ref)
        for j in range(len(refs) - 3):
            do_ref[j] = refs[j][...]

    do = do_ref[i // per, :, pl.ds(pl.multiple_of((i % per) * bq, bq), bq)]
    dop = (do.astype(f32) * linv_ref[0]).astype(bf)
    delta = jnp.sum(dop.astype(f32) * o_ref[...], axis=0, keepdims=True)
    high = delta.astype(bf).astype(f32)
    r = lax.broadcasted_iota(jnp.int32, (16, bq), 0)
    tail = jnp.where(r == 0, high, jnp.where(r == 1, delta - high, 0.0)).astype(bf)
    doe = jnp.concatenate([dop, tail, jnp.zeros((128 - HD - 16, bq), bf)], axis=0)
    zero = jnp.zeros((HD, bq), bf)
    right_v = jnp.concatenate([dop, zero], axis=0)
    right_k = jnp.concatenate([zero, q_ref[0, :HD, :]], axis=0)
    dq = jnp.zeros((HD, bq), f32)
    for c in range(rows // kc):
        at = slice(c * kc, (c + 1) * kc)
        p = p_ref[0, at, :]
        ds = p * dg(v_ref[0, at, :], doe, NN).astype(bf)
        acc_ref[at, :] = acc_ref[at, :] + dg(p, right_v, NT) + dg(ds, right_k, NT)
        dq = dq + dg(kt_ref[0, :, at], ds, NN)
    dq = dq * HD**-0.5
    turned = jnp.concatenate([dq[HD // 2 :], -dq[: HD // 2]], axis=0)
    here = pl.ds(pl.multiple_of(i * bq, bq), bq)
    dq = dq * cos_ref[:, here] + turned * sin_ref[:, here]
    out_ref[i // per, :HD, pl.ds(pl.multiple_of((i % per) * bq, bq), bq)] = dq.astype(bf)

    @pl.when(i == nq - 1)
    def _():
        groups = out_ref.shape[0]
        width = rows // groups
        for j in range(groups):
            at = slice(j * width, (j + 1) * width)
            t = acc_ref[at, :].T
            dk = t[HD:] * LN2
            turned_k = jnp.concatenate([dk[HD // 2 :], -dk[: HD // 2]], axis=0)
            dk = dk * cos_ref[:, at] + turned_k * sin_ref[:, at]
            out_ref[j, HD : 2 * HD] = dk.astype(bf)
            out_ref[j, 2 * HD :] = t[:HD].astype(bf)


def attend_back(h, v, kt, qt, do, o, linv, p, cos, sin, groups, bq=512, kc=512):
    S = v.shape[1]
    nq = S // bq
    per = nq // groups
    return pl.pallas_call(
        functools.partial(attend_back_kernel, kc, nq, per),
        grid=(nq,),
        out_shape=jax.ShapeDtypeStruct((groups, 3 * HD, S // groups), bf),
        in_specs=[
            pl.BlockSpec((1, S, 128), lambda i: (h, 0, 0)),
            pl.BlockSpec((1, HD, S), lambda i: (h, 0, 0)),
            pl.BlockSpec((1, 128, bq), lambda i: (h, 0, i)),
            pl.BlockSpec((HD, bq), lambda i: (0, i)),
            pl.BlockSpec((1, 1, bq), lambda i: (i, 0, 0)),
            pl.BlockSpec((1, S, bq), lambda i: (i, 0, 0)),
            pl.BlockSpec((HD, S), lambda i: (0, 0)),
            pl.BlockSpec((HD, S), lambda i: (0, 0)),
        ]
        + [pl.BlockSpec((HD, S // groups), lambda i: (0, 0))] * groups,
        out_specs=pl.BlockSpec((groups, 3 * HD, S // groups), lambda i: (0, 0, 0)),
        scratch_shapes=[pltpu.VMEM((S, 128), f32), pltpu.VMEM((groups, HD, S // groups), bf)],
        compiler_params=pltpu.CompilerParams(vmem_limit_bytes=48 * 2**20),
        cost_estimate=pl.CostEstimate(
            flops=24 * HD * S * S, bytes_accessed=2 * S * S, transcendentals=0
        ),
        name="attend_back",
    )(v, kt, qt, o, linv, p, cos, sin, *do)


def normalize_back(gradient, unit_rows, inverse, gain_row):
    scaled = gradient * gain_row
    return inverse * (
        scaled
        - jnp.mean(scaled, axis=-1, keepdims=True)
        - unit_rows * jnp.mean(scaled * unit_rows, axis=-1, keepdims=True)
    )


def middle_kernel(
    groups, heads, ff, info_ref, x_ref, dy_ref, w_ref, out_w_ref, *refs
):
    count = groups * heads
    chunks = refs[:count]
    (result_ref, dh_ref, dheads_ref, mixed_ref, second_ref, dgu_ref, inner_ref, branch_ref,
     g_ref, t_ref) = refs[count:]
    width = heads * HD
    me = info_ref[0]

    @pl.when(pl.program_id(0) == 0)
    def _():
        g_ref[...] = w_ref[:, 2 * ff + D :].astype(f32).T[:8]

    for h in range(heads):
        for j in range(groups):
            start = pl.multiple_of((me ^ j) * width + h * HD, HD)
            mixed_ref[pl.ds(start, HD), :] = chunks[h * groups + j][...]
    gain = g_ref[:1]
    proj = w_ref[:, 2 * ff : 2 * ff + D]
    hidden = x_ref[...].astype(f32) + dg(mixed_ref[...], proj, TN)
    unit, inverse = unit_rows_of(hidden)
    second = (unit * gain).astype(bf)
    second_ref[...] = second
    dy = dy_ref[...]
    result = hidden
    d_second = jnp.zeros_like(hidden)
    step = 384
    for c in range(ff // step):
        a = slice(c * step, (c + 1) * step)
        b = slice(ff + c * step, ff + (c + 1) * step)
        gate = dg(second, w_ref[:, a], NN)
        up = dg(second, w_ref[:, b], NN)
        d_inner = dg(dy, out_w_ref[a, :], NT)
        bell = 0.5 + 0.5 * lax.erf(gate * 0.7071067811865476)
        gelu = gate * bell
        inner = (gelu * up).astype(bf)
        inner_ref[:, a] = inner
        result = result + dg(inner, out_w_ref[a, :], NN)
        slope = bell + gate * (jnp.exp(-0.5 * gate * gate) * 0.3989422804014327)
        d_gate = (d_inner * up * slope).astype(bf)
        d_up = (d_inner * gelu).astype(bf)
        dgu_ref[:, a] = d_gate
        dgu_ref[:, b] = d_up
        d_second = d_second + dg(d_gate, w_ref[:, a], NT) + dg(d_up, w_ref[:, b], NT)
    result_ref[...] = result.astype(bf)
    d_hidden = dy.astype(f32) + normalize_back(d_second, unit, inverse, gain)
    dh_ref[...] = d_hidden
    branch = d_hidden.astype(bf)
    branch_ref[...] = branch
    t_ref[...] = dg(proj, branch, NT).astype(bf)
    for h in range(heads):
        for j in range(groups):
            start = pl.multiple_of((me ^ j) * width + h * HD, HD)
            dheads_ref[h, j] = t_ref[pl.ds(start, HD), :]


def middle(groups, heads, info, x, dy, wide, out_w, chunks):
    rows = x.shape[0]
    ff = out_w.shape[0]
    rb = min(256, rows)
    by_row = lambda i: (i, 0)
    by_column = lambda i: (0, i)
    whole = lambda i: (0, 0)
    return pl.pallas_call(
        functools.partial(middle_kernel, groups, heads, ff),
        grid=(rows // rb,),
        out_shape=(
            jax.ShapeDtypeStruct((rows, D), bf),
            jax.ShapeDtypeStruct((rows, D), f32),
            jax.ShapeDtypeStruct((heads, groups, HD, rows), bf),
            jax.ShapeDtypeStruct((D, rows), bf),
            jax.ShapeDtypeStruct((rows, D), bf),
            jax.ShapeDtypeStruct((rows, 2 * ff), bf),
            jax.ShapeDtypeStruct((rows, ff), bf),
            jax.ShapeDtypeStruct((rows, D), bf),
        ),
        in_specs=[
            pl.BlockSpec(memory_space=pltpu.SMEM),
            pl.BlockSpec((rb, D), by_row),
            pl.BlockSpec((rb, D), by_row),
            pl.BlockSpec(wide.shape, whole, pipeline_mode=pl.Buffered(1)),
            pl.BlockSpec(out_w.shape, whole, pipeline_mode=pl.Buffered(1)),
        ]
        + [pl.BlockSpec((HD, rb), by_column)] * (groups * heads),
        out_specs=(
            pl.BlockSpec((rb, D), by_row),
            pl.BlockSpec((rb, D), by_row),
            pl.BlockSpec((heads, groups, HD, rb), lambda i: (0, 0, 0, i)),
            pl.BlockSpec((D, rb), by_column),
            pl.BlockSpec((rb, D), by_row),
            pl.BlockSpec((rb, 2 * ff), by_row),
            pl.BlockSpec((rb, ff), by_row),
            pl.BlockSpec((rb, D), by_row),
        ),
        scratch_shapes=[pltpu.VMEM((8, D), f32), pltpu.VMEM((D, rb), bf)],
        compiler_params=pltpu.CompilerParams(vmem_limit_bytes=48 * 2**20),
        cost_estimate=pl.CostEstimate(
            flops=rows * D * (14 * ff + 4 * D), bytes_accessed=30 * 2**20, transcendentals=rows * ff
        ),
        name="middle",
    )(info, x, dy, wide, out_w, *chunks)


def last_kernel(groups, heads, info_ref, x_ref, dh_ref, w_ref, *refs):
    count = groups * heads
    out_ref, dp_ref, g_ref = refs[count:]
    me = info_ref[0]

    @pl.when(pl.program_id(0) == 0)
    def _():
        g_ref[...] = w_ref[:, 3 * D :].astype(f32).T[:8]

    width = heads * HD
    for h in range(heads):
        for j in range(groups):
            for t in range(3):
                start = pl.multiple_of(t * D + (me ^ j) * width + h * HD, HD)
                dp_ref[pl.ds(start, HD), :] = refs[h * groups + j][t * HD : (t + 1) * HD, :]
    d_normed = dg(w_ref[:, : 3 * D], dp_ref[...], NN).T
    unit, inverse = unit_rows_of(x_ref[...].astype(f32))
    out_ref[...] = dh_ref[...] + normalize_back(d_normed, unit, inverse, g_ref[:1])


def last(groups, heads, info, x, d_hidden, w, chunks):
    rows = x.shape[0]
    rb = min(256, rows)
    by_row = lambda i: (i, 0)
    whole = lambda i: (0, 0)
    return pl.pallas_call(
        functools.partial(last_kernel, groups, heads),
        grid=(rows // rb,),
        out_shape=jax.ShapeDtypeStruct((rows, D), f32),
        in_specs=[
            pl.BlockSpec(memory_space=pltpu.SMEM),
            pl.BlockSpec((rb, D), by_row),
            pl.BlockSpec((rb, D), by_row),
            pl.BlockSpec(w.shape, whole, pipeline_mode=pl.Buffered(1)),
        ]
        + [pl.BlockSpec((3 * HD, rb), lambda i: (0, i))] * (groups * heads),
        out_specs=pl.BlockSpec((rb, D), by_row),
        scratch_shapes=[pltpu.VMEM((3 * D, rb), bf), pltpu.VMEM((8, D), f32)],
        compiler_params=pltpu.CompilerParams(vmem_limit_bytes=48 * 2**20),
        cost_estimate=pl.CostEstimate(
            flops=6 * rows * D * D, bytes_accessed=16 * 2**20, transcendentals=0
        ),
        name="last",
    )(info, x, d_hidden, w, *chunks)


def body(
    tokens, lengths, attn_gain, qkv_weight, proj_weight, ffn_gain, in_weight, out_weight, out_grad
):
    rows = tokens.shape[1]
    groups = lax.axis_size("seq")
    shards = lax.axis_size("fsdp")
    heads = HEADS // groups
    shard = D // shards
    me = lax.axis_index("seq")
    owner = lax.axis_index("fsdp")

    def swap(array, j, axis="seq"):
        size = lax.axis_size(axis)
        return lax.ppermute(array, axis, [(i, i ^ j) for i in range(size)])

    def exchange(chunks):
        return [chunks[0]] + [swap(chunks[j], j) for j in range(1, groups)]

    def relative(array, axis):
        return [lax.dynamic_index_in_dim(array, me ^ j, axis, False) for j in range(groups)]

    def gather(array):
        return lax.all_gather(array, "fsdp", axis=0, tiled=True)

    own = lax.dynamic_index_in_dim(
        qkv_weight.reshape(shard, 3, groups, heads, HD), me, 2, False
    )
    pieces = []
    for h in range(heads):
        pieces += [own[:, 0, h], own[:, 1, h]]
    pieces += [own[:, 2, h] for h in range(heads)] + [attn_gain[:, None]]
    used = 3 * heads * HD + 1
    pieces.append(jnp.zeros((shard, -used % 128), bf))
    own = jnp.concatenate(pieces, axis=1)
    if shards <= 8:
        parts = [own] + [swap(own, j, "fsdp") for j in range(1, shards)]
    else:
        parts = [gather(own)]

    x0 = tokens[0]
    blocks = [x0]
    step = 1
    while step < groups:
        blocks = blocks + [swap(b, step) for b in blocks]
        step *= 2

    half = HD // 2
    frequency = rope_base ** (-(lax.iota(f32, half) * 2.0) / HD)
    starts = [(me ^ j) * rows for j in range(groups)]
    positions = jnp.concatenate([s + lax.iota(jnp.int32, rows) for s in starts]).astype(f32)
    angles = frequency[:, None] * positions[None, :]
    cosine, sine = jnp.cos(angles), jnp.sin(angles)
    cos_t = jnp.concatenate([cosine, cosine], axis=0)
    sin_t = jnp.concatenate([sine, sine], axis=0)
    scale = HD**-0.5 * LOG2E
    cos_rows = jnp.concatenate([cos_t * scale, cos_t], axis=0).T
    signed = jnp.concatenate([-sine, sine], axis=0)
    sin_rows = jnp.concatenate([signed * scale, signed], axis=0).T

    carried = None
    for j in range(groups):
        info = jnp.stack([starts[j], lengths[0], owner]).astype(jnp.int32)
        carried = qkv_call(j, groups, heads, info, blocks[j], cos_rows, sin_rows, parts, carried)
    normed, k, v, qt, kt, vt = carried

    ff2 = in_weight.shape[1]
    wide_shard = jnp.concatenate(
        [in_weight, proj_weight, ffn_gain[:, None], jnp.zeros((shard, 127), bf)], axis=1
    )
    wide_shard, out_shard, qkv_shard, gain_shard, _ = lax.optimization_barrier(
        (wide_shard, out_weight, qkv_weight, attn_gain, parts[-1])
    )
    wide = gather(wide_shard)
    out_full = gather(out_shard)
    qkv_full = gather(jnp.concatenate([qkv_shard, jnp.tile(gain_shard[:, None], (1, 128))], axis=1))

    kept = []
    chunks = []
    for h in range(heads):
        p, o, ob, linv = attend(h, k, qt, vt, groups)
        kept.append((p, o, linv))
        chunks += exchange([ob[j] for j in range(groups)])

    place = jnp.stack([me]).astype(jnp.int32)
    dy = out_grad[0]
    result, d_hidden, d_heads, mixed_t, second, d_gate_up, inner, branch = middle(
        groups, heads, place, x0, dy, wide, out_full, chunks
    )
    d_mixed = [exchange([d_heads[h, j] for j in range(groups)]) for h in range(heads)]

    def over_seq(array):
        parts = array.astype(bf).reshape(array.shape[0], groups, -1)
        mine = relative(parts, 1)
        total = mine[0].astype(f32)
        for j in range(1, groups):
            total = total + swap(mine[j], j).astype(f32)
        return total.astype(bf)

    def to_owner(array):
        parts = array.reshape(shards, array.shape[0] // shards, -1)
        parts = lax.all_to_all(parts, "fsdp", split_axis=0, concat_axis=0, tiled=True)
        return jnp.sum(parts.astype(f32), axis=0).astype(bf)

    def from_seq(array):
        parts = jnp.stack([array] + [swap(array, j) for j in range(1, groups)])
        return relative(parts, 0)

    grad_out = dg(inner, dy, TN)
    grad_in = dg(second, d_gate_up, TN)
    grad_proj = dg(mixed_t, branch, NN)
    part_in = to_owner(over_seq(jnp.concatenate([grad_in, grad_proj], axis=1)))
    part_out = to_owner(over_seq(grad_out))
    wide_grad = jnp.concatenate(from_seq(part_in), axis=1).astype(f32)
    out_weight_grad = jnp.concatenate(from_seq(part_out), axis=1).astype(f32)
    in_weight_grad, proj_weight_grad = wide_grad[:, :ff2], wide_grad[:, ff2:]

    normed_blocks = normed.reshape(groups, rows, D)
    received = []
    qkv_parts = []
    for h in range(heads):
        p, o, linv = kept[h]
        d_own = attend_back(h, v, kt, qt, d_mixed[h], o, linv, p, cos_t, sin_t, groups)
        received += exchange([d_own[j] for j in range(groups)])
        grad = jnp.einsum("jdp,jpf->fd", d_own, normed_blocks, preferred_element_type=f32)
        qkv_parts.append(to_owner(grad.astype(bf)))
    qkv_all = jnp.stack(from_seq(jnp.stack(qkv_parts)))
    qkv_weight_grad = (
        qkv_all.reshape(groups, heads, shard, 3, HD)
        .transpose(2, 3, 0, 1, 4)
        .reshape(shard, 3 * D)
        .astype(f32)
    )
    tokens_grad = last(groups, heads, place, x0, d_hidden, qkv_full, received)

    def gain_grad(weight, grad, gain):
        return jnp.sum(weight.astype(f32) * grad, axis=1) / gain.astype(f32)

    return (
        result[None],
        tokens_grad[None],
        gain_grad(qkv_weight, qkv_weight_grad, attn_gain),
        qkv_weight_grad,
        proj_weight_grad,
        gain_grad(in_weight, in_weight_grad, ffn_gain),
        in_weight_grad,
        out_weight_grad,
    )


def solution(mesh):
    in_specs = (
        P("fsdp", "seq", None),
        P("fsdp"),
        P("fsdp"),
        P("fsdp", None),
        P("fsdp", None),
        P("fsdp"),
        P("fsdp", None),
        P("fsdp", None),
        P("fsdp", "seq", None),
    )
    out_specs = (
        P("fsdp", "seq", None),
        P("fsdp", "seq", None),
        P("fsdp"),
        P("fsdp", None),
        P("fsdp", None),
        P("fsdp"),
        P("fsdp", None),
        P("fsdp", None),
    )
    return jax.shard_map(body, mesh=mesh, in_specs=in_specs, out_specs=out_specs, check_vma=False)
```

time: 725 us -> 587 us (0.81)
  blocking collectives: 109 us -> 0 us
  waiting for transfers between devices: 128 us -> 76.7 us
  matrix products: 74.7 us -> 24.2 us
  starting transfers between devices: 38.5 us -> 76.4 us
  Pallas kernels: 238 us -> 274 us
    all_gather x4 -> x0, blocking collectives: 55.6 us -> none  [the longest x1 30 us: gather(): return lax.all_gather(array, 'fsdp', axis=0, tiled=True)]
    dot_general x12 -> x3, matrix products: 61.4 us -> 9.72 us  [dg(): return lax.dot_general(a, b, (dims, ((), ())), preferred_element_type=f32)]
    psum x1 -> x0, blocking collectives: 35.8 us -> none  [body(): lax.psum(jnp.stack([grad_attn_gain, grad_ffn_gain]), ('seq', 'fsdp'))]
    pallas_call x4 -> x6, Pallas kernels: 28 us -> 63.6 us  [the longest x1 28.1 us: middle(): pl.pallas_call(functools.partial(middle_kernel, groups, heads, ff), grid=...]
    reduce_scatter x4 -> x0, waiting for transfers between devices: 33.2 us -> none  [to_owner(): return lax.psum_scatter(array, 'fsdp', scatter_dimension=0, tiled=True)]
    all_to_all x0 -> x5, starting transfers between devices: none -> 28.2 us  [to_owner(): lax.all_to_all(parts, 'fsdp', split_axis=0, concat_axis=0, tiled=True)]
    ppermute x36 -> x52, waiting for transfers between devices: 92.4 us -> 66.5 us  [swap(): return lax.ppermute(array, axis, [(i, i ^ j) for i in range(size)])]
    unnamed x1 -> x0, blocking collectives: 17.3 us -> none
  transfers between devices with their start and end apart: 45 -> 60, of which waited for: 13 -> 16; matrix products, arithmetic and copies ran while one was open for 23% -> 20% of each run, Pallas kernels for 33% -> 47%
where the time goes in v2:
time: 587 us; the launch traced here: 581 us
  Pallas kernels  274 us (47%)
  local copies, waits for them, and re-layouts  78.5 us (13%)
  waiting for transfers between devices  76.7 us (13%)
  starting transfers between devices  76.4 us (13%)
  other arithmetic  35.7 us (6%)
  matrix products  24.2 us (4%)
  between operations  15.4 us (3%)
    pallas_call x3, Pallas kernels, attend_back(): pl.pallas_call(functools.partial(attend_back_kernel, kc, nq, per), grid=(...  116 us
    pallas_call x3, Pallas kernels, attend(): pl.pallas_call(functools.partial(attend_kernel, kc), grid=(nq,), out_shap...  94.5 us
    ppermute x52, waiting for transfers between devices, swap(): return lax.ppermute(array, axis, [(i, i ^ j) for i in range(size)])  66.5 us
    ppermute x52, starting transfers between devices, swap(): return lax.ppermute(array, axis, [(i, i ^ j) for i in range(size)])  48.2 us
    all_to_all x5, starting transfers between devices, to_owner(): lax.all_to_all(parts, 'fsdp', split_axis=0, concat_axis=0, tiled=True)  28.2 us
    pallas_call x1, Pallas kernels, middle(): pl.pallas_call(functools.partial(middle_kernel, groups, heads, ff), grid=...  28.1 us
    pallas_call x4, Pallas kernels, qkv_call(): pl.pallas_call(functools.partial(qkv_kernel, heads, len(parts)), grid=(st...  25.5 us
    unnamed x98, local copies, waits for them, and re-layouts  23.6 us
  transfers between devices with their start and end apart: 60, of which 16 were waited for; matrix products, arithmetic and copies ran while one was open for 20% of the time, Pallas kernels for 47%

profile of v2, /device:TPU:1, one launch (start us, length us, event | category | flops | bytes accessed | tf_op | source)
XLA Modules:
  0.0 581.0 jit_solution(16410981374112408937)
XLA Ops:
  9.7 5.1 collective-permute-start
  18.9 2.3 collective-permute-start.4
  28.7 2.8 maximum_bitcast_fusion.1
  33.9 2.7 maximum_bitcast_fusion
  36.8 2.7 collective-permute-start.6
  40.7 2.4 collective-permute-start.8
  43.2 3.1 copy.82.sin_ref
  46.4 2.9 copy.81.cos_ref
  49.4 2.3 collective-permute-done.6.refs_4_
  51.7 3.1 collective-permute-done.7.refs_5_
  54.9 6.1 %qkv.4 = (bf16[4096,768]{1,0:T(8,128)(2,1)}, bf16[3,4096,128]{2,1,0:T(8,128)(2,1)}, bf16[3,4096,128]{2,1,0:T(8,128)(2,1)}, bf16[3,128,4096]{2,1,0:T(8,128)(2,1)}...) custom-call(s32[3]{0:T(128)S(1)} %add_add_fusion.3.info_ref, bf16[1024,768]{1,0:T(8,128)(2,1)S(1)} %bitcast.208, ...), custom_call_target="tpu_custom_call" | custom-call | flops 2013265920 | bytes 8388608 | tf_op jit(solution)/shard_map/qkv/pallas_call | solution.py:111
  61.0 6.5 %qkv.5 = (bf16[4096,768]{1,0:T(8,128)(2,1)}, bf16[3,4096,128]{2,1,0:T(8,128)(2,1)}, bf16[3,4096,128]{2,1,0:T(8,128)(2,1)}, bf16[3,128,4096]{2,1,0:T(8,128)(2,1)}...) custom-call(s32[3]{0:T(128)S(1)} %add_add_fusion.2.info_ref, ...), custom_call_target="tpu_custom_call", output_to_operand_aliasing={{0}: (12, {}), {1}: (13, {}), {2}: (14, {}), {3}: (15, {}),... | custom-call | flops 2013265920 | bytes 8388608 | tf_op jit(solution)/shard_map/qkv/pallas_call | solution.py:111
  67.5 6.5 %qkv.6 = (bf16[4096,768]{1,0:T(8,128)(2,1)}, bf16[3,4096,128]{2,1,0:T(8,128)(2,1)}, bf16[3,4096,128]{2,1,0:T(8,128)(2,1)}, bf16[3,128,4096]{2,1,0:T(8,128)(2,1)}...) custom-call(s32[3]{0:T(128)S(1)} %add_add_fusion.1.info_ref, ...), custom_call_target="tpu_custom_call", output_to_operand_aliasing={{0}: (12, {}), {1}: (13, {}), {2}: (14, {}), {3}: (15, {}),... | custom-call | flops 2013265920 | bytes 8388608 | tf_op jit(solution)/shard_map/qkv/pallas_call | solution.py:111
  73.9 18.9 %collective-permute-done.2.x_ref = bf16[1024,768]{1,0:T(8,128)(2,1)} collective-permute-done((bf16[1024,768]{1,0:T(8,128)(2,1)}, bf16[1024,768]{1,0:T(8,128)(2,1)}, u32[]{:S(2)}, u32[]{:S(2)}) %collective-permute-start.2) | collective-permute-done | bytes 1572896 | tf_op jit(solution)/shard_map/ppermute | solution.py:443
  92.9 6.5 %qkv.7 = (bf16[4096,768]{1,0:T(8,128)(2,1)}, bf16[3,4096,128]{2,1,0:T(8,128)(2,1)}, bf16[3,4096,128]{2,1,0:T(8,128)(2,1)}, bf16[3,128,4096]{2,1,0:T(8,128)(2,1)}...) custom-call(s32[3]{0:T(128)S(1)} %add_add_fusion.info_ref, ...), custom_call_target="tpu_custom_call", output_to_operand_aliasing={{0}: (12, {}), {1}: (13, {}), {2}: (14, {}), {3}: (15, {}),... | custom-call | flops 2013265920 | bytes 8388608 | tf_op jit(solution)/shard_map/qkv/pallas_call | solution.py:111
  99.3 31.7 %attend.5 = (bf16[8,4096,512]{2,1,0:T(8,128)(2,1)}, f32[64,4096]{1,0:T(8,128)S(1)}, bf16[4,64,1024]{2,1,0:T(8,128)(2,1)S(1)}, f32[8,1,512]{2,1,0:T(1,128)S(1)}) custom-call(bf16[3,4096,128]{2,1,0:T(8,128)(2,1)} %get-tuple-element.76.k_ref, bf16[3,128,4096]{2,1,0:T(8,128)(2,1)} %get-tuple-element.77.q_ref, bf16[3,80,4096]{2,1,0:T(8,128)(2,1)S(1)} %get-tuple-element.78.v_ref), custom_call_target="tpu_custom_call" | custom-call | flops 17179869184 | bytes 33554432 | tf_op jit(solution)/shard_map/attend/pallas_call | solution.py:162
  134.0 31.2 %attend.4 = (bf16[8,4096,512]{2,1,0:T(8,128)(2,1)}, f32[64,4096]{1,0:T(8,128)S(1)}, bf16[4,64,1024]{2,1,0:T(8,128)(2,1)S(1)}, f32[8,1,512]{2,1,0:T(1,128)S(1)}) custom-call(bf16[3,4096,128]{2,1,0:T(8,128)(2,1)} %get-tuple-element.76.k_ref, bf16[3,128,4096]{2,1,0:T(8,128)(2,1)} %get-tuple-element.77.q_ref, bf16[3,80,4096]{2,1,0:T(8,128)(2,1)S(1)} %get-tuple-element.78.v_ref), custom_call_target="tpu_custom_call" | custom-call | flops 17179869184 | bytes 33554432 | tf_op jit(solution)/shard_map/attend/pallas_call | solution.py:162
  167.8 31.6 %attend.3 = (bf16[8,4096,512]{2,1,0:T(8,128)(2,1)}, f32[64,4096]{1,0:T(8,128)S(1)}, bf16[4,64,1024]{2,1,0:T(8,128)(2,1)S(1)}, f32[8,1,512]{2,1,0:T(1,128)S(1)}) custom-call(bf16[3,4096,128]{2,1,0:T(8,128)(2,1)} %get-tuple-element.76.k_ref, bf16[3,128,4096]{2,1,0:T(8,128)(2,1)} %get-tuple-element.77.q_ref, bf16[3,80,4096]{2,1,0:T(8,128)(2,1)S(1)} %get-tuple-element.78.v_ref), custom_call_target="tpu_custom_call" | custom-call | flops 17179869184 | bytes 33554432 | tf_op jit(solution)/shard_map/attend/pallas_call | solution.py:162
  205.9 2.6 collective-permute-done.11.refs_2_
  208.5 2.8 collective-permute-done.12.refs_3_
  211.3 28.1 %middle.1 = (bf16[1024,768]{1,0:T(8,128)(2,1)}, f32[1024,768]{1,0:T(8,128)}, bf16[3,4,64,1024]{3,2,1,0:T(8,128)(2,1)S(1)}, bf16[768,1024]{1,0:T(8,128)(2,1)S(1)}...) custom-call(s32[1]{0:T(128)} %bitcast.info_ref, ...), custom_call_target="tpu_custom_call" | custom-call | flops 15099494400 | bytes 31457280 | tf_op jit(solution)/shard_map/middle/pallas_call | solution.py:344
  239.4 4.1 convolution_convert_fusion.1
  245.6 4.3 convolution_convert_fusion
  251.2 2.8 pad_maximum_fusion
  254.0 9.8 %convert_element_type.110 = bf16[768,4,768]{2,1,0:T(4,128)(2,1)} reshape(bf16[768,3072]{1,0:T(8,128)(2,1)} %pad_maximum_fusion) | data formatting | bytes 9437184 | tf_op jit(solution)/shard_map/convert_element_type | solution.py:521
  266.8 16.6 %constant_dynamic-slice_fusion.4 = (bf16[768,1,768]{2,1,0:T(2,128)(2,1)}, bf16[768,1,768]{2,1,0:T(2,128)(2,1)}, bf16[768,1,768]{2,1,0:T(2,128)(2,1)}, bf16[768,1,768]{2,1,0:T(2,128)(2,1)}) fusion(bf16[768,4,768]{2,1,0:T(4,128)(2,1)} %convert_element_type.110, s32[]{:T(128)S(6)} %select_n.35, s32[]{:T(128)S(6)} %select_n.37, s32[]{:T(128)S(6)} %select_n.36, ...), kind=kLoop, calls=%fused_computation.108 | loop fusion | bytes 9437200 | tf_op jit(solution)/shard_map/jit(dynamic_index_in_dim)/dynamic_slice | solution.py:449
  284.5 3.0 copy.112
  293.0 38.6 %attend_back.3 = bf16[4,192,1024]{2,1,0:T(8,128)(2,1)S(1)} custom-call(bf16[3,4096,128]{2,1,0:T(8,128)(2,1)} %get-tuple-element.86.v_ref, bf16[3,64,4096]{2,1,0:T(8,128)(2,1)} %copy-done, bf16[3,128,4096]{2,1,0:T(8,128)(2,1)} %get-tuple-element.77.q_ref, f32[64,4096]{1,0:T(8,128)S(1)} %copy-done.19, f32[8,1,512]{2,1,0:T(1,128)S(1)} %copy-done.23, ...), custom_call_target="tpu_custom_call" | custom-call | flops 25769803776 | bytes 33554432 | tf_op jit(solution)/shard_map/attend_back/pallas_call | solution.py:246
  331.6 4.2 fusion.3
  337.0 5.6 all-to-all-start
  352.4 38.7 %attend_back.4 = bf16[4,192,1024]{2,1,0:T(8,128)(2,1)S(1)} custom-call(bf16[3,4096,128]{2,1,0:T(8,128)(2,1)} %get-tuple-element.86.v_ref, bf16[3,64,4096]{2,1,0:T(8,128)(2,1)} %copy-done, bf16[3,128,4096]{2,1,0:T(8,128)(2,1)} %get-tuple-element.77.q_ref, f32[64,4096]{1,0:T(8,128)S(1)} %copy-done.17, f32[8,1,512]{2,1,0:T(1,128)S(1)} %copy-done.21, ...), custom_call_target="tpu_custom_call" | custom-call | flops 25769803776 | bytes 33554432 | tf_op jit(solution)/shard_map/attend_back/pallas_call | solution.py:246
  393.1 38.6 %attend_back.5 = bf16[4,192,1024]{2,1,0:T(8,128)(2,1)S(1)} custom-call(bf16[3,4096,128]{2,1,0:T(8,128)(2,1)} %get-tuple-element.86.v_ref, bf16[3,64,4096]{2,1,0:T(8,128)(2,1)} %copy-done, bf16[3,128,4096]{2,1,0:T(8,128)(2,1)} %get-tuple-element.77.q_ref, f32[64,4096]{1,0:T(8,128)S(1)} %copy-done.15, f32[8,1,512]{2,1,0:T(1,128)S(1)} %get-tuple-element.96.linv_ref, ...), custom_call_target="tpu_custom_call" | custom-call | flops 25769803776 | bytes 33554432 | tf_op jit(solution)/shard_map/attend_back/pallas_call | solution.py:246
  432.9 4.9 fusion.4
  441.3 5.8 %all-to-all-start.1 = ((bf16[8,96,192]{1,2,0:T(8,128)(2,1)}), bf16[8,96,192]{1,2,0:T(8,128)(2,1)S(1)}, u32[]{:S(2)}, u32[]{:S(2)}) async-start(bf16[8,96,192]{1,2,0:T(8,128)(2,1)} %copy.85), calls=%async_computation.1 | async-start | bytes 786432 | tf_op jit(solution)/shard_map/all_to_all | solution.py:530
  447.1 5.4 fusion.5
  462.7 5.4 all-to-all-start.2
  468.2 2.7 fusion.8
  470.9 6.6 %all-to-all-done.2 = bf16[8,96,192]{1,2,0:T(8,128)(2,1)} async-done(((bf16[8,96,192]{1,2,0:T(8,128)(2,1)}), bf16[8,96,192]{1,2,0:T(8,128)(2,1)}, u32[]{:S(2)}, u32[]{:S(2)}) %all-to-all-start.2) | async-done | bytes 294944 | tf_op jit(solution)/shard_map/all_to_all | solution.py:530
  477.5 6.1 %all-to-all-start.4 = ((bf16[8,144,192]{2,1,0:T(8,128)(2,1)}), bf16[8,144,192]{2,1,0:T(8,128)(2,1)}, u32[]{:S(2)}, u32[]{:S(2)}) async-start(bf16[8,144,192]{2,1,0:T(8,128)(2,1)} %bitcast.217), calls=%async_computation.4 | async-start | bytes 1179648 | tf_op jit(solution)/shard_map/all_to_all | solution.py:530
  483.6 2.4 slice_bitcast_fusion
  491.0 3.5 fusion.2
  494.5 3.6 all-to-all-done.4
  498.1 5.2 all-to-all-start.3
  516.7 8.0 %collective-permute-done.30.refs_7_ = bf16[192,1024]{1,0:T(8,128)(2,1)S(1)} collective-permute-done((bf16[192,1024]{1,0:T(8,128)(2,1)}, bf16[192,1024]{1,0:T(8,128)(2,1)S(1)}, u32[]{:S(2)}, u32[]{:S(2)}) %collective-permute-start.30) | collective-permute-done | bytes 393248 | tf_op jit(solution)/shard_map/ppermute | solution.py:443
  525.8 6.5 %collective-permute-done.23.refs_2_ = bf16[192,1024]{1,0:T(8,128)(2,1)S(1)} collective-permute-done((bf16[192,1024]{1,0:T(8,128)(2,1)}, bf16[192,1024]{1,0:T(8,128)(2,1)S(1)}, u32[]{:S(2)}, u32[]{:S(2)}) %collective-permute-start.23) | collective-permute-done | bytes 393248 | tf_op jit(solution)/shard_map/ppermute | solution.py:443
  532.3 8.9 %collective-permute-done.24.refs_3_ = bf16[192,1024]{1,0:T(8,128)(2,1)S(1)} collective-permute-done((bf16[192,1024]{1,0:T(8,128)(2,1)}, bf16[192,1024]{1,0:T(8,128)(2,1)S(1)}, u32[]{:S(2)}, u32[]{:S(2)}) %collective-permute-start.24) | collective-permute-done | bytes 393248 | tf_op jit(solution)/shard_map/ppermute | solution.py:443
  541.2 10.0 %last.1 = f32[1024,768]{1,0:T(8,128)} custom-call(s32[1]{0:T(128)} %bitcast.info_ref, bf16[1024,768]{1,0:T(8,128)(2,1)} %bitcast.205, f32[1024,768]{1,0:T(8,128)} %get-tuple-element.83.dh_ref, bf16[768,2432]{1,0:T(8,128)(2,1)} %all-gather.8.cloned.1.call-done.w_ref, bf16[192,1024]{1,0:T(8,128)(2,1)S(1)} %get-tuple-element.153.refs_0_, ...), custom_call_target="tpu_custom_call" | custom-call | flops 3623878656 | bytes 16777216 | tf_op jit(solution)/shard_map/last/pallas_call | solution.py:409
  567.7 3.7 collective-permute-done.45
  (260 shorter events, 108.4 us)
Async XLA Ops:
  7.2 196.6 %all-gather.6.cloned.1.call-start = ((), (), s32[]{:S(2)}) async-start(), calls=%async_computation.6 | async-start | bytes 1990656 | tf_op jit(solution)/shard_map/all_gather | solution.py:452
  18.0 193.3 %all-gather.4.cloned.1.call-start = ((), (), s32[]{:S(2)}) async-start(), calls=%async_computation.5 | async-start | bytes 5529600 | tf_op jit(solution)/shard_map/all_gather | solution.py:452
  18.0 18.8 %collective-permute-start.3 = (bf16[96,640]{1,0:T(8,128)(2,1)S(1)}, bf16[96,640]{1,0:T(8,128)(2,1)S(1)}, u32[]{:S(2)}, u32[]{:S(2)}) collective-permute-start(bf16[96,640]{1,0:T(8,128)(2,1)S(1)} %concatenate.44.refs_0_), channel_id=1, source_target_pairs={{0,1},{1,0},{2,3},{3,2},{4,5},{5,4},{6,7},{7,6},{8,9},{9,8},{10,11... | collective-permute-start | bytes 368648 | tf_op jit(solution)/shard_map/ppermute | solution.py:443
  18.9 20.6 %collective-permute-start.4 = (bf16[96,640]{1,0:T(8,128)(2,1)S(1)}, bf16[96,640]{1,0:T(8,128)(2,1)S(1)}, u32[]{:S(2)}, u32[]{:S(2)}) collective-permute-start(bf16[96,640]{1,0:T(8,128)(2,1)S(1)} %concatenate.44.refs_0_), channel_id=1, source_target_pairs={{0,2},{1,3},{2,0},{3,1},{4,6},{5,7},{6,4},{7,5},{8,10},{9,11},{10,... | collective-permute-start | bytes 368648 | tf_op jit(solution)/shard_map/ppermute | solution.py:443
  21.2 19.5 %collective-permute-start.5 = (bf16[96,640]{1,0:T(8,128)(2,1)S(1)}, bf16[96,640]{1,0:T(8,128)(2,1)S(1)}, u32[]{:S(2)}, u32[]{:S(2)}) collective-permute-start(bf16[96,640]{1,0:T(8,128)(2,1)S(1)} %concatenate.44.refs_0_), channel_id=1, source_target_pairs={{0,3},{1,2},{2,1},{3,0},{4,7},{5,6},{6,5},{7,4},{8,11},{9,10},{10,... | collective-permute-start | bytes 368648 | tf_op jit(solution)/shard_map/ppermute | solution.py:443
  23.1 44.3 %collective-permute-start.9 = (bf16[1024,768]{1,0:T(8,128)(2,1)S(1)}, bf16[1024,768]{1,0:T(8,128)(2,1)}, u32[]{:S(2)}, u32[]{:S(2)}) collective-permute-start(bf16[1024,768]{1,0:T(8,128)(2,1)S(1)} %bitcast.207), channel_id=1, source_target_pairs={{0,16},{8,24},{16,0},{24,8},{1,17},{9,25},{17,1},{25,9},{2,18},{10... | collective-permute-start | bytes 4718600 | tf_op jit(solution)/shard_map/ppermute | solution.py:443
  28.6 497.1 %all-gather.8.cloned.1.call-start = ((), (), s32[]{:S(2)}) async-start(), calls=%async_computation.7 | async-start | bytes 4202496 | tf_op jit(solution)/shard_map/all_gather | solution.py:452
  31.5 61.3 %collective-permute-start.2 = (bf16[1024,768]{1,0:T(8,128)(2,1)}, bf16[1024,768]{1,0:T(8,128)(2,1)}, u32[]{:S(2)}, u32[]{:S(2)}) collective-permute-start(bf16[1024,768]{1,0:T(8,128)(2,1)} %collective-permute-done.1.x_ref), channel_id=1, source_target_pairs={{0,16},{8,24},{16,0},{24,8},{1,17},{9,25},{17,1},{25,9},{2,18},{10... | collective-permute-start | bytes 4718600 | tf_op jit(solution)/shard_map/ppermute | solution.py:443
  36.8 14.9 %collective-permute-start.6 = (bf16[96,640]{1,0:T(8,128)(2,1)S(1)}, bf16[96,640]{1,0:T(8,128)(2,1)S(1)}, u32[]{:S(2)}, u32[]{:S(2)}) collective-permute-start(bf16[96,640]{1,0:T(8,128)(2,1)S(1)} %concatenate.44.refs_0_), channel_id=1, source_target_pairs={{0,4},{1,5},{2,6},{3,7},{4,0},{5,1},{6,2},{7,3},{8,12},{9,13},{10,... | collective-permute-start | bytes 368648 | tf_op jit(solution)/shard_map/ppermute | solution.py:443
  39.6 15.3 %collective-permute-start.7 = (bf16[96,640]{1,0:T(8,128)(2,1)S(1)}, bf16[96,640]{1,0:T(8,128)(2,1)S(1)}, u32[]{:S(2)}, u32[]{:S(2)}) collective-permute-start(bf16[96,640]{1,0:T(8,128)(2,1)S(1)} %concatenate.44.refs_0_), channel_id=1, source_target_pairs={{0,5},{1,4},{2,7},{3,6},{4,1},{5,0},{6,3},{7,2},{8,13},{9,12},{10,... | collective-permute-start | bytes 368648 | tf_op jit(solution)/shard_map/ppermute | solution.py:443
  40.7 14.1 %collective-permute-start.8 = (bf16[96,640]{1,0:T(8,128)(2,1)S(1)}, bf16[96,640]{1,0:T(8,128)(2,1)S(1)}, u32[]{:S(2)}, u32[]{:S(2)}) collective-permute-start(bf16[96,640]{1,0:T(8,128)(2,1)S(1)} %concatenate.44.refs_0_), channel_id=1, source_target_pairs={{0,6},{1,7},{2,4},{3,5},{4,2},{5,3},{6,0},{7,1},{8,14},{9,15},{10,... | collective-permute-start | bytes 368648 | tf_op jit(solution)/shard_map/ppermute | solution.py:443
  131.1 69.0 %collective-permute-start.16 = (bf16[64,1024]{1,0:T(8,128)(2,1)S(1)}, bf16[64,1024]{1,0:T(8,128)(2,1)S(1)}, u32[]{:S(2)}, u32[]{:S(2)}) collective-permute-start(bf16[64,1024]{1,0:T(8,128)(2,1)S(1)} %get-tuple-element.168), channel_id=1, source_target_pairs={{0,8},{8,0},{16,24},{24,16},{1,9},{9,1},{17,25},{25,17},{2,10},{10... | collective-permute-start | bytes 393224 | tf_op jit(solution)/shard_map/ppermute | solution.py:443
  132.0 68.7 %collective-permute-start.17 = (bf16[64,1024]{1,0:T(8,128)(2,1)S(1)}, bf16[64,1024]{1,0:T(8,128)(2,1)S(1)}, u32[]{:S(2)}, u32[]{:S(2)}) collective-permute-start(bf16[64,1024]{1,0:T(8,128)(2,1)S(1)} %get-tuple-element.167), channel_id=1, source_target_pairs={{0,16},{8,24},{16,0},{24,8},{1,17},{9,25},{17,1},{25,9},{2,18},{10... | collective-permute-start | bytes 393224 | tf_op jit(solution)/shard_map/ppermute | solution.py:443
  133.2 67.8 %collective-permute-start.18 = (bf16[64,1024]{1,0:T(8,128)(2,1)S(1)}, bf16[64,1024]{1,0:T(8,128)(2,1)S(1)}, u32[]{:S(2)}, u32[]{:S(2)}) collective-permute-start(bf16[64,1024]{1,0:T(8,128)(2,1)S(1)} %get-tuple-element.166), channel_id=1, source_target_pairs={{0,24},{8,16},{16,8},{24,0},{1,25},{9,17},{17,9},{25,1},{2,26},{10... | collective-permute-start | bytes 393224 | tf_op jit(solution)/shard_map/ppermute | solution.py:443
  165.8 36.2 %collective-permute-start.13 = (bf16[64,1024]{1,0:T(8,128)(2,1)S(1)}, bf16[64,1024]{1,0:T(8,128)(2,1)S(1)}, u32[]{:S(2)}, u32[]{:S(2)}) collective-permute-start(bf16[64,1024]{1,0:T(8,128)(2,1)S(1)} %get-tuple-element.172), channel_id=1, source_target_pairs={{0,8},{8,0},{16,24},{24,16},{1,9},{9,1},{17,25},{25,17},{2,10},{10... | collective-permute-start | bytes 393224 | tf_op jit(solution)/shard_map/ppermute | solution.py:443
  166.8 37.0 %collective-permute-start.14 = (bf16[64,1024]{1,0:T(8,128)(2,1)S(1)}, bf16[64,1024]{1,0:T(8,128)(2,1)S(1)}, u32[]{:S(2)}, u32[]{:S(2)}) collective-permute-start(bf16[64,1024]{1,0:T(8,128)(2,1)S(1)} %get-tuple-element.171), channel_id=1, source_target_pairs={{0,16},{8,24},{16,0},{24,8},{1,17},{9,25},{17,1},{25,9},{2,18},{10... | collective-permute-start | bytes 393224 | tf_op jit(solution)/shard_map/ppermute | solution.py:443
  244.7 195.3 %collective-permute-start.46 = (bf16[1152,192]{0,1:T(8,128)(2,1)}, bf16[1152,192]{0,1:T(8,128)(2,1)}, u32[]{:S(2)}, u32[]{:S(2)}) collective-permute-start(bf16[1152,192]{0,1:T(8,128)(2,1)} %get-tuple-element.129), channel_id=1, source_target_pairs={{0,8},{8,0},{16,24},{24,16},{1,9},{9,1},{17,25},{25,17},{2,10},{10... | collective-permute-start | bytes 1327112 | tf_op jit(solution)/shard_map/ppermute | solution.py:443
  245.1 213.5 %collective-permute-start.47 = (bf16[1152,192]{0,1:T(8,128)(2,1)}, bf16[1152,192]{0,1:T(8,128)(2,1)}, u32[]{:S(2)}, u32[]{:S(2)}) collective-permute-start(bf16[1152,192]{0,1:T(8,128)(2,1)} %get-tuple-element.128), channel_id=1, source_target_pairs={{0,16},{8,24},{16,0},{24,8},{1,17},{9,25},{17,1},{25,9},{2,18},{10... | collective-permute-start | bytes 1327112 | tf_op jit(solution)/shard_map/ppermute | solution.py:443
  264.7 26.2 %collective-permute-start.19 = (bf16[64,1024]{1,0:T(8,128)(2,1)S(1)}, bf16[64,1024]{1,0:T(8,128)(2,1)S(1)}, u32[]{:S(2)}, u32[]{:S(2)}) collective-permute-start(bf16[64,1024]{1,0:T(8,128)(2,1)S(1)} %get-tuple-element.144), channel_id=1, source_target_pairs={{0,8},{8,0},{16,24},{24,16},{1,9},{9,1},{17,25},{25,17},{2,10},{10... | collective-permute-start | bytes 393224 | tf_op jit(solution)/shard_map/ppermute | solution.py:443
  265.0 25.9 %collective-permute-start.20 = (bf16[64,1024]{1,0:T(8,128)(2,1)S(1)}, bf16[64,1024]{1,0:T(8,128)(2,1)S(1)}, u32[]{:S(2)}, u32[]{:S(2)}) collective-permute-start(bf16[64,1024]{1,0:T(8,128)(2,1)S(1)} %get-tuple-element.143), channel_id=1, source_target_pairs={{0,16},{8,24},{16,0},{24,8},{1,17},{9,25},{17,1},{25,9},{2,18},{10... | collective-permute-start | bytes 393224 | tf_op jit(solution)/shard_map/ppermute | solution.py:443
  266.1 25.9 %collective-permute-start.21 = (bf16[64,1024]{1,0:T(8,128)(2,1)S(1)}, bf16[64,1024]{1,0:T(8,128)(2,1)S(1)}, u32[]{:S(2)}, u32[]{:S(2)}) collective-permute-start(bf16[64,1024]{1,0:T(8,128)(2,1)S(1)} %get-tuple-element.142), channel_id=1, source_target_pairs={{0,24},{8,16},{16,8},{24,0},{1,25},{9,17},{17,9},{25,1},{2,26},{10... | collective-permute-start | bytes 393224 | tf_op jit(solution)/shard_map/ppermute | solution.py:443
  290.8 51.8 %collective-permute-start.25 = (bf16[64,1024]{1,0:T(8,128)(2,1)}, bf16[64,1024]{1,0:T(8,128)(2,1)S(1)}, u32[]{:S(2)}, u32[]{:S(2)}) collective-permute-start(bf16[64,1024]{1,0:T(8,128)(2,1)} %get-tuple-element.140), channel_id=1, source_target_pairs={{0,8},{8,0},{16,24},{24,16},{1,9},{9,1},{17,25},{25,17},{2,10},{10... | collective-permute-start | bytes 393224 | tf_op jit(solution)/shard_map/ppermute | solution.py:443
  290.9 51.9 %collective-permute-start.26 = (bf16[64,1024]{1,0:T(8,128)(2,1)S(1)}, bf16[64,1024]{1,0:T(8,128)(2,1)S(1)}, u32[]{:S(2)}, u32[]{:S(2)}) collective-permute-start(bf16[64,1024]{1,0:T(8,128)(2,1)S(1)} %get-tuple-element.139), channel_id=1, source_target_pairs={{0,16},{8,24},{16,0},{24,8},{1,17},{9,25},{17,1},{25,9},{2,18},{10... | collective-permute-start | bytes 393224 | tf_op jit(solution)/shard_map/ppermute | solution.py:443
  292.0 52.5 %collective-permute-start.27 = (bf16[64,1024]{1,0:T(8,128)(2,1)S(1)}, bf16[64,1024]{1,0:T(8,128)(2,1)S(1)}, u32[]{:S(2)}, u32[]{:S(2)}) collective-permute-start(bf16[64,1024]{1,0:T(8,128)(2,1)S(1)} %get-tuple-element.138), channel_id=1, source_target_pairs={{0,24},{8,16},{16,8},{24,0},{1,25},{9,17},{17,9},{25,1},{2,26},{10... | collective-permute-start | bytes 393224 | tf_op jit(solution)/shard_map/ppermute | solution.py:443
  337.0 104.3 %all-to-all-start = ((bf16[8,96,192]{1,2,0:T(8,128)(2,1)}), bf16[8,96,192]{1,2,0:T(8,128)(2,1)}, u32[]{:S(2)}, u32[]{:S(2)}) async-start(bf16[8,96,192]{1,2,0:T(8,128)(2,1)} %copy.84), calls=%async_computation | async-start | bytes 786432 | tf_op jit(solution)/shard_map/all_to_all | solution.py:530
  342.6 48.5 %collective-permute-start.31 = (bf16[64,1024]{1,0:T(8,128)(2,1)}, bf16[64,1024]{1,0:T(8,128)(2,1)S(1)}, u32[]{:S(2)}, u32[]{:S(2)}) collective-permute-start(bf16[64,1024]{1,0:T(8,128)(2,1)} %get-tuple-element.136), channel_id=1, source_target_pairs={{0,8},{8,0},{16,24},{24,16},{1,9},{9,1},{17,25},{25,17},{2,10},{10... | collective-permute-start | bytes 393224 | tf_op jit(solution)/shard_map/ppermute | solution.py:443
  343.5 48.5 %collective-permute-start.32 = (bf16[64,1024]{1,0:T(8,128)(2,1)}, bf16[64,1024]{1,0:T(8,128)(2,1)S(1)}, u32[]{:S(2)}, u32[]{:S(2)}) collective-permute-start(bf16[64,1024]{1,0:T(8,128)(2,1)} %get-tuple-element.135), channel_id=1, source_target_pairs={{0,16},{8,24},{16,0},{24,8},{1,17},{9,25},{17,1},{25,9},{2,18},{10... | collective-permute-start | bytes 393224 | tf_op jit(solution)/shard_map/ppermute | solution.py:443
  345.2 47.4 %collective-permute-start.33 = (bf16[64,1024]{1,0:T(8,128)(2,1)}, bf16[64,1024]{1,0:T(8,128)(2,1)S(1)}, u32[]{:S(2)}, u32[]{:S(2)}) collective-permute-start(bf16[64,1024]{1,0:T(8,128)(2,1)} %get-tuple-element.134), channel_id=1, source_target_pairs={{0,24},{8,16},{16,8},{24,0},{1,25},{9,17},{17,9},{25,1},{2,26},{10... | collective-permute-start | bytes 393224 | tf_op jit(solution)/shard_map/ppermute | solution.py:443
  391.1 69.5 %collective-permute-start.48 = (bf16[1152,192]{0,1:T(8,128)(2,1)}, bf16[1152,192]{0,1:T(8,128)(2,1)}, u32[]{:S(2)}, u32[]{:S(2)}) collective-permute-start(bf16[1152,192]{0,1:T(8,128)(2,1)} %get-tuple-element.127), channel_id=1, source_target_pairs={{0,24},{8,16},{16,8},{24,0},{1,25},{9,17},{17,9},{25,1},{2,26},{10... | collective-permute-start | bytes 1327112 | tf_op jit(solution)/shard_map/ppermute | solution.py:443
  392.0 97.1 %collective-permute-start.40 = (bf16[768,768]{1,0:T(8,128)(2,1)}, bf16[768,768]{1,0:T(8,128)(2,1)}, u32[]{:S(2)}, u32[]{:S(2)}) collective-permute-start(bf16[768,768]{1,0:T(8,128)(2,1)} %bitcast.203), channel_id=1, source_target_pairs={{0,8},{8,0},{16,24},{24,16},{1,9},{9,1},{17,25},{25,17},{2,10},{10... | collective-permute-start | bytes 3538952 | tf_op jit(solution)/shard_map/ppermute | solution.py:443
  392.6 97.8 %collective-permute-start.41 = (bf16[768,768]{1,0:T(8,128)(2,1)}, bf16[768,768]{1,0:T(8,128)(2,1)}, u32[]{:S(2)}, u32[]{:S(2)}) collective-permute-start(bf16[768,768]{1,0:T(8,128)(2,1)} %bitcast.202), channel_id=1, source_target_pairs={{0,16},{8,24},{16,0},{24,8},{1,17},{9,25},{17,1},{25,9},{2,18},{10... | collective-permute-start | bytes 3538952 | tf_op jit(solution)/shard_map/ppermute | solution.py:443
  440.0 50.6 %collective-permute-start.42 = (bf16[768,768]{1,0:T(8,128)(2,1)}, bf16[768,768]{1,0:T(8,128)(2,1)}, u32[]{:S(2)}, u32[]{:S(2)}) collective-permute-start(bf16[768,768]{1,0:T(8,128)(2,1)} %bitcast.219), channel_id=1, source_target_pairs={{0,24},{8,16},{16,8},{24,0},{1,25},{9,17},{17,9},{25,1},{2,26},{10... | collective-permute-start | bytes 3538952 | tf_op jit(solution)/shard_map/ppermute | solution.py:443
  441.3 21.4 %all-to-all-start.1 = ((bf16[8,96,192]{1,2,0:T(8,128)(2,1)}), bf16[8,96,192]{1,2,0:T(8,128)(2,1)S(1)}, u32[]{:S(2)}, u32[]{:S(2)}) async-start(bf16[8,96,192]{1,2,0:T(8,128)(2,1)} %copy.85), calls=%async_computation.1 | async-start | bytes 786432 | tf_op jit(solution)/shard_map/all_to_all | solution.py:530
  462.7 14.7 %all-to-all-start.2 = ((bf16[8,96,192]{1,2,0:T(8,128)(2,1)}), bf16[8,96,192]{1,2,0:T(8,128)(2,1)}, u32[]{:S(2)}, u32[]{:S(2)}) async-start(bf16[8,96,192]{1,2,0:T(8,128)(2,1)} %copy.86), calls=%async_computation.2 | async-start | bytes 786432 | tf_op jit(solution)/shard_map/all_to_all | solution.py:530
  477.5 20.6 %all-to-all-start.4 = ((bf16[8,144,192]{2,1,0:T(8,128)(2,1)}), bf16[8,144,192]{2,1,0:T(8,128)(2,1)}, u32[]{:S(2)}, u32[]{:S(2)}) async-start(bf16[8,144,192]{2,1,0:T(8,128)(2,1)} %bitcast.217), calls=%async_computation.4 | async-start | bytes 1179648 | tf_op jit(solution)/shard_map/all_to_all | solution.py:530
  486.0 18.3 %collective-permute-start.34 = (bf16[192,1024]{1,0:T(8,128)(2,1)}, bf16[192,1024]{1,0:T(8,128)(2,1)}, u32[]{:S(2)}, u32[]{:S(2)}) collective-permute-start(bf16[192,1024]{1,0:T(8,128)(2,1)} %get-tuple-element.132), channel_id=1, source_target_pairs={{0,8},{8,0},{16,24},{24,16},{1,9},{9,1},{17,25},{25,17},{2,10},{10... | collective-permute-start | bytes 1179656 | tf_op jit(solution)/shard_map/ppermute | solution.py:443
  487.6 18.4 %collective-permute-start.35 = (bf16[192,1024]{1,0:T(8,128)(2,1)}, bf16[192,1024]{1,0:T(8,128)(2,1)}, u32[]{:S(2)}, u32[]{:S(2)}) collective-permute-start(bf16[192,1024]{1,0:T(8,128)(2,1)} %get-tuple-element.131), channel_id=1, source_target_pairs={{0,16},{8,24},{16,0},{24,8},{1,17},{9,25},{17,1},{25,9},{2,18},{10... | collective-permute-start | bytes 1179656 | tf_op jit(solution)/shard_map/ppermute | solution.py:443
  489.1 18.4 %collective-permute-start.36 = (bf16[192,1024]{1,0:T(8,128)(2,1)}, bf16[192,1024]{1,0:T(8,128)(2,1)S(1)}, u32[]{:S(2)}, u32[]{:S(2)}) collective-permute-start(bf16[192,1024]{1,0:T(8,128)(2,1)} %get-tuple-element.130), channel_id=1, source_target_pairs={{0,24},{8,16},{16,8},{24,0},{1,25},{9,17},{17,9},{25,1},{2,26},{10... | collective-permute-start | bytes 1179656 | tf_op jit(solution)/shard_map/ppermute | solution.py:443
  490.4 17.4 %collective-permute-start.28 = (bf16[192,1024]{1,0:T(8,128)(2,1)}, bf16[192,1024]{1,0:T(8,128)(2,1)S(1)}, u32[]{:S(2)}, u32[]{:S(2)}) collective-permute-start(bf16[192,1024]{1,0:T(8,128)(2,1)} %get-tuple-element.148), channel_id=1, source_target_pairs={{0,8},{8,0},{16,24},{24,16},{1,9},{9,1},{17,25},{25,17},{2,10},{10... | collective-permute-start | bytes 1179656 | tf_op jit(solution)/shard_map/ppermute | solution.py:443
  490.6 25.1 %collective-permute-start.29 = (bf16[192,1024]{1,0:T(8,128)(2,1)}, bf16[192,1024]{1,0:T(8,128)(2,1)}, u32[]{:S(2)}, u32[]{:S(2)}) collective-permute-start(bf16[192,1024]{1,0:T(8,128)(2,1)} %get-tuple-element.147), channel_id=1, source_target_pairs={{0,16},{8,24},{16,0},{24,8},{1,17},{9,25},{17,1},{25,9},{2,18},{10... | collective-permute-start | bytes 1179656 | tf_op jit(solution)/shard_map/ppermute | solution.py:443
  498.1 63.0 %all-to-all-start.3 = ((bf16[8,96,768]{2,1,0:T(8,128)(2,1)}), bf16[8,96,768]{2,1,0:T(8,128)(2,1)}, u32[]{:S(2)}, u32[]{:S(2)}) async-start(bf16[8,96,768]{2,1,0:T(8,128)(2,1)} %bitcast.213), calls=%async_computation.3 | async-start | bytes 2359296 | tf_op jit(solution)/shard_map/all_to_all | solution.py:530
  504.3 20.4 %collective-permute-start.30 = (bf16[192,1024]{1,0:T(8,128)(2,1)}, bf16[192,1024]{1,0:T(8,128)(2,1)S(1)}, u32[]{:S(2)}, u32[]{:S(2)}) collective-permute-start(bf16[192,1024]{1,0:T(8,128)(2,1)} %get-tuple-element.146), channel_id=1, source_target_pairs={{0,24},{8,16},{16,8},{24,0},{1,25},{9,17},{17,9},{25,1},{2,26},{10... | collective-permute-start | bytes 1179656 | tf_op jit(solution)/shard_map/ppermute | solution.py:443
  505.9 19.1 %collective-permute-start.22 = (bf16[192,1024]{1,0:T(8,128)(2,1)}, bf16[192,1024]{1,0:T(8,128)(2,1)S(1)}, u32[]{:S(2)}, u32[]{:S(2)}) collective-permute-start(bf16[192,1024]{1,0:T(8,128)(2,1)} %get-tuple-element.152), channel_id=1, source_target_pairs={{0,8},{8,0},{16,24},{24,16},{1,9},{9,1},{17,25},{25,17},{2,10},{10... | collective-permute-start | bytes 1179656 | tf_op jit(solution)/shard_map/ppermute | solution.py:443
  507.5 24.8 %collective-permute-start.23 = (bf16[192,1024]{1,0:T(8,128)(2,1)}, bf16[192,1024]{1,0:T(8,128)(2,1)S(1)}, u32[]{:S(2)}, u32[]{:S(2)}) collective-permute-start(bf16[192,1024]{1,0:T(8,128)(2,1)} %get-tuple-element.151), channel_id=1, source_target_pairs={{0,16},{8,24},{16,0},{24,8},{1,17},{9,25},{17,1},{25,9},{2,18},{10... | collective-permute-start | bytes 1179656 | tf_op jit(solution)/shard_map/ppermute | solution.py:443
  507.8 33.3 %collective-permute-start.24 = (bf16[192,1024]{1,0:T(8,128)(2,1)}, bf16[192,1024]{1,0:T(8,128)(2,1)S(1)}, u32[]{:S(2)}, u32[]{:S(2)}) collective-permute-start(bf16[192,1024]{1,0:T(8,128)(2,1)} %get-tuple-element.150), channel_id=1, source_target_pairs={{0,24},{8,16},{16,8},{24,0},{1,25},{9,17},{17,9},{25,1},{2,26},{10... | collective-permute-start | bytes 1179656 | tf_op jit(solution)/shard_map/ppermute | solution.py:443
  515.7 35.5 %collective-permute-start.37 = (bf16[3,96,192]{1,2,0:T(8,128)(2,1)}, bf16[3,96,192]{1,2,0:T(8,128)(2,1)}, u32[]{:S(2)}, u32[]{:S(2)}) collective-permute-start(bf16[3,96,192]{1,2,0:T(8,128)(2,1)} %get-tuple-element.192), channel_id=1, source_target_pairs={{0,8},{8,0},{16,24},{24,16},{1,9},{9,1},{17,25},{25,17},{2,10},{10... | collective-permute-start | bytes 331784 | tf_op jit(solution)/shard_map/ppermute | solution.py:443
  524.7 26.4 %collective-permute-start.38 = (bf16[3,96,192]{1,2,0:T(8,128)(2,1)}, bf16[3,96,192]{1,2,0:T(8,128)(2,1)}, u32[]{:S(2)}, u32[]{:S(2)}) collective-permute-start(bf16[3,96,192]{1,2,0:T(8,128)(2,1)} %get-tuple-element.192), channel_id=1, source_target_pairs={{0,16},{8,24},{16,0},{24,8},{1,17},{9,25},{17,1},{25,9},{2,18},{10... | collective-permute-start | bytes 331784 | tf_op jit(solution)/shard_map/ppermute | solution.py:443
  525.1 26.1 %collective-permute-start.39 = (bf16[3,96,192]{1,2,0:T(8,128)(2,1)}, bf16[3,96,192]{1,2,0:T(8,128)(2,1)}, u32[]{:S(2)}, u32[]{:S(2)}) collective-permute-start(bf16[3,96,192]{1,2,0:T(8,128)(2,1)} %get-tuple-element.192), channel_id=1, source_target_pairs={{0,24},{8,16},{16,8},{24,0},{1,25},{9,17},{17,9},{25,1},{2,26},{10... | collective-permute-start | bytes 331784 | tf_op jit(solution)/shard_map/ppermute | solution.py:443
  (58 other events, 521.2 us)
Sparse Core Ops, SparseCore 0:
  18.1 53.0 all-gather.5
  73.9 81.9 all-gather.3
  203.9 67.0 all-gather.7

commit v3 on v2

--- a/solution.py
+++ b/solution.py
@@ -180,7 +180,7 @@
             pl.BlockSpec((1, 1, bq), lambda i: (i, 0, 0)),
         ),
         scratch_shapes=[pltpu.VMEM((S, bq), f32)],
-        compiler_params=pltpu.CompilerParams(vmem_limit_bytes=48 * 2**20),
+        compiler_params=pltpu.CompilerParams(vmem_limit_bytes=58 * 2**20),
         cost_estimate=pl.CostEstimate(
             flops=16 * HD * S * S, bytes_accessed=2 * S * S, transcendentals=S * S
         ),
@@ -189,17 +189,20 @@
 
 
 def attend_back_kernel(
-    kc, nq, per, v_ref, kt_ref, q_ref, o_ref, linv_ref, p_ref, cos_ref, sin_ref, *refs
+    kc, nq, per, v_ref, kt_ref, q_ref, o_ref, linv_ref, p_ref, cos_ref, sin_ref, n_ref, *refs
 ):
-    out_ref, acc_ref, do_ref = refs[-3:]
+    out_ref, grad_ref, acc_ref, do_ref, held_ref, sem = refs[-6:]
     i = pl.program_id(0)
     rows = v_ref.shape[1]
     bq = q_ref.shape[2]
+    groups = out_ref.shape[0]
+    fetch = pltpu.make_async_copy(n_ref, held_ref, sem)
 
     @pl.when(i == 0)
     def _():
+        fetch.start()
         acc_ref[...] = jnp.zeros_like(acc_ref)
-        for j in range(len(refs) - 3):
+        for j in range(groups):
             do_ref[j] = refs[j][...]
 
     do = do_ref[i // per, :, pl.ds(pl.multiple_of((i % per) * bq, bq), bq)]
@@ -227,8 +230,9 @@
 
     @pl.when(i == nq - 1)
     def _():
-        groups = out_ref.shape[0]
+        fetch.wait()
         width = rows // groups
+        grad = jnp.zeros((3 * HD, D), f32)
         for j in range(groups):
             at = slice(j * width, (j + 1) * width)
             t = acc_ref[at, :].T
@@ -237,16 +241,24 @@
             dk = dk * cos_ref[:, at] + turned_k * sin_ref[:, at]
             out_ref[j, HD : 2 * HD] = dk.astype(bf)
             out_ref[j, 2 * HD :] = t[:HD].astype(bf)
-
-
-def attend_back(h, v, kt, qt, do, o, linv, p, cos, sin, groups, bq=512, kc=512):
+            grad = grad + dg(out_ref[j], held_ref[at, :], NN)
+        grad_ref[:, : 3 * HD] = grad.T.astype(bf)
+        grad_ref[:, 3 * HD :] = jnp.zeros((D, HD), bf)
+
+
+def attend_back(h, v, kt, qt, do, o, linv, p, cos, sin, normed, groups, place, after, bq=512, kc=512):
     S = v.shape[1]
     nq = S // bq
     per = nq // groups
+    columns, column, earlier = place
+    extra = list(after) if earlier is None else [earlier] + list(after)
     return pl.pallas_call(
         functools.partial(attend_back_kernel, kc, nq, per),
         grid=(nq,),
-        out_shape=jax.ShapeDtypeStruct((groups, 3 * HD, S // groups), bf),
+        out_shape=(
+            jax.ShapeDtypeStruct((groups, 3 * HD, S // groups), bf),
+            jax.ShapeDtypeStruct((D, columns), bf),
+        ),
         in_specs=[
             pl.BlockSpec((1, S, 128), lambda i: (h, 0, 0)),
             pl.BlockSpec((1, HD, S), lambda i: (h, 0, 0)),
@@ -256,16 +268,27 @@
             pl.BlockSpec((1, S, bq), lambda i: (i, 0, 0)),
             pl.BlockSpec((HD, S), lambda i: (0, 0)),
             pl.BlockSpec((HD, S), lambda i: (0, 0)),
+            pl.BlockSpec(memory_space=pl.ANY),
         ]
-        + [pl.BlockSpec((HD, S // groups), lambda i: (0, 0))] * groups,
-        out_specs=pl.BlockSpec((groups, 3 * HD, S // groups), lambda i: (0, 0, 0)),
-        scratch_shapes=[pltpu.VMEM((S, 128), f32), pltpu.VMEM((groups, HD, S // groups), bf)],
-        compiler_params=pltpu.CompilerParams(vmem_limit_bytes=48 * 2**20),
+        + [pl.BlockSpec((HD, S // groups), lambda i: (0, 0))] * groups
+        + [pl.BlockSpec(memory_space=pl.ANY)] * len(extra),
+        out_specs=(
+            pl.BlockSpec((groups, 3 * HD, S // groups), lambda i: (0, 0, 0)),
+            pl.BlockSpec((D, 256), lambda i: (0, column)),
+        ),
+        scratch_shapes=[
+            pltpu.VMEM((S, 128), f32),
+            pltpu.VMEM((groups, HD, S // groups), bf),
+            pltpu.VMEM((S, D), bf),
+            pltpu.SemaphoreType.DMA,
+        ],
+        input_output_aliases={} if earlier is None else {9 + groups: 1},
+        compiler_params=pltpu.CompilerParams(vmem_limit_bytes=58 * 2**20),
         cost_estimate=pl.CostEstimate(
             flops=24 * HD * S * S, bytes_accessed=2 * S * S, transcendentals=0
         ),
         name="attend_back",
-    )(v, kt, qt, o, linv, p, cos, sin, *do)
+    )(v, kt, qt, o, linv, p, cos, sin, normed, *do, *extra)
 
 
 def normalize_back(gradient, unit_rows, inverse, gain_row):
@@ -427,6 +450,185 @@
     )(info, x, d_hidden, w, *chunks)
 
 
+def own_kernel(groups, heads, info_ref, w_ref, gain_ref, out_ref):
+    for g in range(groups):
+
+        @pl.when(info_ref[0] == g)
+        def _():
+            def piece(t, h):
+                start = t * D + (g * heads + h) * HD
+                return w_ref[:, start : start + HD]
+
+            pieces = []
+            for h in range(heads):
+                pieces += [piece(0, h), piece(1, h)]
+            pieces += [piece(2, h) for h in range(heads)] + [gain_ref[...]]
+            missing = out_ref.shape[1] - 3 * heads * HD - 1
+            pieces.append(jnp.zeros((w_ref.shape[0], missing), bf))
+            out_ref[...] = jnp.concatenate(pieces, axis=1)
+
+
+def own_columns(groups, heads, info, w, gain):
+    width = (3 * heads * HD + 128) // 128 * 128
+    return pl.pallas_call(
+        functools.partial(own_kernel, groups, heads),
+        out_shape=jax.ShapeDtypeStruct((w.shape[0], width), bf),
+        in_specs=[
+            pl.BlockSpec(memory_space=pltpu.SMEM),
+            pl.BlockSpec(memory_space=pltpu.VMEM),
+            pl.BlockSpec(memory_space=pltpu.VMEM),
+        ],
+        out_specs=pl.BlockSpec(memory_space=pltpu.VMEM),
+        name="own_columns",
+    )(info, w, gain)
+
+
+def tables_kernel(cos_ref, sin_ref, cos_rows_ref, sin_rows_ref, cos_t_ref, sin_t_ref):
+    c, s = cos_ref[...], sin_ref[...]
+    cos_t_ref[...] = jnp.concatenate([c, c], axis=0)
+    sin_t_ref[...] = jnp.concatenate([s, s], axis=0)
+    scale = HD**-0.5 * LOG2E
+    cos_rows_ref[...] = jnp.concatenate([c * scale, c * scale, c, c], axis=0).T
+    sin_rows_ref[...] = jnp.concatenate([s * -scale, s * scale, -s, s], axis=0).T
+
+
+def tables(cosine, sine):
+    half, S = cosine.shape
+    rb = min(1024, S)
+    return pl.pallas_call(
+        tables_kernel,
+        grid=(S // rb,),
+        out_shape=(jax.ShapeDtypeStruct((S, 4 * half), f32),) * 2
+        + (jax.ShapeDtypeStruct((2 * half, S), f32),) * 2,
+        in_specs=[pl.BlockSpec((half, rb), lambda i: (0, i))] * 2,
+        out_specs=(pl.BlockSpec((rb, 4 * half), lambda i: (i, 0)),) * 2
+        + (pl.BlockSpec((2 * half, rb), lambda i: (0, i)),) * 2,
+        name="tables",
+    )(cosine, sine)
+
+
+def grads_kernel(place_ref, second_ref, dgu_ref, mixed_ref, branch_ref, inner_ref, dy_ref, wide_ref, tall_ref):
+    g = pl.program_id(0)
+    end = pl.num_programs(0) - 1
+
+    @pl.when(g < end)
+    def _():
+        wide_ref[0] = dg(second_ref[...], dgu_ref[...], TN).astype(bf)
+        tall_ref[...] = dg(inner_ref[...], dy_ref[...], TN).astype(bf)
+
+    @pl.when(g == end)
+    def _():
+        wide_ref[0] = dg(mixed_ref[...], branch_ref[...], NN).astype(bf)
+
+
+def grads(place, second, d_gate_up, mixed_t, branch, inner, dy):
+    rows = second.shape[0]
+    ff = inner.shape[1]
+    steps = 2 * ff // D
+    whole = lambda i, p: (0, 0)
+    column = lambda i, p: (0, jnp.minimum(i, steps - 1))
+    return pl.pallas_call(
+        grads_kernel,
+        grid_spec=pltpu.PrefetchScalarGridSpec(
+            num_scalar_prefetch=1,
+            grid=(steps + 1,),
+            in_specs=[
+                pl.BlockSpec((rows, D), whole),
+                pl.BlockSpec((rows, D), column),
+                pl.BlockSpec((D, rows), whole),
+                pl.BlockSpec((rows, D), whole),
+                pl.BlockSpec((rows, ff // steps), column),
+                pl.BlockSpec((rows, D), whole),
+            ],
+            out_specs=(
+                pl.BlockSpec((1, D, D), lambda i, p: (i ^ p[0], 0, 0)),
+                pl.BlockSpec((ff // steps, D), lambda i, p: (jnp.minimum(i, steps - 1), 0)),
+            ),
+        ),
+        out_shape=(
+            jax.ShapeDtypeStruct((steps + 1, D, D), bf),
+            jax.ShapeDtypeStruct((ff, D), bf),
+        ),
+        compiler_params=pltpu.CompilerParams(vmem_limit_bytes=48 * 2**20),
+        cost_estimate=pl.CostEstimate(
+            flops=2 * rows * D * (3 * ff + D), bytes_accessed=20 * 2**20, transcendentals=0
+        ),
+        name="grads",
+    )(place, second, d_gate_up, mixed_t, branch, inner, dy)
+
+
+def add_kernel(count, *refs):
+    total = None
+    for ref in refs[:count]:
+        for j in range(ref.shape[0]):
+            term = ref[j].astype(f32)
+            total = term if total is None else total + term
+    out_ref = refs[-1]
+    out_ref[...] = total.astype(out_ref.dtype)
+
+
+def add_up(arrays, after, dtype=bf, leading=None):
+    arrays = [a if a.ndim == 3 else a[None] for a in arrays]
+    rows, columns = arrays[0].shape[1:]
+    rb = 256 if rows % 256 == 0 else rows
+    first = arrays[0].shape[0] if leading is None else leading
+    lead = [first] + [a.shape[0] for a in arrays[1:]]
+    return pl.pallas_call(
+        functools.partial(add_kernel, len(arrays)),
+        grid=(rows // rb,),
+        out_shape=jax.ShapeDtypeStruct((rows, columns), dtype),
+        in_specs=[pl.BlockSpec((n, rb, columns), lambda i: (0, i, 0)) for n in lead]
+        + [pl.BlockSpec(memory_space=pl.ANY)] * len(after),
+        out_specs=pl.BlockSpec((rb, columns), lambda i: (i, 0)),
+        compiler_params=pltpu.CompilerParams(vmem_limit_bytes=48 * 2**20),
+        name="add_up",
+    )(*arrays, *after)
+
+
+def finish_wide_kernel(groups, info_ref, w_ref, gain_ref, *refs):
+    in_ref, proj_ref, dgain_ref, held_ref = refs[groups : groups + 4]
+    for j in range(groups):
+        held_ref[info_ref[0] ^ j] = refs[j][...]
+    total = 0.0
+    for g in range(groups - 1):
+        at = slice(g * D, (g + 1) * D)
+        grad = held_ref[g].astype(f32)
+        in_ref[:, at] = grad
+        total = total + jnp.sum(w_ref[:, at].astype(f32) * grad, axis=1, keepdims=True)
+    proj_ref[...] = held_ref[groups - 1].astype(f32)
+    dgain_ref[...] = total / gain_ref[...].astype(f32)
+
+
+def finish_qkv_kernel(groups, heads, info_ref, w_ref, gain_ref, *refs):
+    out_ref, dgain_ref, held_ref = refs[groups : groups + 3]
+    for j in range(groups):
+        held_ref[info_ref[0] ^ j] = refs[j][...]
+    pieces = []
+    for t in range(3):
+        for g in range(groups):
+            for h in range(heads):
+                start = h * 256 + t * HD
+                pieces.append(held_ref[g, :, start : start + HD].astype(f32))
+    grad = jnp.concatenate(pieces, axis=1)
+    out_ref[...] = grad
+    total = jnp.sum(w_ref[...].astype(f32) * grad, axis=1, keepdims=True)
+    dgain_ref[...] = total / gain_ref[...].astype(f32)
+
+
+def finish(kernel, groups, info, w, gain, parts, widths, name):
+    shard = w.shape[0]
+    vmem = pl.BlockSpec(memory_space=pltpu.VMEM)
+    return pl.pallas_call(
+        kernel,
+        out_shape=tuple(jax.ShapeDtypeStruct((shard, n), f32) for n in widths),
+        in_specs=[pl.BlockSpec(memory_space=pltpu.SMEM)] + [vmem] * (2 + groups),
+        out_specs=(vmem,) * len(widths),
+        scratch_shapes=[pltpu.VMEM((groups,) + parts[0].shape, bf)],
+        compiler_params=pltpu.CompilerParams(vmem_limit_bytes=48 * 2**20),
+        name=name,
+    )(info, w, gain, *parts)
+
+
 def body(
     tokens, lengths, attn_gain, qkv_weight, proj_weight, ffn_gain, in_weight, out_weight, out_grad
 ):
@@ -445,46 +647,26 @@
     def exchange(chunks):
         return [chunks[0]] + [swap(chunks[j], j) for j in range(1, groups)]
 
-    def relative(array, axis):
-        return [lax.dynamic_index_in_dim(array, me ^ j, axis, False) for j in range(groups)]
-
     def gather(array):
         return lax.all_gather(array, "fsdp", axis=0, tiled=True)
 
-    own = lax.dynamic_index_in_dim(
-        qkv_weight.reshape(shard, 3, groups, heads, HD), me, 2, False
-    )
-    pieces = []
-    for h in range(heads):
-        pieces += [own[:, 0, h], own[:, 1, h]]
-    pieces += [own[:, 2, h] for h in range(heads)] + [attn_gain[:, None]]
-    used = 3 * heads * HD + 1
-    pieces.append(jnp.zeros((shard, -used % 128), bf))
-    own = jnp.concatenate(pieces, axis=1)
+    place = jnp.stack([me]).astype(jnp.int32)
+    x0 = tokens[0]
+    across = swap(x0, 2)
+    near = swap(x0, 1)
+    own = own_columns(groups, heads, place, qkv_weight, attn_gain[:, None])
     if shards <= 8:
         parts = [own] + [swap(own, j, "fsdp") for j in range(1, shards)]
     else:
         parts = [gather(own)]
-
-    x0 = tokens[0]
-    blocks = [x0]
-    step = 1
-    while step < groups:
-        blocks = blocks + [swap(b, step) for b in blocks]
-        step *= 2
+    blocks = [x0, near, across, swap(across, 1)]
 
     half = HD // 2
     frequency = rope_base ** (-(lax.iota(f32, half) * 2.0) / HD)
     starts = [(me ^ j) * rows for j in range(groups)]
     positions = jnp.concatenate([s + lax.iota(jnp.int32, rows) for s in starts]).astype(f32)
     angles = frequency[:, None] * positions[None, :]
-    cosine, sine = jnp.cos(angles), jnp.sin(angles)
-    cos_t = jnp.concatenate([cosine, cosine], axis=0)
-    sin_t = jnp.concatenate([sine, sine], axis=0)
-    scale = HD**-0.5 * LOG2E
-    cos_rows = jnp.concatenate([cos_t * scale, cos_t], axis=0).T
-    signed = jnp.concatenate([-sine, sine], axis=0)
-    sin_rows = jnp.concatenate([signed * scale, signed], axis=0).T
+    cos_rows, sin_rows, cos_t, sin_t = tables(jnp.cos(angles), jnp.sin(angles))
 
     carried = None
     for j in range(groups):
@@ -510,67 +692,64 @@
         kept.append((p, o, linv))
         chunks += exchange([ob[j] for j in range(groups)])
 
-    place = jnp.stack([me]).astype(jnp.int32)
     dy = out_grad[0]
     result, d_hidden, d_heads, mixed_t, second, d_gate_up, inner, branch = middle(
         groups, heads, place, x0, dy, wide, out_full, chunks
     )
     d_mixed = [exchange([d_heads[h, j] for j in range(groups)]) for h in range(heads)]
 
-    def over_seq(array):
-        parts = array.astype(bf).reshape(array.shape[0], groups, -1)
-        mine = relative(parts, 1)
-        total = mine[0].astype(f32)
-        for j in range(1, groups):
-            total = total + swap(mine[j], j).astype(f32)
-        return total.astype(bf)
-
     def to_owner(array):
         parts = array.reshape(shards, array.shape[0] // shards, -1)
-        parts = lax.all_to_all(parts, "fsdp", split_axis=0, concat_axis=0, tiled=True)
-        return jnp.sum(parts.astype(f32), axis=0).astype(bf)
-
-    def from_seq(array):
-        parts = jnp.stack([array] + [swap(array, j) for j in range(1, groups)])
-        return relative(parts, 0)
-
-    grad_out = dg(inner, dy, TN)
-    grad_in = dg(second, d_gate_up, TN)
-    grad_proj = dg(mixed_t, branch, NN)
-    part_in = to_owner(over_seq(jnp.concatenate([grad_in, grad_proj], axis=1)))
-    part_out = to_owner(over_seq(grad_out))
-    wide_grad = jnp.concatenate(from_seq(part_in), axis=1).astype(f32)
-    out_weight_grad = jnp.concatenate(from_seq(part_out), axis=1).astype(f32)
-    in_weight_grad, proj_weight_grad = wide_grad[:, :ff2], wide_grad[:, ff2:]
-
-    normed_blocks = normed.reshape(groups, rows, D)
-    received = []
-    qkv_parts = []
-    for h in range(heads):
+        return lax.all_to_all(parts, "fsdp", split_axis=0, concat_axis=0, tiled=True)
+
+    def from_peers(array):
+        return [array] + [swap(array, j) for j in range(1, groups)]
+
+    wide_grad, tall_grad = grads(place, second, d_gate_up, mixed_t, branch, inner, dy)
+    wide_sent = [swap(wide_grad[j], j) for j in range(1, groups)]
+    tall_parts = to_owner(tall_grad)
+
+    def back(h, grad_place, after):
         p, o, linv = kept[h]
-        d_own = attend_back(h, v, kt, qt, d_mixed[h], o, linv, p, cos_t, sin_t, groups)
-        received += exchange([d_own[j] for j in range(groups)])
-        grad = jnp.einsum("jdp,jpf->fd", d_own, normed_blocks, preferred_element_type=f32)
-        qkv_parts.append(to_owner(grad.astype(bf)))
-    qkv_all = jnp.stack(from_seq(jnp.stack(qkv_parts)))
-    qkv_weight_grad = (
-        qkv_all.reshape(groups, heads, shard, 3, HD)
-        .transpose(2, 3, 0, 1, 4)
-        .reshape(shard, 3 * D)
-        .astype(f32)
-    )
+        own, grad = attend_back(
+            h, v, kt, qt, d_mixed[h], o, linv, p, cos_t, sin_t, normed, groups, grad_place, after
+        )
+        return exchange([own[j] for j in range(groups)]), grad
+
+    received, qkv_first = back(0, (512, 0, None), [tall_grad])
+    wide_sum = add_up([wide_grad] + wide_sent, [qkv_first], leading=1)
+    wide_parts = to_owner(wide_sum)
+    tall_sum = add_up([tall_parts], [qkv_first])
+    tall_peers = from_peers(tall_sum)
+    more, qkv_first = back(1, (512, 1, qkv_first), [wide_sum, tall_sum])
+    received += more
+    qkv_parts = to_owner(qkv_first)
+    wide_owned = add_up([wide_parts], [qkv_first])
+    wide_peers = from_peers(wide_owned)
+    out_weight_grad = add_up(tall_peers, [qkv_first], dtype=f32)
+    more, qkv_second = back(2, (256, 0, None), [wide_owned, out_weight_grad])
+    received += more
+    qkv_second_parts = to_owner(qkv_second)
+
+    in_weight_grad, proj_weight_grad, ffn_gain_grad = finish(
+        functools.partial(finish_wide_kernel, groups),
+        groups, place, in_weight, ffn_gain[:, None], wide_peers, (ff2, D, 1), "finish_wide",
+    )
+    first_sum = add_up([qkv_parts], [qkv_second])
+    second_sum = add_up([qkv_second_parts], [])
+    qkv_peers = from_peers(jnp.concatenate([first_sum, second_sum], axis=1))
     tokens_grad = last(groups, heads, place, x0, d_hidden, qkv_full, received)
-
-    def gain_grad(weight, grad, gain):
-        return jnp.sum(weight.astype(f32) * grad, axis=1) / gain.astype(f32)
-
+    qkv_weight_grad, attn_gain_grad = finish(
+        functools.partial(finish_qkv_kernel, groups, heads),
+        groups, place, qkv_weight, attn_gain[:, None], qkv_peers, (3 * D, 1), "finish_qkv",
+    )
     return (
         result[None],
         tokens_grad[None],
-        gain_grad(qkv_weight, qkv_weight_grad, attn_gain),
+        attn_gain_grad[:, 0],
         qkv_weight_grad,
         proj_weight_grad,
-        gain_grad(in_weight, in_weight_grad, ffn_gain),
+        ffn_gain_grad[:, 0],
         in_weight_grad,
         out_weight_grad,
     )

time: 587 us -> 549 us (0.935)
  local copies, waits for them, and re-layouts: 78.5 us -> 29.5 us
  Pallas kernels: 274 us -> 312 us
  other arithmetic: 35.7 us -> 5.17 us
  matrix products: 24.2 us -> 0 us
  waiting for transfers between devices: 76.7 us -> 97.1 us
  blocking collectives: 0 us -> 14.2 us
  starting transfers between devices: 76.4 us -> 65.9 us
    ppermute x52 -> x49, waiting for transfers between devices: 66.5 us -> 95.8 us  [swap(): return lax.ppermute(array, axis, [(i, i ^ j) for i in range(size)])]
    pallas_call x0 -> x11, Pallas kernels: none -> 27.1 us  [the longest x1 11.2 us: grads(): pl.pallas_call(grads_kernel, grid_spec=pltpu.PrefetchScalarGridSpec(num_s...]
    dot_general x6 -> x0, matrix products: 24.2 us -> none  [the longest x3 14.4 us: body(): jnp.einsum('jdp,jpf->fd', d_own, normed_blocks, preferred_element_type=f32)]
    dynamic_slice x5 -> x0, local copies, waits for them, and re-layouts: 18.1 us -> none  [the longest x3 17.9 us: relative(): lax.dynamic_index_in_dim(array, me ^ j, axis, False)]
    all_to_all x0 -> x1, blocking collectives: none -> 14.2 us  [to_owner(): lax.all_to_all(parts, 'fsdp', split_axis=0, concat_axis=0, tiled=True)]
    all_to_all x5 -> x3, starting transfers between devices: 28.2 us -> 15.2 us  [to_owner(): lax.all_to_all(parts, 'fsdp', split_axis=0, concat_axis=0, tiled=True)]
    unnamed x98 -> x68, local copies, waits for them, and re-layouts: 23.6 us -> 11.9 us
    pallas_call x3, Pallas kernels: 116 us -> 126 us  [attend_back(): pl.pallas_call(functools.partial(attend_back_kernel, kc, nq, per), grid=(...]
  transfers between devices with their start and end apart: 60 -> 55, of which waited for: 16 -> 18; matrix products, arithmetic and copies ran while one was open for 20% -> 4% of each run, Pallas kernels for 47% -> 50%
where the time goes in v3:
time: 549 us; the launch traced here: 539 us
  Pallas kernels  312 us (57%)
  waiting for transfers between devices  97.1 us (18%)
  starting transfers between devices  65.9 us (12%)
  local copies, waits for them, and re-layouts  29.5 us (5%)
  between operations  15 us (3%)
  blocking collectives  14.2 us (3%)
    pallas_call x3, Pallas kernels, attend_back(): pl.pallas_call(functools.partial(attend_back_kernel, kc, nq, per), grid=(...  126 us
    ppermute x49, waiting for transfers between devices, swap(): return lax.ppermute(array, axis, [(i, i ^ j) for i in range(size)])  95.8 us
    pallas_call x3, Pallas kernels, attend(): pl.pallas_call(functools.partial(attend_kernel, kc), grid=(nq,), out_shap...  95.4 us
    ppermute x49, starting transfers between devices, swap(): return lax.ppermute(array, axis, [(i, i ^ j) for i in range(size)])  50.6 us
    pallas_call x1, Pallas kernels, middle(): pl.pallas_call(functools.partial(middle_kernel, groups, heads, ff), grid=...  27.9 us
    pallas_call x4, Pallas kernels, qkv_call(): pl.pallas_call(functools.partial(qkv_kernel, heads, len(parts)), grid=(st...  25.6 us
    all_to_all x3, starting transfers between devices, to_owner(): lax.all_to_all(parts, 'fsdp', split_axis=0, concat_axis=0, tiled=True)  15.2 us
    all_to_all x1, blocking collectives, to_owner(): lax.all_to_all(parts, 'fsdp', split_axis=0, concat_axis=0, tiled=True)  14.2 us
  transfers between devices with their start and end apart: 55, of which 18 were waited for; matrix products, arithmetic and copies ran while one was open for 4% of the time, Pallas kernels for 50%

profile of v3, /device:TPU:1, one launch (start us, length us, event | category | flops | bytes accessed | tf_op | source)
XLA Modules:
  0.0 539.1 jit_solution(3280720905082130603)
XLA Ops:
  10.5 5.1 collective-permute-start
  16.3 2.0 concatenate.16
  21.2 2.3 collective-permute-start.4
  23.5 2.1 collective-permute-start.9
  26.3 27.5 %collective-permute-done.1.x_ref = bf16[1024,768]{1,0:T(8,128)(2,1)} collective-permute-done((bf16[1024,768]{1,0:T(8,128)(2,1)S(1)}, bf16[1024,768]{1,0:T(8,128)(2,1)}, u32[]{:S(2)}, u32[]{:S(2)}) %collective-permute-start.1) | collective-permute-done | bytes 1572896 | tf_op jit(solution)/shard_map/ppermute | solution.py:645
  53.8 2.2 collective-permute-start.2
  56.0 2.8 multiply_sine_fusion
  59.9 1.9 collective-permute-start.7
  61.8 3.3 collective-permute-start.8
  65.2 4.8 tables.1
  70.1 7.7 %collective-permute-done.6.refs_4_ = bf16[96,640]{1,0:T(8,128)(2,1)S(1)} collective-permute-done((bf16[96,640]{1,0:T(8,128)(2,1)S(1)}, bf16[96,640]{1,0:T(8,128)(2,1)S(1)}, u32[]{:S(2)}, u32[]{:S(2)}) %collective-permute-start.6) | collective-permute-done | bytes 122912 | tf_op jit(solution)/shard_map/ppermute | solution.py:645
  77.8 2.6 collective-permute-done.7.refs_5_
  80.4 6.1 %qkv.4 = (bf16[4096,768]{1,0:T(8,128)(2,1)}, bf16[3,4096,128]{2,1,0:T(8,128)(2,1)}, bf16[3,4096,128]{2,1,0:T(8,128)(2,1)}, bf16[3,128,4096]{2,1,0:T(8,128)(2,1)}...) custom-call(s32[3]{0:T(128)S(1)} %add_add_fusion.3.info_ref, bf16[1024,768]{1,0:T(8,128)(2,1)S(1)} %bitcast.105, ...), custom_call_target="tpu_custom_call" | custom-call | flops 2013265920 | bytes 8388608 | tf_op jit(solution)/shard_map/qkv/pallas_call | solution.py:111
  86.6 6.5 %qkv.5 = (bf16[4096,768]{1,0:T(8,128)(2,1)}, bf16[3,4096,128]{2,1,0:T(8,128)(2,1)}, bf16[3,4096,128]{2,1,0:T(8,128)(2,1)}, bf16[3,128,4096]{2,1,0:T(8,128)(2,1)}...) custom-call(s32[3]{0:T(128)S(1)} %add_add_fusion.2.info_ref, ...), custom_call_target="tpu_custom_call", output_to_operand_aliasing={{0}: (12, {}), {1}: (13, {}), {2}: (14, {}), {3}: (15, {}),... | custom-call | flops 2013265920 | bytes 8388608 | tf_op jit(solution)/shard_map/qkv/pallas_call | solution.py:111
  93.1 6.4 %qkv.6 = (bf16[4096,768]{1,0:T(8,128)(2,1)}, bf16[3,4096,128]{2,1,0:T(8,128)(2,1)}, bf16[3,4096,128]{2,1,0:T(8,128)(2,1)}, bf16[3,128,4096]{2,1,0:T(8,128)(2,1)}...) custom-call(s32[3]{0:T(128)S(1)} %add_add_fusion.1.info_ref, ...), custom_call_target="tpu_custom_call", output_to_operand_aliasing={{0}: (12, {}), {1}: (13, {}), {2}: (14, {}), {3}: (15, {}),... | custom-call | flops 2013265920 | bytes 8388608 | tf_op jit(solution)/shard_map/qkv/pallas_call | solution.py:111
  99.5 6.5 %qkv.7 = (bf16[4096,768]{1,0:T(8,128)(2,1)}, bf16[3,4096,128]{2,1,0:T(8,128)(2,1)}, bf16[3,4096,128]{2,1,0:T(8,128)(2,1)}, bf16[3,128,4096]{2,1,0:T(8,128)(2,1)}...) custom-call(s32[3]{0:T(128)S(1)} %add_add_fusion.info_ref, ...), custom_call_target="tpu_custom_call", output_to_operand_aliasing={{0}: (12, {}), {1}: (13, {}), {2}: (14, {}), {3}: (15, {}),... | custom-call | flops 2013265920 | bytes 8388608 | tf_op jit(solution)/shard_map/qkv/pallas_call | solution.py:111
  107.4 32.1 %attend.5 = (bf16[8,4096,512]{2,1,0:T(8,128)(2,1)}, f32[64,4096]{1,0:T(8,128)}, bf16[4,64,1024]{2,1,0:T(8,128)(2,1)}, f32[8,1,512]{2,1,0:T(1,128)}) custom-call(bf16[3,4096,128]{2,1,0:T(8,128)(2,1)} %get-tuple-element.95.k_ref, bf16[3,128,4096]{2,1,0:T(8,128)(2,1)} %get-tuple-element.96.q_ref, bf16[3,80,4096]{2,1,0:T(8,128)(2,1)} %copy-done), custom_call_target="tpu_custom_call" | custom-call | flops 17179869184 | bytes 33554432 | tf_op jit(solution)/shard_map/attend/pallas_call | solution.py:162
  143.0 31.8 %attend.4 = (bf16[8,4096,512]{2,1,0:T(8,128)(2,1)}, f32[64,4096]{1,0:T(8,128)}, bf16[4,64,1024]{2,1,0:T(8,128)(2,1)}, f32[8,1,512]{2,1,0:T(1,128)}) custom-call(bf16[3,4096,128]{2,1,0:T(8,128)(2,1)} %get-tuple-element.95.k_ref, bf16[3,128,4096]{2,1,0:T(8,128)(2,1)} %get-tuple-element.96.q_ref, bf16[3,80,4096]{2,1,0:T(8,128)(2,1)} %copy-done), custom_call_target="tpu_custom_call" | custom-call | flops 17179869184 | bytes 33554432 | tf_op jit(solution)/shard_map/attend/pallas_call | solution.py:162
  177.3 31.6 %attend.3 = (bf16[8,4096,512]{2,1,0:T(8,128)(2,1)}, f32[64,4096]{1,0:T(8,128)}, bf16[4,64,1024]{2,1,0:T(8,128)(2,1)}, f32[8,1,512]{2,1,0:T(1,128)}) custom-call(bf16[3,4096,128]{2,1,0:T(8,128)(2,1)} %get-tuple-element.95.k_ref, bf16[3,128,4096]{2,1,0:T(8,128)(2,1)} %get-tuple-element.96.q_ref, bf16[3,80,4096]{2,1,0:T(8,128)(2,1)} %copy-done), custom_call_target="tpu_custom_call" | custom-call | flops 17179869184 | bytes 33554432 | tf_op jit(solution)/shard_map/attend/pallas_call | solution.py:162
  213.0 3.0 collective-permute-done.15.refs_7_
  216.0 2.8 collective-permute-done.11.refs_2_
  218.8 2.8 collective-permute-done.12.refs_3_
  221.6 27.9 %middle.1 = (bf16[1024,768]{1,0:T(8,128)(2,1)}, f32[1024,768]{1,0:T(8,128)}, bf16[3,4,64,1024]{3,2,1,0:T(8,128)(2,1)S(1)}, bf16[768,1024]{1,0:T(8,128)(2,1)S(1)}...) custom-call(s32[1]{0:T(128)} %bitcast.info_ref.place_ref, ...), custom_call_target="tpu_custom_call" | custom-call | flops 15099494400 | bytes 31457280 | tf_op jit(solution)/shard_map/middle/pallas_call | solution.py:367
  253.5 11.2 %grads.1 = (bf16[4,768,768]{2,1,0:T(8,128)(2,1)}, bf16[1152,768]{1,0:T(8,128)(2,1)}) custom-call(s32[1]{0:T(128)} %bitcast.info_ref.place_ref, bf16[1024,768]{1,0:T(8,128)(2,1)S(1)} %copy-done.21, bf16[1024,2304]{1,0:T(8,128)(2,1)} %get-tuple-element.115.dgu_ref, bf16[768,1024]{1,0:T(8,128)(2,1)S(1)} %get-tuple-element.116.mixed_ref, ...), custom_call_target="tpu_custom_call" | custom-call | flops 6643777536 | bytes 20971520 | tf_op jit(solution)/shard_map/grads/pallas_call | solution.py:530
  264.7 4.1 all-to-all-start
  268.8 2.4 slice_bitcast_fusion.15
  273.7 3.8 slice_bitcast_fusion
  277.9 1.8 collective-permute-start.30
  281.0 42.3 %attend_back.3 = (bf16[4,192,1024]{2,1,0:T(8,128)(2,1)}, bf16[768,512]{1,0:T(8,128)(2,1)}) custom-call(bf16[3,4096,128]{2,1,0:T(8,128)(2,1)} %get-tuple-element.105.v_ref, bf16[3,64,4096]{2,1,0:T(8,128)(2,1)} %copy-done.1, bf16[3,128,4096]{2,1,0:T(8,128)(2,1)} %get-tuple-element.96.q_ref, f32[64,4096]{1,0:T(8,128)} %get-tuple-element.107.o_ref, ...), custom_call_target="tpu_custom_call" | custom-call | flops 25769803776 | bytes 33554432 | tf_op jit(solution)/shard_map/attend_back/pallas_call | solution.py:255
  326.4 5.4 %collective-permute-done.30 = bf16[768,768]{1,0:T(8,128)(2,1)} collective-permute-done((bf16[768,768]{1,0:T(8,128)(2,1)}, bf16[768,768]{1,0:T(8,128)(2,1)}, u32[]{:S(2)}, u32[]{:S(2)}) %collective-permute-start.30) | collective-permute-done | bytes 1179680 | tf_op jit(solution)/shard_map/ppermute | solution.py:645
  331.8 4.0 add_up.6.refs_5_
  335.8 6.0 %all-to-all-start.1 = ((bf16[8,96,768]{2,1,0:T(8,128)(2,1)}), bf16[8,96,768]{2,1,0:T(8,128)(2,1)S(1)}, u32[]{:S(2)}, u32[]{:S(2)}) async-start(bf16[8,96,768]{2,1,0:T(8,128)(2,1)} %bitcast.50), calls=%async_computation.1 | async-start | bytes 2359296 | tf_op jit(solution)/shard_map/all_to_all | solution.py:703
  342.1 2.3 collective-permute-start.36
  345.4 42.0 %attend_back.4 = (bf16[4,192,1024]{2,1,0:T(8,128)(2,1)}, bf16[768,512]{1,0:T(8,128)(2,1)}) custom-call(bf16[3,4096,128]{2,1,0:T(8,128)(2,1)} %get-tuple-element.105.v_ref, bf16[3,64,4096]{2,1,0:T(8,128)(2,1)} %copy-done.1, bf16[3,128,4096]{2,1,0:T(8,128)(2,1)} %get-tuple-element.96.q_ref, ...), custom_call_target="tpu_custom_call", output_to_operand_aliasing={{1}: (13, {})} | custom-call | flops 25769803776 | bytes 33554432 | tf_op jit(solution)/shard_map/attend_back/pallas_call | solution.py:255
  389.5 1.8 add_up.9.refs_5_
  392.0 42.0 %attend_back.5 = (bf16[4,192,1024]{2,1,0:T(8,128)(2,1)}, bf16[768,256]{1,0:T(8,128)(2,1)}) custom-call(bf16[3,4096,128]{2,1,0:T(8,128)(2,1)} %get-tuple-element.105.v_ref, bf16[3,64,4096]{2,1,0:T(8,128)(2,1)} %copy-done.1, bf16[3,128,4096]{2,1,0:T(8,128)(2,1)} %get-tuple-element.96.q_ref, f32[64,4096]{1,0:T(8,128)} %get-tuple-element.127.o_ref, ...), custom_call_target="tpu_custom_call" | custom-call | flops 25769803776 | bytes 33554432 | tf_op jit(solution)/shard_map/attend_back/pallas_call | solution.py:255
  434.0 14.2 %all_to_all.20.refs_0_ = bf16[8,96,256]{2,1,0:T(8,128)(2,1)S(1)} all-to-all(bf16[8,96,256]{2,1,0:T(8,128)(2,1)} %bitcast.106), channel_id=1, replica_groups=mesh['seq'=4,'fsdp'=8] {'fsdp'}, dimensions={0} | all-to-all | bytes 786432 | tf_op jit(solution)/shard_map/all_to_all | solution.py:703
  448.2 5.1 all-to-all-start.2
  454.9 1.8 collective-permute-start.22
  461.8 5.7 %collective-permute-done.23.refs_2_ = bf16[192,1024]{1,0:T(8,128)(2,1)S(1)} collective-permute-done((bf16[192,1024]{1,0:T(8,128)(2,1)S(1)}, bf16[192,1024]{1,0:T(8,128)(2,1)S(1)}, u32[]{:S(2)}, u32[]{:S(2)}) %collective-permute-start.23) | collective-permute-done | bytes 393248 | tf_op jit(solution)/shard_map/ppermute | solution.py:645
  467.4 2.2 collective-permute-start.48
  470.7 5.8 %collective-permute-done.24.refs_3_ = bf16[192,1024]{1,0:T(8,128)(2,1)S(1)} collective-permute-done((bf16[192,1024]{1,0:T(8,128)(2,1)S(1)}, bf16[192,1024]{1,0:T(8,128)(2,1)S(1)}, u32[]{:S(2)}, u32[]{:S(2)}) %collective-permute-start.24) | collective-permute-done | bytes 393248 | tf_op jit(solution)/shard_map/ppermute | solution.py:645
  480.3 2.5 collective-permute-done.48.refs_3_
  486.2 4.5 collective-permute-done.32.refs_6_
  492.0 7.7 %collective-permute-done.33.refs_7_ = bf16[192,1024]{1,0:T(8,128)(2,1)} collective-permute-done((bf16[192,1024]{1,0:T(8,128)(2,1)}, bf16[192,1024]{1,0:T(8,128)(2,1)}, u32[]{:S(2)}, u32[]{:S(2)}) %collective-permute-start.33) | collective-permute-done | bytes 393248 | tf_op jit(solution)/shard_map/ppermute | solution.py:645
  501.2 6.4 %collective-permute-done.41.refs_10_ = bf16[192,1024]{1,0:T(8,128)(2,1)} collective-permute-done((bf16[192,1024]{1,0:T(8,128)(2,1)}, bf16[192,1024]{1,0:T(8,128)(2,1)}, u32[]{:S(2)}, u32[]{:S(2)}) %collective-permute-start.41) | collective-permute-done | bytes 393248 | tf_op jit(solution)/shard_map/ppermute | solution.py:645
  507.6 9.0 %collective-permute-done.42.refs_11_ = bf16[192,1024]{1,0:T(8,128)(2,1)} collective-permute-done((bf16[192,1024]{1,0:T(8,128)(2,1)}, bf16[192,1024]{1,0:T(8,128)(2,1)}, u32[]{:S(2)}, u32[]{:S(2)}) %collective-permute-start.42) | collective-permute-done | bytes 393248 | tf_op jit(solution)/shard_map/ppermute | solution.py:645
  520.6 10.0 %last.1 = f32[1024,768]{1,0:T(8,128)} custom-call(s32[1]{0:T(128)} %bitcast.info_ref.place_ref, bf16[1024,768]{1,0:T(8,128)(2,1)} %bitcast.102, f32[1024,768]{1,0:T(8,128)} %get-tuple-element.102.dh_ref, bf16[768,2432]{1,0:T(8,128)(2,1)} %all-gather.8.cloned.1.call-done.w_ref, bf16[192,1024]{1,0:T(8,128)(2,1)S(1)} %get-tuple-element.164.refs_0_, ...), custom_call_target="tpu_custom_call" | custom-call | flops 3623878656 | bytes 16777216 | tf_op jit(solution)/shard_map/last/pallas_call | solution.py:432
  (184 shorter events, 58.5 us)
Async XLA Ops:
  7.2 205.8 %all-gather.6.cloned.1.call-start = ((), (), s32[]{:S(2)}) async-start(), calls=%async_computation.5 | async-start | bytes 1990656 | tf_op jit(solution)/shard_map/all_gather | solution.py:651
  10.5 8.5 %collective-permute-start = (bf16[96,640]{1,0:T(8,128)(2,1)}, bf16[96,640]{1,0:T(8,128)(2,1)S(1)}, u32[]{:S(2)}, u32[]{:S(2)}) collective-permute-start(bf16[96,640]{1,0:T(8,128)(2,1)} %own_columns.1.refs_0_), channel_id=1, source_target_pairs={{0,7},{1,6},{2,5},{3,4},{4,3},{5,2},{6,1},{7,0},{8,15},{9,14},{10,... | collective-permute-start | bytes 368648 | tf_op jit(solution)/shard_map/ppermute | solution.py:645
  19.0 202.7 %all-gather.4.cloned.1.call-start = ((), (), s32[]{:S(2)}) async-start(), calls=%async_computation.4 | async-start | bytes 5529600 | tf_op jit(solution)/shard_map/all_gather | solution.py:651
  19.0 34.8 %collective-permute-start.1 = (bf16[1024,768]{1,0:T(8,128)(2,1)S(1)}, bf16[1024,768]{1,0:T(8,128)(2,1)}, u32[]{:S(2)}, u32[]{:S(2)}) collective-permute-start(bf16[1024,768]{1,0:T(8,128)(2,1)S(1)} %bitcast.103), channel_id=1, source_target_pairs={{0,16},{8,24},{16,0},{24,8},{1,17},{9,25},{17,1},{25,9},{2,18},{10... | collective-permute-start | bytes 4718600 | tf_op jit(solution)/shard_map/ppermute | solution.py:645
  20.2 38.7 %collective-permute-start.3 = (bf16[96,640]{1,0:T(8,128)(2,1)S(1)}, bf16[96,640]{1,0:T(8,128)(2,1)S(1)}, u32[]{:S(2)}, u32[]{:S(2)}) collective-permute-start(bf16[96,640]{1,0:T(8,128)(2,1)S(1)} %copy-done.3), channel_id=1, source_target_pairs={{0,1},{1,0},{2,3},{3,2},{4,5},{5,4},{6,7},{7,6},{8,9},{9,8},{10,11... | collective-permute-start | bytes 368648 | tf_op jit(solution)/shard_map/ppermute | solution.py:645
  21.2 38.7 %collective-permute-start.4 = (bf16[96,640]{1,0:T(8,128)(2,1)S(1)}, bf16[96,640]{1,0:T(8,128)(2,1)S(1)}, u32[]{:S(2)}, u32[]{:S(2)}) collective-permute-start(bf16[96,640]{1,0:T(8,128)(2,1)S(1)} %copy-done.3), channel_id=1, source_target_pairs={{0,2},{1,3},{2,0},{3,1},{4,6},{5,7},{6,4},{7,5},{8,10},{9,11},{10,... | collective-permute-start | bytes 368648 | tf_op jit(solution)/shard_map/ppermute | solution.py:645
  23.5 38.3 %collective-permute-start.5 = (bf16[96,640]{1,0:T(8,128)(2,1)S(1)}, bf16[96,640]{1,0:T(8,128)(2,1)S(1)}, u32[]{:S(2)}, u32[]{:S(2)}) collective-permute-start(bf16[96,640]{1,0:T(8,128)(2,1)S(1)} %copy-done.3), channel_id=1, source_target_pairs={{0,3},{1,2},{2,1},{3,0},{4,7},{5,6},{6,5},{7,4},{8,11},{9,10},{10,... | collective-permute-start | bytes 368648 | tf_op jit(solution)/shard_map/ppermute | solution.py:645
  23.5 63.1 %collective-permute-start.9 = (bf16[1024,768]{1,0:T(8,128)(2,1)S(1)}, bf16[1024,768]{1,0:T(8,128)(2,1)}, u32[]{:S(2)}, u32[]{:S(2)}) collective-permute-start(bf16[1024,768]{1,0:T(8,128)(2,1)S(1)} %bitcast.104), channel_id=1, source_target_pairs={{0,8},{8,0},{16,24},{24,16},{1,9},{9,1},{17,25},{25,17},{2,10},{10... | collective-permute-start | bytes 4718600 | tf_op jit(solution)/shard_map/ppermute | solution.py:645
  53.8 45.7 %collective-permute-start.2 = (bf16[1024,768]{1,0:T(8,128)(2,1)}, bf16[1024,768]{1,0:T(8,128)(2,1)}, u32[]{:S(2)}, u32[]{:S(2)}) collective-permute-start(bf16[1024,768]{1,0:T(8,128)(2,1)} %collective-permute-done.1.x_ref), channel_id=1, source_target_pairs={{0,8},{8,0},{16,24},{24,16},{1,9},{9,1},{17,25},{25,17},{2,10},{10... | collective-permute-start | bytes 4718600 | tf_op jit(solution)/shard_map/ppermute | solution.py:645
  58.9 18.8 %collective-permute-start.6 = (bf16[96,640]{1,0:T(8,128)(2,1)S(1)}, bf16[96,640]{1,0:T(8,128)(2,1)S(1)}, u32[]{:S(2)}, u32[]{:S(2)}) collective-permute-start(bf16[96,640]{1,0:T(8,128)(2,1)S(1)} %copy-done.3), channel_id=1, source_target_pairs={{0,4},{1,5},{2,6},{3,7},{4,0},{5,1},{6,2},{7,3},{8,12},{9,13},{10,... | collective-permute-start | bytes 368648 | tf_op jit(solution)/shard_map/ppermute | solution.py:645
  59.9 20.5 %collective-permute-start.7 = (bf16[96,640]{1,0:T(8,128)(2,1)S(1)}, bf16[96,640]{1,0:T(8,128)(2,1)S(1)}, u32[]{:S(2)}, u32[]{:S(2)}) collective-permute-start(bf16[96,640]{1,0:T(8,128)(2,1)S(1)} %copy-done.3), channel_id=1, source_target_pairs={{0,5},{1,4},{2,7},{3,6},{4,1},{5,0},{6,3},{7,2},{8,13},{9,12},{10,... | collective-permute-start | bytes 368648 | tf_op jit(solution)/shard_map/ppermute | solution.py:645
  61.8 18.6 %collective-permute-start.8 = (bf16[96,640]{1,0:T(8,128)(2,1)S(1)}, bf16[96,640]{1,0:T(8,128)(2,1)S(1)}, u32[]{:S(2)}, u32[]{:S(2)}) collective-permute-start(bf16[96,640]{1,0:T(8,128)(2,1)S(1)} %copy-done.3), channel_id=1, source_target_pairs={{0,6},{1,7},{2,4},{3,5},{4,2},{5,3},{6,0},{7,1},{8,14},{9,15},{10,... | collective-permute-start | bytes 368648 | tf_op jit(solution)/shard_map/ppermute | solution.py:645
  140.6 69.4 %collective-permute-start.16 = (bf16[64,1024]{1,0:T(8,128)(2,1)S(1)}, bf16[64,1024]{1,0:T(8,128)(2,1)S(1)}, u32[]{:S(2)}, u32[]{:S(2)}) collective-permute-start(bf16[64,1024]{1,0:T(8,128)(2,1)S(1)} %get-tuple-element.167), channel_id=1, source_target_pairs={{0,8},{8,0},{16,24},{24,16},{1,9},{9,1},{17,25},{25,17},{2,10},{10... | collective-permute-start | bytes 393224 | tf_op jit(solution)/shard_map/ppermute | solution.py:645
  141.3 69.6 %collective-permute-start.17 = (bf16[64,1024]{1,0:T(8,128)(2,1)S(1)}, bf16[64,1024]{1,0:T(8,128)(2,1)S(1)}, u32[]{:S(2)}, u32[]{:S(2)}) collective-permute-start(bf16[64,1024]{1,0:T(8,128)(2,1)S(1)} %get-tuple-element.166), channel_id=1, source_target_pairs={{0,16},{8,24},{16,0},{24,8},{1,17},{9,25},{17,1},{25,9},{2,18},{10... | collective-permute-start | bytes 393224 | tf_op jit(solution)/shard_map/ppermute | solution.py:645
  142.5 68.4 %collective-permute-start.18 = (bf16[64,1024]{1,0:T(8,128)(2,1)S(1)}, bf16[64,1024]{1,0:T(8,128)(2,1)S(1)}, u32[]{:S(2)}, u32[]{:S(2)}) collective-permute-start(bf16[64,1024]{1,0:T(8,128)(2,1)S(1)} %get-tuple-element.165), channel_id=1, source_target_pairs={{0,24},{8,16},{16,8},{24,0},{1,25},{9,17},{17,9},{25,1},{2,26},{10... | collective-permute-start | bytes 393224 | tf_op jit(solution)/shard_map/ppermute | solution.py:645
  175.9 36.2 %collective-permute-start.13 = (bf16[64,1024]{1,0:T(8,128)(2,1)S(1)}, bf16[64,1024]{1,0:T(8,128)(2,1)S(1)}, u32[]{:S(2)}, u32[]{:S(2)}) collective-permute-start(bf16[64,1024]{1,0:T(8,128)(2,1)S(1)} %get-tuple-element.171), channel_id=1, source_target_pairs={{0,8},{8,0},{16,24},{24,16},{1,9},{9,1},{17,25},{25,17},{2,10},{10... | collective-permute-start | bytes 393224 | tf_op jit(solution)/shard_map/ppermute | solution.py:645
  176.1 36.9 %collective-permute-start.14 = (bf16[64,1024]{1,0:T(8,128)(2,1)S(1)}, bf16[64,1024]{1,0:T(8,128)(2,1)S(1)}, u32[]{:S(2)}, u32[]{:S(2)}) collective-permute-start(bf16[64,1024]{1,0:T(8,128)(2,1)S(1)} %get-tuple-element.170), channel_id=1, source_target_pairs={{0,16},{8,24},{16,0},{24,8},{1,17},{9,25},{17,1},{25,9},{2,18},{10... | collective-permute-start | bytes 393224 | tf_op jit(solution)/shard_map/ppermute | solution.py:645
  212.1 9.5 %collective-permute-start.12 = (bf16[64,1024]{1,0:T(8,128)(2,1)S(1)}, bf16[64,1024]{1,0:T(8,128)(2,1)S(1)}, u32[]{:S(2)}, u32[]{:S(2)}) collective-permute-start(bf16[64,1024]{1,0:T(8,128)(2,1)S(1)} %get-tuple-element.173), channel_id=1, source_target_pairs={{0,24},{8,16},{16,8},{24,0},{1,25},{9,17},{17,9},{25,1},{2,26},{10... | collective-permute-start | bytes 393224 | tf_op jit(solution)/shard_map/ppermute | solution.py:645
  264.7 58.6 %all-to-all-start = ((bf16[8,144,768]{2,1,0:T(8,128)(2,1)}), bf16[8,144,768]{2,1,0:T(8,128)(2,1)S(1)}, u32[]{:S(2)}, u32[]{:S(2)}) async-start(bf16[8,144,768]{2,1,0:T(8,128)(2,1)} %bitcast.112), calls=%async_computation | async-start | bytes 3538944 | tf_op jit(solution)/shard_map/all_to_all | solution.py:703
  268.8 232.4 %all-gather.8.cloned.1.call-start = ((), (), s32[]{:S(2)}) async-start(), calls=%async_computation.6 | async-start | bytes 4202496 | tf_op jit(solution)/shard_map/all_gather | solution.py:651
  277.6 46.7 %collective-permute-start.28 = (bf16[768,768]{1,0:T(8,128)(2,1)}, bf16[768,768]{1,0:T(8,128)(2,1)S(1)}, u32[]{:S(2)}, u32[]{:S(2)}) collective-permute-start(bf16[768,768]{1,0:T(8,128)(2,1)} %get-tuple-element.140), channel_id=1, source_target_pairs={{0,8},{8,0},{16,24},{24,16},{1,9},{9,1},{17,25},{25,17},{2,10},{10... | collective-permute-start | bytes 3538952 | tf_op jit(solution)/shard_map/ppermute | solution.py:645
  277.7 47.5 %collective-permute-start.29 = (bf16[768,768]{1,0:T(8,128)(2,1)}, bf16[768,768]{1,0:T(8,128)(2,1)}, u32[]{:S(2)}, u32[]{:S(2)}) collective-permute-start(bf16[768,768]{1,0:T(8,128)(2,1)} %get-tuple-element.139), channel_id=1, source_target_pairs={{0,16},{8,24},{16,0},{24,8},{1,17},{9,25},{17,1},{25,9},{2,18},{10... | collective-permute-start | bytes 3538952 | tf_op jit(solution)/shard_map/ppermute | solution.py:645
  277.9 53.9 %collective-permute-start.30 = (bf16[768,768]{1,0:T(8,128)(2,1)}, bf16[768,768]{1,0:T(8,128)(2,1)}, u32[]{:S(2)}, u32[]{:S(2)}) collective-permute-start(bf16[768,768]{1,0:T(8,128)(2,1)} %get-tuple-element.138), channel_id=1, source_target_pairs={{0,24},{8,16},{16,8},{24,0},{1,25},{9,17},{17,9},{25,1},{2,26},{10... | collective-permute-start | bytes 3538952 | tf_op jit(solution)/shard_map/ppermute | solution.py:645
  279.7 62.1 %collective-permute-start.25 = (bf16[64,1024]{1,0:T(8,128)(2,1)}, bf16[64,1024]{1,0:T(8,128)(2,1)}, u32[]{:S(2)}, u32[]{:S(2)}) collective-permute-start(bf16[64,1024]{1,0:T(8,128)(2,1)} %get-tuple-element.151), channel_id=1, source_target_pairs={{0,8},{8,0},{16,24},{24,16},{1,9},{9,1},{17,25},{25,17},{2,10},{10... | collective-permute-start | bytes 393224 | tf_op jit(solution)/shard_map/ppermute | solution.py:645
  280.4 61.7 %collective-permute-start.26 = (bf16[64,1024]{1,0:T(8,128)(2,1)}, bf16[64,1024]{1,0:T(8,128)(2,1)}, u32[]{:S(2)}, u32[]{:S(2)}) collective-permute-start(bf16[64,1024]{1,0:T(8,128)(2,1)} %get-tuple-element.150), channel_id=1, source_target_pairs={{0,16},{8,24},{16,0},{24,8},{1,17},{9,25},{17,1},{25,9},{2,18},{10... | collective-permute-start | bytes 393224 | tf_op jit(solution)/shard_map/ppermute | solution.py:645
  324.2 20.1 %collective-permute-start.27 = (bf16[64,1024]{1,0:T(8,128)(2,1)}, bf16[64,1024]{1,0:T(8,128)(2,1)S(1)}, u32[]{:S(2)}, u32[]{:S(2)}) collective-permute-start(bf16[64,1024]{1,0:T(8,128)(2,1)} %get-tuple-element.149), channel_id=1, source_target_pairs={{0,24},{8,16},{16,8},{24,0},{1,25},{9,17},{17,9},{25,1},{2,26},{10... | collective-permute-start | bytes 393224 | tf_op jit(solution)/shard_map/ppermute | solution.py:645
  325.2 19.3 %collective-permute-start.37 = (bf16[144,768]{1,0:T(8,128)(2,1)}, bf16[144,768]{1,0:T(8,128)(2,1)S(1)}, u32[]{:S(2)}, u32[]{:S(2)}) collective-permute-start(bf16[144,768]{1,0:T(8,128)(2,1)} %add_up.7.refs_6_), channel_id=1, source_target_pairs={{0,8},{8,0},{16,24},{24,16},{1,9},{9,1},{17,25},{25,17},{2,10},{10... | collective-permute-start | bytes 663560 | tf_op jit(solution)/shard_map/ppermute | solution.py:645
  331.8 59.5 %collective-permute-start.34 = (bf16[64,1024]{1,0:T(8,128)(2,1)}, bf16[64,1024]{1,0:T(8,128)(2,1)S(1)}, u32[]{:S(2)}, u32[]{:S(2)}) collective-permute-start(bf16[64,1024]{1,0:T(8,128)(2,1)} %get-tuple-element.147), channel_id=1, source_target_pairs={{0,8},{8,0},{16,24},{24,16},{1,9},{9,1},{17,25},{25,17},{2,10},{10... | collective-permute-start | bytes 393224 | tf_op jit(solution)/shard_map/ppermute | solution.py:645
  335.8 52.8 %all-to-all-start.1 = ((bf16[8,96,768]{2,1,0:T(8,128)(2,1)}), bf16[8,96,768]{2,1,0:T(8,128)(2,1)S(1)}, u32[]{:S(2)}, u32[]{:S(2)}) async-start(bf16[8,96,768]{2,1,0:T(8,128)(2,1)} %bitcast.50), calls=%async_computation.1 | async-start | bytes 2359296 | tf_op jit(solution)/shard_map/all_to_all | solution.py:703
  341.9 49.4 %collective-permute-start.35 = (bf16[64,1024]{1,0:T(8,128)(2,1)S(1)}, bf16[64,1024]{1,0:T(8,128)(2,1)S(1)}, u32[]{:S(2)}, u32[]{:S(2)}) collective-permute-start(bf16[64,1024]{1,0:T(8,128)(2,1)S(1)} %copy-done.25), channel_id=1, source_target_pairs={{0,16},{8,24},{16,0},{24,8},{1,17},{9,25},{17,1},{25,9},{2,18},{10... | collective-permute-start | bytes 393224 | tf_op jit(solution)/shard_map/ppermute | solution.py:645
  342.1 49.3 %collective-permute-start.36 = (bf16[64,1024]{1,0:T(8,128)(2,1)S(1)}, bf16[64,1024]{1,0:T(8,128)(2,1)S(1)}, u32[]{:S(2)}, u32[]{:S(2)}) collective-permute-start(bf16[64,1024]{1,0:T(8,128)(2,1)S(1)} %get-tuple-element.145), channel_id=1, source_target_pairs={{0,24},{8,16},{16,8},{24,0},{1,25},{9,17},{17,9},{25,1},{2,26},{10... | collective-permute-start | bytes 393224 | tf_op jit(solution)/shard_map/ppermute | solution.py:645
  344.3 45.1 %collective-permute-start.38 = (bf16[144,768]{1,0:T(8,128)(2,1)}, bf16[144,768]{1,0:T(8,128)(2,1)S(1)}, u32[]{:S(2)}, u32[]{:S(2)}) collective-permute-start(bf16[144,768]{1,0:T(8,128)(2,1)} %add_up.7.refs_6_), channel_id=1, source_target_pairs={{0,16},{8,24},{16,0},{24,8},{1,17},{9,25},{17,1},{25,9},{2,18},{10... | collective-permute-start | bytes 663560 | tf_op jit(solution)/shard_map/ppermute | solution.py:645
  344.5 45.0 %collective-permute-start.39 = (bf16[144,768]{1,0:T(8,128)(2,1)}, bf16[144,768]{1,0:T(8,128)(2,1)S(1)}, u32[]{:S(2)}, u32[]{:S(2)}) collective-permute-start(bf16[144,768]{1,0:T(8,128)(2,1)} %add_up.7.refs_6_), channel_id=1, source_target_pairs={{0,24},{8,16},{16,8},{24,0},{1,25},{9,17},{17,9},{25,1},{2,26},{10... | collective-permute-start | bytes 663560 | tf_op jit(solution)/shard_map/ppermute | solution.py:645
  448.2 37.8 %all-to-all-start.2 = ((bf16[8,96,512]{2,1,0:T(8,128)(2,1)}), bf16[8,96,512]{2,1,0:T(8,128)(2,1)S(1)}, u32[]{:S(2)}, u32[]{:S(2)}) async-start(bf16[8,96,512]{2,1,0:T(8,128)(2,1)} %bitcast.60), calls=%async_computation.2 | async-start | bytes 1572864 | tf_op jit(solution)/shard_map/all_to_all | solution.py:703
  456.7 10.7 %collective-permute-start.23 = (bf16[192,1024]{1,0:T(8,128)(2,1)S(1)}, bf16[192,1024]{1,0:T(8,128)(2,1)S(1)}, u32[]{:S(2)}, u32[]{:S(2)}) collective-permute-start(bf16[192,1024]{1,0:T(8,128)(2,1)S(1)} %get-tuple-element.162), channel_id=1, source_target_pairs={{0,16},{8,24},{16,0},{24,8},{1,17},{9,25},{17,1},{25,9},{2,18},{10... | collective-permute-start | bytes 1179656 | tf_op jit(solution)/shard_map/ppermute | solution.py:645
  457.8 18.7 %collective-permute-start.24 = (bf16[192,1024]{1,0:T(8,128)(2,1)S(1)}, bf16[192,1024]{1,0:T(8,128)(2,1)S(1)}, u32[]{:S(2)}, u32[]{:S(2)}) collective-permute-start(bf16[192,1024]{1,0:T(8,128)(2,1)S(1)} %get-tuple-element.161), channel_id=1, source_target_pairs={{0,24},{8,16},{16,8},{24,0},{1,25},{9,17},{17,9},{25,1},{2,26},{10... | collective-permute-start | bytes 1179656 | tf_op jit(solution)/shard_map/ppermute | solution.py:645
  459.5 24.3 %collective-permute-start.31 = (bf16[192,1024]{1,0:T(8,128)(2,1)S(1)}, bf16[192,1024]{1,0:T(8,128)(2,1)S(1)}, u32[]{:S(2)}, u32[]{:S(2)}) collective-permute-start(bf16[192,1024]{1,0:T(8,128)(2,1)S(1)} %get-tuple-element.159), channel_id=1, source_target_pairs={{0,8},{8,0},{16,24},{24,16},{1,9},{9,1},{17,25},{25,17},{2,10},{10... | collective-permute-start | bytes 1179656 | tf_op jit(solution)/shard_map/ppermute | solution.py:645
  459.6 17.9 %collective-permute-start.46 = (bf16[96,768]{1,0:T(8,128)(2,1)S(1)}, bf16[96,768]{1,0:T(8,128)(2,1)S(1)}, u32[]{:S(2)}, u32[]{:S(2)}) collective-permute-start(bf16[96,768]{1,0:T(8,128)(2,1)S(1)} %copy-done.9), channel_id=1, source_target_pairs={{0,8},{8,0},{16,24},{24,16},{1,9},{9,1},{17,25},{25,17},{2,10},{10... | collective-permute-start | bytes 442376 | tf_op jit(solution)/shard_map/ppermute | solution.py:645
  460.7 18.3 %collective-permute-start.47 = (bf16[96,768]{1,0:T(8,128)(2,1)S(1)}, bf16[96,768]{1,0:T(8,128)(2,1)S(1)}, u32[]{:S(2)}, u32[]{:S(2)}) collective-permute-start(bf16[96,768]{1,0:T(8,128)(2,1)S(1)} %copy-done.9), channel_id=1, source_target_pairs={{0,16},{8,24},{16,0},{24,8},{1,17},{9,25},{17,1},{25,9},{2,18},{10... | collective-permute-start | bytes 442376 | tf_op jit(solution)/shard_map/ppermute | solution.py:645
  467.4 15.4 %collective-permute-start.48 = (bf16[96,768]{1,0:T(8,128)(2,1)S(1)}, bf16[96,768]{1,0:T(8,128)(2,1)S(1)}, u32[]{:S(2)}, u32[]{:S(2)}) collective-permute-start(bf16[96,768]{1,0:T(8,128)(2,1)S(1)} %copy-done.9), channel_id=1, source_target_pairs={{0,24},{8,16},{16,8},{24,0},{1,25},{9,17},{17,9},{25,1},{2,26},{10... | collective-permute-start | bytes 442376 | tf_op jit(solution)/shard_map/ppermute | solution.py:645
  476.5 14.2 %collective-permute-start.32 = (bf16[192,1024]{1,0:T(8,128)(2,1)}, bf16[192,1024]{1,0:T(8,128)(2,1)}, u32[]{:S(2)}, u32[]{:S(2)}) collective-permute-start(bf16[192,1024]{1,0:T(8,128)(2,1)} %get-tuple-element.158), channel_id=1, source_target_pairs={{0,16},{8,24},{16,0},{24,8},{1,17},{9,25},{17,1},{25,9},{2,18},{10... | collective-permute-start | bytes 1179656 | tf_op jit(solution)/shard_map/ppermute | solution.py:645
  477.5 22.2 %collective-permute-start.33 = (bf16[192,1024]{1,0:T(8,128)(2,1)}, bf16[192,1024]{1,0:T(8,128)(2,1)}, u32[]{:S(2)}, u32[]{:S(2)}) collective-permute-start(bf16[192,1024]{1,0:T(8,128)(2,1)} %get-tuple-element.157), channel_id=1, source_target_pairs={{0,24},{8,16},{16,8},{24,0},{1,25},{9,17},{17,9},{25,1},{2,26},{10... | collective-permute-start | bytes 1179656 | tf_op jit(solution)/shard_map/ppermute | solution.py:645
  479.0 21.8 %collective-permute-start.40 = (bf16[192,1024]{1,0:T(8,128)(2,1)}, bf16[192,1024]{1,0:T(8,128)(2,1)}, u32[]{:S(2)}, u32[]{:S(2)}) collective-permute-start(bf16[192,1024]{1,0:T(8,128)(2,1)} %get-tuple-element.143), channel_id=1, source_target_pairs={{0,8},{8,0},{16,24},{24,16},{1,9},{9,1},{17,25},{25,17},{2,10},{10... | collective-permute-start | bytes 1179656 | tf_op jit(solution)/shard_map/ppermute | solution.py:645
  482.8 24.8 %collective-permute-start.41 = (bf16[192,1024]{1,0:T(8,128)(2,1)}, bf16[192,1024]{1,0:T(8,128)(2,1)}, u32[]{:S(2)}, u32[]{:S(2)}) collective-permute-start(bf16[192,1024]{1,0:T(8,128)(2,1)} %get-tuple-element.142), channel_id=1, source_target_pairs={{0,16},{8,24},{16,0},{24,8},{1,17},{9,25},{17,1},{25,9},{2,18},{10... | collective-permute-start | bytes 1179656 | tf_op jit(solution)/shard_map/ppermute | solution.py:645
  483.8 32.8 %collective-permute-start.42 = (bf16[192,1024]{1,0:T(8,128)(2,1)}, bf16[192,1024]{1,0:T(8,128)(2,1)}, u32[]{:S(2)}, u32[]{:S(2)}) collective-permute-start(bf16[192,1024]{1,0:T(8,128)(2,1)} %get-tuple-element.141), channel_id=1, source_target_pairs={{0,24},{8,16},{16,8},{24,0},{1,25},{9,17},{17,9},{25,1},{2,26},{10... | collective-permute-start | bytes 1179656 | tf_op jit(solution)/shard_map/ppermute | solution.py:645
  490.7 39.8 %collective-permute-start.43 = (bf16[96,768]{1,0:T(8,128)(2,1)S(1)}, bf16[96,768]{1,0:T(8,128)(2,1)S(1)}, u32[]{:S(2)}, u32[]{:S(2)}) collective-permute-start(bf16[96,768]{1,0:T(8,128)(2,1)S(1)} %pad_maximum_fusion.1.refs_0_), channel_id=1, source_target_pairs={{0,8},{8,0},{16,24},{24,16},{1,9},{9,1},{17,25},{25,17},{2,10},{10... | collective-permute-start | bytes 442376 | tf_op jit(solution)/shard_map/ppermute | solution.py:645
  499.7 30.8 %collective-permute-start.44 = (bf16[96,768]{1,0:T(8,128)(2,1)S(1)}, bf16[96,768]{1,0:T(8,128)(2,1)S(1)}, u32[]{:S(2)}, u32[]{:S(2)}) collective-permute-start(bf16[96,768]{1,0:T(8,128)(2,1)S(1)} %pad_maximum_fusion.1.refs_0_), channel_id=1, source_target_pairs={{0,16},{8,24},{16,0},{24,8},{1,17},{9,25},{17,1},{25,9},{2,18},{10... | collective-permute-start | bytes 442376 | tf_op jit(solution)/shard_map/ppermute | solution.py:645
  500.8 29.8 %collective-permute-start.45 = (bf16[96,768]{1,0:T(8,128)(2,1)S(1)}, bf16[96,768]{1,0:T(8,128)(2,1)S(1)}, u32[]{:S(2)}, u32[]{:S(2)}) collective-permute-start(bf16[96,768]{1,0:T(8,128)(2,1)S(1)} %pad_maximum_fusion.1.refs_0_), channel_id=1, source_target_pairs={{0,24},{8,16},{16,8},{24,0},{1,25},{9,17},{17,9},{25,1},{2,26},{10... | collective-permute-start | bytes 442376 | tf_op jit(solution)/shard_map/ppermute | solution.py:645
  (41 other events, 259.2 us)
Sparse Core Ops, SparseCore 0:
  19.1 58.8 all-gather.5
  80.7 79.1 all-gather.3
  326.5 83.3 all-gather.7
